TPU v7x, 32 devices: a whole 2x2x4 slice. The times are simulated.
32 devices in a mesh: dev: 32 (over z, y, x, core).
Axes of the slice: x: 2, y: 2, z: 4, core: 2. Of those that a mesh axis runs over, the one named last changes fastest.
Arguments:
- tokens: bfloat16 [8192, 1536], P('dev'), may hold values from -6 to 6
- positions: int32 [8192], P('dev'), may hold values from 0 to 1999, as said below
- expert_picks: int32 [8192, 8], P('dev'), may hold values from 0 to 31, all different within a row
- priority: int32 [8192, 8], P('dev'), may hold values from 0 to 2047, as said below
- first_gain: bfloat16 [1536], P('dev'), may hold values from 0.5 to 1.5
- query_weight: bfloat16 [1536, 1536], P('dev'), may hold values from -0.15625 to 0.15625
- key_projection_matrix: bfloat16 [1536, 512], P('dev'), may hold values from -0.15625 to 0.15625
- value_projection_matrix: bfloat16 [1536, 512], P('dev'), may hold values from -0.15625 to 0.15625
- output_weight: bfloat16 [1536, 1536], P('dev'), may hold values from -1.75 to 1.75
- second_gain: bfloat16 [1536], P('dev'), may hold values from 0.5 to 1.5
- router_weight: bfloat16 [1536, 32], P('dev'), may hold values from -0.078125 to 0.078125
- gate_weight: bfloat16 [1536, 16384], P(None, 'dev'), may hold values from -0.15625 to 0.15625
- up_weight: bfloat16 [1536, 16384], P(None, 'dev'), may hold values from -0.15625 to 0.15625
- down_weight: bfloat16 [16384, 1536], P('dev'), may hold values from -1 to 1
- cotangent: bfloat16 [8192, 1536], P('dev'), may hold values from -6 to 6
Outputs:
- layer_output: bfloat16 [8192, 1536], P('dev')
- tokens_gradient: float32 [8192, 1536], P('dev')
- first_gain_gradient: float32 [1536], P('dev')
- query_weight_gradient: float32 [1536, 1536], P('dev')
- key_weight_gradient: float32 [1536, 512], P('dev')
- value_weight_gradient: float32 [1536, 512], P('dev')
- output_weight_gradient: float32 [1536, 1536], P('dev')
- second_gain_gradient: float32 [1536], P('dev')
- router_weight_gradient: float32 [1536, 32], P('dev')
- gate_weight_gradient: float32 [1536, 16384], P(None, 'dev')
- up_weight_gradient: float32 [1536, 16384], P(None, 'dev')
- down_weight_gradient: float32 [16384, 1536], P('dev')
Inputs may be any that keep to these rules, and one draw needn't show every extreme that they name: `positions`: each token's position counts the tokens before it in its document. Documents are runs of tokens inside aligned blocks of 8192 tokens and hold 200 to 2000 tokens, except that the last one of a block may be shorter; each block holds one document of exactly 2000 tokens. `expert_picks`: each row names 8 different experts. `priority`: within each aligned block of 256 rows the 2048 entries are all different.
All inputs are finite; a program needn't handle non-finite values.
Results may differ from a plain program's by a relative error of at most 0.015.
Values may be sent and summed in bfloat16 or wider, within the bound.
A program may use at most 512 MiB of HBM per device.

v0:
```python
import jax
import jax.numpy as jnp
from jax import lax
from jax.sharding import PartitionSpec as P

QUERY_HEADS = 24
KEY_HEADS = 8
HEAD_DIM = 64
TOP = 8
EXPERTS = 32
MAXDOC = 2000


epsilon = 1e-06
masked_score = -1e30


def from_behind(block, axis, distance):
    devices = range(lax.axis_size(axis))
    route = [(i - distance, i) for i in devices if i - distance in devices]
    return lax.ppermute(block, axis, route)


def matmul(first_operand, second_operand):
    return jnp.dot(first_operand, second_operand, preferred_element_type=jnp.float32)


def contract_last(first_operand, second_operand):
    return lax.dot_general(
        first_operand, second_operand, (((1,), (1,)), ((), ())), preferred_element_type=jnp.float32
    )


def contract_first(first_operand, second_operand):
    return lax.dot_general(
        first_operand, second_operand, (((0,), (0,)), ((), ())), preferred_element_type=jnp.float32
    )


def rms_scale(values):
    return lax.rsqrt(jnp.mean(values * values, axis=-1, keepdims=True) + epsilon)


def rotary_tables(positions, head_size):
    half_dim = head_size // 2
    frequency = jnp.power(10000.0, -(jnp.arange(half_dim, dtype=jnp.float32) * 2.0) / head_size)
    angle = positions.astype(jnp.float32)[:, None] * frequency[None, :]
    return (jnp.cos(angle), jnp.sin(angle))


def rotate(values, cosine, sine_part):
    half_dim = cosine.shape[1]
    shaped = values.reshape(values.shape[0], -1, 2 * half_dim)
    leading = shaped[..., :half_dim]
    trailing = shaped[..., half_dim:]
    cosine_rows = cosine[:, None, :]
    sine_rows = sine_part[:, None, :]
    turned = jnp.concatenate(
        [
            leading * cosine_rows - trailing * sine_rows,
            trailing * cosine_rows + leading * sine_rows,
        ],
        axis=-1,
    )
    return turned.reshape(values.shape)


def route_slots(expert_picks, priority, experts, capacity):
    flat_picks = expert_picks.reshape(-1)
    flat_priority = priority.reshape(-1)
    pick_count = flat_picks.shape[0]
    by_priority = (
        jnp.zeros((pick_count,), jnp.int32)
        .at[flat_priority]
        .set(jnp.arange(pick_count, dtype=jnp.int32))
    )
    ordered = flat_picks[by_priority]
    matches = (ordered[:, None] == jnp.arange(experts, dtype=jnp.int32)[None, :]).astype(jnp.int32)
    running = jnp.cumsum(matches, axis=0, dtype=jnp.int32)
    ordered_rank = jnp.sum(running * matches, axis=1, dtype=jnp.int32) - 1
    pick_rank = ordered_rank[flat_priority]
    return jnp.where(pick_rank < capacity, flat_picks * capacity + pick_rank, experts * capacity)


def split_into_heads(values, kv_heads, head_size):
    row_count = values.shape[0]
    query_group_width = values.shape[1] // (kv_heads * head_size)
    shaped = values.reshape(row_count, kv_heads, query_group_width, head_size).transpose(1, 2, 0, 3)
    return shaped.reshape(kv_heads, query_group_width * row_count, head_size)


def from_heads(values, row_count):
    kv_heads, stacked, head_size = values.shape
    query_group_width = stacked // row_count
    shaped = values.reshape(kv_heads, query_group_width, row_count, head_size).transpose(2, 0, 1, 3)
    return shaped.reshape(row_count, kv_heads * query_group_width * head_size)


def to_experts(send_rows):
    devices = lax.axis_size("dev")
    experts, capacity, model_width = send_rows.shape
    width_split = devices // experts
    copied = jnp.repeat(send_rows, width_split, axis=0)
    arrived = lax.all_to_all(copied, "dev", split_axis=0, concat_axis=0, tiled=True)
    gathered_rows = arrived.reshape(devices * capacity, model_width)
    return gathered_rows


def from_experts(partial_rows, capacity):
    devices = lax.axis_size("dev")
    model_width = partial_rows.shape[-1]
    width_split = devices // EXPERTS
    arrived = lax.all_to_all(
        partial_rows.reshape(devices, capacity, model_width),
        "dev",
        split_axis=0,
        concat_axis=0,
        tiled=True,
    )
    summed = jnp.sum(arrived.reshape(EXPERTS, width_split, capacity, model_width), axis=1)
    return summed.reshape(EXPERTS * capacity, model_width)


def on_device(
    tokens,
    positions,
    expert_picks,
    priority,
    first_gain,
    query_weight,
    key_projection_matrix,
    value_projection_matrix,
    output_weight,
    second_gain,
    router_weight,
    gate_weight,
    up_weight,
    down_weight,
    cotangent,
):
    gathered = (
        lax.all_gather(first_gain, "dev", axis=0, tiled=True),
        lax.all_gather(query_weight, "dev", axis=0, tiled=True),
        lax.all_gather(key_projection_matrix, "dev", axis=0, tiled=True),
        lax.all_gather(value_projection_matrix, "dev", axis=0, tiled=True),
        lax.all_gather(output_weight, "dev", axis=0, tiled=True),
        lax.all_gather(second_gain, "dev", axis=0, tiled=True),
        lax.all_gather(router_weight, "dev", axis=0, tiled=True),
    )
    gain_one, query_matrix, key_matrix, value_matrix, output_matrix, gain_two, router_matrix = (
        gathered
    )
    tok_rows, model_width = tokens.shape
    query_group_width = QUERY_HEADS // KEY_HEADS
    reach_back = (MAXDOC + tok_rows - 2) // tok_rows
    key_token_rows = (reach_back + 1) * tok_rows
    score_scale = HEAD_DIM ** (-0.5)
    gain_first = gain_one.astype(jnp.float32)
    gain_second = gain_two.astype(jnp.float32)
    inputs = tokens.astype(jnp.float32)
    scale_one = rms_scale(inputs)
    normed_one = (inputs * scale_one * gain_first).astype(jnp.bfloat16)
    cosine, sine_part = rotary_tables(positions, HEAD_DIM)
    query_lower_bound = rotate(matmul(normed_one, query_matrix), cosine, sine_part).astype(
        jnp.bfloat16
    )
    key_low = rotate(matmul(normed_one, key_matrix), cosine, sine_part).astype(jnp.bfloat16)
    value_low = matmul(normed_one, value_matrix).astype(jnp.bfloat16)
    key_parts = []
    value_parts = []
    for distance in range(reach_back, 0, -1):
        moved_key, moved_value = from_behind((key_low, value_low), "dev", distance)
        key_parts.append(moved_key)
        value_parts.append(moved_value)
    every_key_row = jnp.concatenate(key_parts + [key_low], axis=0)
    every_value_row = jnp.concatenate(value_parts + [value_low], axis=0)
    relative = jnp.arange(key_token_rows, dtype=jnp.int32) - reach_back * tok_rows
    rows_here = jnp.arange(tok_rows, dtype=jnp.int32)
    allowed = (relative[None, :] <= rows_here[:, None]) & (
        relative[None, :] >= (rows_here - positions)[:, None]
    )
    query_head_rows = split_into_heads(query_lower_bound, KEY_HEADS, HEAD_DIM)
    key_head_rows = every_key_row.reshape(key_token_rows, KEY_HEADS, HEAD_DIM).transpose(1, 0, 2)
    value_head_rows = every_value_row.reshape(key_token_rows, KEY_HEADS, HEAD_DIM).transpose(
        1, 0, 2
    )

    def attend(operands):
        query_group, key_group, value_group = operands
        scores = (contract_last(query_group, key_group) * score_scale).reshape(
            query_group_width, tok_rows, key_token_rows
        )
        scores = jnp.where(allowed[None], scores, masked_score)
        row_max = jnp.max(scores, axis=-1, keepdims=True)
        exponent = jnp.exp(scores - row_max)
        row_total = jnp.sum(exponent, axis=-1, keepdims=True)
        probability = exponent / row_total
        log_total = (row_max + jnp.log(row_total)).reshape(query_group_width * tok_rows)
        probability_low = probability.astype(jnp.bfloat16).reshape(
            query_group_width * tok_rows, key_token_rows
        )
        return (matmul(probability_low, value_group), log_total)

    head_out, log_totals = lax.map(attend, (query_head_rows, key_head_rows, value_head_rows))
    attended = from_heads(head_out, tok_rows).astype(jnp.bfloat16)
    residual = inputs + matmul(attended, output_matrix)
    scale_two = rms_scale(residual)
    normed_two = (residual * scale_two * gain_second).astype(jnp.bfloat16)
    logits = matmul(normed_two, router_matrix)
    picked = jnp.take_along_axis(logits, expert_picks, axis=1)
    picked_max = jnp.max(picked, axis=-1, keepdims=True)
    picked_exp = jnp.exp(picked - picked_max)
    pick_gates = picked_exp / jnp.sum(picked_exp, axis=-1, keepdims=True)
    devices = lax.axis_size("dev")
    width_split = devices // EXPERTS
    capacity = width_split * (
        (9 * tok_rows * TOP + 8 * EXPERTS * width_split - 1) // (8 * EXPERTS * width_split)
    )
    gate_use, up_use, down_use = (gate_weight, up_weight, down_weight)
    slot_index = route_slots(expert_picks, priority, EXPERTS, capacity)
    token_of_pick = jnp.arange(tok_rows * TOP, dtype=jnp.int32) // TOP
    send_rows = (
        jnp.zeros((EXPERTS * capacity, model_width), jnp.bfloat16)
        .at[slot_index]
        .set(normed_two[token_of_pick], mode="drop")
    )
    expert_in = to_experts(send_rows.reshape(EXPERTS, capacity, model_width))
    gate_in = matmul(expert_in, gate_use)
    up_in = matmul(expert_in, up_use)
    sigmoid_gate = 1.0 / (1.0 + jnp.exp(-gate_in))
    silu_gate = gate_in * sigmoid_gate
    hidden = (silu_gate * up_in).astype(jnp.bfloat16)
    partial_out = matmul(hidden, down_use)
    returned = from_experts(partial_out, capacity)
    pick_out = jnp.take(returned, slot_index, axis=0, mode="fill", fill_value=0.0).reshape(
        tok_rows, TOP, model_width
    )
    final = residual + jnp.sum(pick_gates[..., None] * pick_out, axis=1)
    layer_output = final.astype(jnp.bfloat16)
    upstream = cotangent.astype(jnp.float32)
    pick_grad_rows = (pick_gates[..., None] * upstream[:, None, :]).reshape(
        tok_rows * TOP, model_width
    )
    send_grad = (
        jnp.zeros((EXPERTS * capacity, model_width), jnp.bfloat16)
        .at[slot_index]
        .set(pick_grad_rows.astype(jnp.bfloat16), mode="drop")
    )
    gate_grad = jnp.sum(upstream[:, None, :] * pick_out, axis=-1)
    pick_grad = pick_gates * (gate_grad - jnp.sum(pick_gates * gate_grad, axis=-1, keepdims=True))
    pick_onehot = expert_picks[..., None] == jnp.arange(EXPERTS, dtype=jnp.int32)[None, None, :]
    logit_grad = jnp.sum(jnp.where(pick_onehot, pick_grad[..., None], 0.0), axis=1).astype(
        jnp.bfloat16
    )
    router_gradient = contract_first(normed_two, logit_grad)
    normed_two_grad = contract_last(logit_grad, router_matrix)
    expert_grad = to_experts(send_grad.reshape(EXPERTS, capacity, model_width))
    hidden_grad = contract_last(expert_grad, down_use)
    down_gradient = contract_first(hidden, expert_grad)
    gate_in_grad = (
        hidden_grad * up_in * sigmoid_gate * (1.0 + gate_in * (1.0 - sigmoid_gate))
    ).astype(jnp.bfloat16)
    up_in_grad = (hidden_grad * silu_gate).astype(jnp.bfloat16)
    gate_gradient = contract_first(expert_in, gate_in_grad)
    up_gradient = contract_first(expert_in, up_in_grad)
    partial_in = contract_last(gate_in_grad, gate_use) + contract_last(up_in_grad, up_use)
    returned_grad = from_experts(partial_in, capacity)
    normed_two_grad = normed_two_grad + jnp.sum(
        jnp.take(returned_grad, slot_index, axis=0, mode="fill", fill_value=0.0).reshape(
            tok_rows, TOP, model_width
        ),
        axis=1,
    )
    weighted_two = normed_two_grad * gain_second
    second_gain_grad = jnp.sum(normed_two_grad * residual * scale_two, axis=0)
    residual_grad = (
        upstream
        + scale_two * weighted_two
        - residual * scale_two**3 * jnp.mean(weighted_two * residual, axis=-1, keepdims=True)
    )
    branch_grad = residual_grad.astype(jnp.bfloat16)
    output_gradient = contract_first(attended, branch_grad)
    attended_output_gradient = contract_last(branch_grad, output_matrix).astype(jnp.bfloat16)
    attended_head_rows = split_into_heads(attended_output_gradient, KEY_HEADS, HEAD_DIM)

    def attend_back(operands):
        query_group, key_group, value_group, grad_group, log_total = operands
        scores = (contract_last(query_group, key_group) * score_scale).reshape(
            query_group_width, tok_rows, key_token_rows
        )
        scores = jnp.where(allowed[None], scores, masked_score)
        probability = jnp.exp(scores - log_total.reshape(query_group_width, tok_rows, 1))
        probability_low = probability.astype(jnp.bfloat16).reshape(
            query_group_width * tok_rows, key_token_rows
        )
        probability_grad = contract_last(grad_group, value_group).reshape(
            query_group_width, tok_rows, key_token_rows
        )
        value_grad = contract_first(probability_low, grad_group)
        row_delta = jnp.sum(probability * probability_grad, axis=-1, keepdims=True)
        score_grad = (
            (probability * (probability_grad - row_delta))
            .astype(jnp.bfloat16)
            .reshape(query_group_width * tok_rows, key_token_rows)
        )
        query_grad = matmul(score_grad, key_group) * score_scale
        key_grad = contract_first(score_grad, query_group) * score_scale
        return (query_grad, key_grad, value_grad)

    query_grads, key_gradient_sums, value_gradient_sums = lax.map(
        attend_back,
        (query_head_rows, key_head_rows, value_head_rows, attended_head_rows, log_totals),
    )
    query_grad_rows = from_heads(query_grads, tok_rows)
    key_gradient_lines = key_gradient_sums.transpose(1, 0, 2).reshape(
        key_token_rows, KEY_HEADS * HEAD_DIM
    )
    value_gradient_lines = value_gradient_sums.transpose(1, 0, 2).reshape(
        key_token_rows, KEY_HEADS * HEAD_DIM
    )
    own_key_grad = key_gradient_lines[reach_back * tok_rows :]
    own_value_grad = value_gradient_lines[reach_back * tok_rows :]
    for distance in range(1, reach_back + 1):
        lower_row = (reach_back - distance) * tok_rows
        piece_key = key_gradient_lines[lower_row : lower_row + tok_rows]
        piece_value = value_gradient_lines[lower_row : lower_row + tok_rows]
        moved_key, moved_value = (
            from_behind(piece_key.astype(jnp.bfloat16), "dev", -distance).astype(piece_key.dtype),
            from_behind(piece_value.astype(jnp.bfloat16), "dev", -distance).astype(
                piece_value.dtype
            ),
        )
        own_key_grad = own_key_grad + moved_key
        own_value_grad = own_value_grad + moved_value
    query_pre_grad = rotate(query_grad_rows, cosine, -sine_part).astype(jnp.bfloat16)
    key_pre_grad = rotate(own_key_grad, cosine, -sine_part).astype(jnp.bfloat16)
    value_pre_grad = own_value_grad.astype(jnp.bfloat16)
    query_gradient = contract_first(normed_one, query_pre_grad)
    key_gradient = contract_first(normed_one, key_pre_grad)
    value_gradient = contract_first(normed_one, value_pre_grad)
    normed_one_grad = (
        contract_last(query_pre_grad, query_matrix)
        + contract_last(key_pre_grad, key_matrix)
        + contract_last(value_pre_grad, value_matrix)
    )
    weighted_one = normed_one_grad * gain_first
    first_gain_grad = jnp.sum(normed_one_grad * inputs * scale_one, axis=0)
    tokens_gradient = (
        residual_grad
        + scale_one * weighted_one
        - inputs * scale_one**3 * jnp.mean(weighted_one * inputs, axis=-1, keepdims=True)
    )
    reduced = (
        lax.psum_scatter(first_gain_grad, "dev", scatter_dimension=0, tiled=True),
        lax.psum_scatter(query_gradient, "dev", scatter_dimension=0, tiled=True),
        lax.psum_scatter(key_gradient, "dev", scatter_dimension=0, tiled=True),
        lax.psum_scatter(value_gradient, "dev", scatter_dimension=0, tiled=True),
        lax.psum_scatter(output_gradient, "dev", scatter_dimension=0, tiled=True),
        lax.psum_scatter(second_gain_grad, "dev", scatter_dimension=0, tiled=True),
        lax.psum_scatter(router_gradient, "dev", scatter_dimension=0, tiled=True),
    )
    return (
        layer_output,
        tokens_gradient,
        reduced[0],
        reduced[1],
        reduced[2],
        reduced[3],
        reduced[4],
        reduced[5],
        reduced[6],
        gate_gradient,
        up_gradient,
        down_gradient,
    )


def solution(mesh):
    return jax.shard_map(
        on_device,
        mesh=mesh,
        in_specs=(
            P("dev", None),
            P("dev"),
            P("dev", None),
            P("dev", None),
            P("dev"),
            P("dev", None),
            P("dev", None),
            P("dev", None),
            P("dev", None),
            P("dev"),
            P("dev", None),
            P(None, "dev"),
            P(None, "dev"),
            P("dev", None),
            P("dev", None),
        ),
        out_specs=(
            P("dev", None),
            P("dev", None),
            P("dev"),
            P("dev", None),
            P("dev", None),
            P("dev", None),
            P("dev", None),
            P("dev"),
            P("dev", None),
            P(None, "dev"),
            P(None, "dev"),
            P("dev", None),
        ),
        check_vma=False,
    )
```

profile of v0, /device:TPU:0, one launch (start us, length us, event | category | flops | bytes accessed | tf_op | source)
XLA Modules:
  0.0 2449.2 jit_solution(4133866229744441953)
XLA Ops:
  16.0 42.2 %all-reduce.5 = (bf16[1536]{0:T(1024)(128)(2,1)S(1)}, bf16[1536]{0:T(1024)(128)(2,1)S(1)}) all-reduce(bf16[1536]{0:T(1024)(128)(2,1)S(1)} %dynamic-update-slice, bf16[1536]{0:T(1024)(128)(2,1)S(1)} %dynamic-update-slice.1), channel_id=1, replica_groups=mesh['dev'=32] {'dev'}, use_global_device_ids=true, to_apply=%add | all-reduce | flops 3072 | bytes 12288
  58.7 8.0 scatter_custom_fusion
  66.9 11.8 gather_fusion
  78.7 9.1 reduce-window.6
  89.5 11.8 gather_fusion.1
  113.9 12.3 all-gather.10.cloned.1.call-done
  152.2 11.8 collective-permute-done.4
  168.0 9.9 collective-permute-start.8
  183.4 6.3 collective-permute-done.8
  191.7 6.7 collective-permute-start.12
  199.2 15.1 collective-permute-start.13
  226.0 5.5 copy.142
  239.5 89.9 %while.30 = (s32[]{:T(128)}, bf16[8,768,64]{1,2,0:T(8,128)(2,1)S(1)}, f32[8,768]{1,0:T(8,128)}, bf16[8,768,64]{2,1,0:T(8,128)(2,1)}, bf16[8,2304,64]{2,1,0:T(8,1...) while((s32[]{:T(128)}, ...), condition=%wide.region_4.5_spmd.clone.clone, body=%wide.region_1.4_spmd.clone.sunk.clone | while | flops 475987200 | bytes 31998048 | solution.py:204
  337.4 35.6 %scatter_custom_fusion.1 = bf16[2304,1536]{1,0:T(8,128)(2,1)} fusion(s32[2048]{0:T(1024)S(1)} %bitcast.384, bf16[256,1536]{1,0:T(8,128)(2,1)S(1)} %multiply_convert_fusion.4, s32[2048]{0:T(1024)S(1)} %get-tuple-element.357, bf16[]{:T(256)} %constant.124.clone.1), kind=kCustom, calls=%fused_computation.79 | custom fusion | bytes 7077890 | tf_op jit(solution)/shard_map/scatter | solution.py:225
  373.0 165.9 %all_to_all.20 = bf16[32,72,1536]{2,1,0:T(8,128)(2,1)S(1)} all-to-all(bf16[32,72,1536]{2,1,0:T(8,128)(2,1)} %bitcast.322), channel_id=1, replica_groups=mesh['dev'=32] {'dev'}, dimensions={0} | all-to-all | bytes 14155776 | tf_op jit(solution)/shard_map/all_to_all | solution.py:104
  542.8 6.1 multiply_convert_fusion.3
  548.9 7.0 fusion.115
  560.1 276.9 %all-gather = bf16[32,48,32]{1,2,0:T(8,128)(2,1)S(1)} all-gather(bf16[1,48,32]{1,2,0:T(8,128)(2,1)S(1)} %bitcast.383), channel_id=1, replica_groups=mesh['dev'=32] {'dev'}, dimensions={0}, use_global_device_ids=true | all-gather | bytes 101376 | tf_op jit(solution)/shard_map/all_gather | solution.py:148
  840.3 17.0 gather_fusion.2
  857.6 16.9 all-to-all-done.1
  874.4 19.3 gather_fusion.3
  893.8 6.4 fusion.48
  900.7 15.0 scatter_custom_fusion.2
  915.6 204.1 %all_to_all.21 = bf16[32,72,1536]{2,1,0:T(8,128)(2,1)S(1)} all-to-all(bf16[32,72,1536]{2,1,0:T(8,128)(2,1)} %bitcast.321), channel_id=1, replica_groups=mesh['dev'=32] {'dev'}, dimensions={0} | all-to-all | bytes 14155776 | tf_op jit(solution)/shard_map/all_to_all | solution.py:104
  1119.7 11.6 multiply_convert_fusion.1
  1131.4 6.4 fusion.116
  1137.8 7.3 convolution_add_fusion
  1149.2 314.0 %all-to-all-done.3 = f32[32,72,1536]{2,1,0:T(8,128)} async-done(((f32[32,72,1536]{2,1,0:T(8,128)}), f32[32,72,1536]{2,1,0:T(8,128)}, u32[]{:S(2)}, u32[]{:S(2)}) %all-to-all-start.3) | async-done | bytes 14155808 | tf_op jit(solution)/shard_map/all_to_all | solution.py:113
  1463.2 19.7 gather_fusion.4
  1483.0 22.7 bitcast_reduce_fusion
  1512.3 303.9 %while.31 = (s32[]{:T(128)}, f32[8,768,64]{1,2,0:T(8,128)}, f32[8,2304,64]{1,2,0:T(8,128)}, f32[8,2304,64]{1,2,0:T(8,128)}, bf16[8,768,64]{2,1,0:T(8,128)(2,1)},...) while((s32[]{:T(128)}, f32[8,768,64]{1,2,0:T(8,128)}, ...), condition=%wide.region_22.24_spmd.clone.clone, body=%wide.region_20.23_spmd.clone.sunk.clone | while | flops 1155664896 | bytes 68157624 | solution.py:310
  1515.4 5.1 fusion.221
  1520.5 7.1 exponential_convert_fusion.3
  1527.5 14.8 multiply_convert_fusion.7
  1558.5 7.1 exponential_convert_fusion.3
  1565.5 14.8 multiply_convert_fusion.7
  1591.4 5.1 fusion.221
  1596.5 7.1 exponential_convert_fusion.3
  1603.5 14.8 multiply_convert_fusion.7
  1634.4 7.1 exponential_convert_fusion.3
  1641.5 14.8 multiply_convert_fusion.7
  1672.4 7.1 exponential_convert_fusion.3
  1679.5 14.8 multiply_convert_fusion.7
  1710.4 7.1 exponential_convert_fusion.3
  1717.4 14.8 multiply_convert_fusion.7
  1748.3 7.1 exponential_convert_fusion.3
  1755.4 14.8 multiply_convert_fusion.7
  1781.2 5.1 fusion.221
  1786.3 7.1 exponential_convert_fusion.3
  1793.3 14.8 multiply_convert_fusion.7
  1836.0 8.4 collective-permute-done.28
  1858.7 20.0 collective-permute-done.23
  1881.3 6.2 collective-permute-done.22
  1890.0 11.1 collective-permute-done.19
  1916.2 5.2 fusion.103
  1921.4 24.7 %reduce-scatter.16.cloned.1.call-done = f32[48,32]{1,0:T(8,128)} async-done(((f32[1536,32]{1,0:T(8,128)}), f32[48,32]{1,0:T(8,128)}) %reduce-scatter.16.cloned.1.call-update) | async-done | bytes 6160
  1947.5 9.4 fusion.120
  1956.9 8.9 fusion.119
  1965.8 5.7 fusion.118
  1976.8 40.6 %all-reduce.4 = (f32[1536]{0:T(1024)S(1)}, f32[1536]{0:T(1024)S(1)}) all-reduce(f32[1536]{0:T(1024)S(1)} %get-tuple-element.261, f32[1536]{0:T(1024)S(1)} %copy-done.45), channel_id=2, replica_groups=mesh['dev'=32] {'dev'}, use_global_device_ids=true, to_apply=%region_25.27.clone | all-reduce | flops 3072 | bytes 24576
  2022.2 30.6 %reduce-scatter.12.cloned.1.call-done = f32[48,512]{1,0:T(8,128)} async-done(((f32[1536,512]{1,0:T(8,128)}), f32[48,512]{1,0:T(8,128)}) %reduce-scatter.12.cloned.1.call-update) | async-done | bytes 98320 | tf_op jit(solution)/shard_map/reduce_scatter | solution.py:357
  2052.9 106.5 %reduce-scatter.10.cloned.1.call-done = f32[48,512]{1,0:T(8,128)} async-done(((f32[1536,512]{1,0:T(8,128)}), f32[48,512]{1,0:T(8,128)}) %reduce-scatter.10.cloned.1.call-update) | async-done | bytes 98320 | tf_op jit(solution)/shard_map/reduce_scatter | solution.py:356
  2159.3 140.9 %reduce-scatter.14.cloned.1.call-done = f32[48,1536]{1,0:T(8,128)} async-done(((f32[1536,1536]{1,0:T(8,128)}), f32[48,1536]{1,0:T(8,128)}) %reduce-scatter.14.cloned.1.call-update) | async-done | bytes 294928 | tf_op jit(solution)/shard_map/reduce_scatter | solution.py:358
  2300.2 142.0 %reduce-scatter.8.cloned.1.call-done = f32[48,1536]{1,0:T(8,128)} async-done(((f32[1536,1536]{1,0:T(8,128)}), f32[48,1536]{1,0:T(8,128)}) %reduce-scatter.8.cloned.1.call-update) | async-done | bytes 294928 | tf_op jit(solution)/shard_map/reduce_scatter | solution.py:355
  (490 shorter events, 380.3 us)
Async XLA Ops:
  7.2 541.7 %copy-start = (bf16[512,1536]{1,0:T(8,128)(2,1)S(1)}, bf16[512,1536]{1,0:T(8,128)(2,1)}, u32[]{:S(2)}) copy-start(bf16[512,1536]{1,0:T(8,128)(2,1)} %param.34) | copy-start | bytes 4718596
  7.2 51.2 %copy-start.48 = (s32[256,8]{0,1:T(8,128)S(1)}, s32[256,8]{0,1:T(8,128)}, u32[]{:S(2)}) copy-start(s32[256,8]{0,1:T(8,128)} %param.24) | copy-start | bytes 24580
  7.2 94.1 %all-gather.8.cloned.1.call-start = ((), (), s32[]{:S(2)}) async-start(), calls=%async_computation.10 | async-start | bytes 1622016 | tf_op jit(solution)/shard_map/all_gather | solution.py:144
  7.9 118.2 %all-gather.10.cloned.1.call-start = ((), (), s32[]{:S(2)}) async-start(), calls=%async_computation.11 | async-start | bytes 1622016 | tf_op jit(solution)/shard_map/all_gather | solution.py:145
  8.7 222.8 %all-gather.6.cloned.1.call-start = ((), (), s32[]{:S(2)}) async-start(), calls=%async_computation.9 | async-start | bytes 4866048 | tf_op jit(solution)/shard_map/all_gather | solution.py:143
  9.4 322.5 %all-gather.12.cloned.1.call-start = ((), (), s32[]{:S(2)}) async-start(), calls=%async_computation.12 | async-start | bytes 4866048 | tf_op jit(solution)/shard_map/all_gather | solution.py:146
  13.6 217.9 %copy-start.43 = (f32[256]{0:T(256)}, f32[256]{0:T(256)S(1)}, u32[]{:S(2)}) copy-start(f32[256]{0:T(256)S(1)} %get-tuple-element.345) | copy-start | bytes 3076
  58.2 173.3 %copy-start.33 = (f32[1536]{0:T(1024)}, f32[1536]{0:T(1024)S(1)}, u32[]{:S(2)}) copy-start(f32[1536]{0:T(1024)S(1)} %convert_element_type.209) | copy-start | bytes 18436
  58.2 278.5 %copy-start.39 = (f32[1536]{0:T(1024)}, f32[1536]{0:T(1024)S(1)}, u32[]{:S(2)}) copy-start(f32[1536]{0:T(1024)S(1)} %convert_element_type.219) | copy-start | bytes 18436
  89.5 146.4 %copy-start.30 = (f32[256,32]{0,1:T(8,128)}, f32[256,32]{0,1:T(8,128)S(1)}, u32[]{:S(2)}) copy-start(f32[256,32]{0,1:T(8,128)S(1)} %get-tuple-element.343) | copy-start | bytes 98308
  103.6 40.5 %collective-permute-start.2 = (bf16[256,512]{0,1:T(8,128)(2,1)S(1)}, bf16[256,512]{0,1:T(8,128)(2,1)}, u32[]{:S(2)}, u32[]{:S(2)}) collective-permute-start(bf16[256,512]{0,1:T(8,128)(2,1)S(1)} %bitcast.349), channel_id=1, source_target_pairs={{0,6},{1,7},{2,8},{3,9},{4,10},{5,11},{6,12},{7,13},{8,14},{9,15},... | collective-permute-start | bytes 786440 | tf_op jit(solution)/shard_map/ppermute | solution.py:21
  108.6 30.5 %collective-permute-start.1 = (bf16[256,512]{0,1:T(8,128)(2,1)S(1)}, bf16[256,512]{0,1:T(8,128)(2,1)}, u32[]{:S(2)}, u32[]{:S(2)}) collective-permute-start(bf16[256,512]{0,1:T(8,128)(2,1)S(1)} %bitcast.350), channel_id=1, source_target_pairs={{0,7},{1,8},{2,9},{3,10},{4,11},{5,12},{6,13},{7,14},{8,15},{9,16}... | collective-permute-start | bytes 786440 | tf_op jit(solution)/shard_map/ppermute | solution.py:21
  110.6 23.2 collective-permute-start
  128.2 92.0 %collective-permute-start.15 = (bf16[256,512]{1,0:T(8,128)(2,1)S(1)}, bf16[256,512]{1,0:T(8,128)(2,1)S(1)}, u32[]{:S(2)}, u32[]{:S(2)}) collective-permute-start(bf16[256,512]{1,0:T(8,128)(2,1)S(1)} %convolution_convert_fusion.1), channel_id=1, source_target_pairs={{0,1},{1,2},{2,3},{3,4},{4,5},{5,6},{6,7},{7,8},{8,9},{9,10},{10,1... | collective-permute-start | bytes 786440 | tf_op jit(solution)/shard_map/ppermute | solution.py:21
  130.4 89.1 %collective-permute-start.14 = (bf16[256,512]{1,0:T(8,128)(2,1)S(1)}, bf16[256,512]{1,0:T(8,128)(2,1)S(1)}, u32[]{:S(2)}, u32[]{:S(2)}) collective-permute-start(bf16[256,512]{1,0:T(8,128)(2,1)S(1)} %convolution_convert_fusion.1), channel_id=1, source_target_pairs={{0,2},{1,3},{2,4},{3,5},{4,6},{5,7},{6,8},{7,9},{8,10},{9,11},{10,... | collective-permute-start | bytes 786440 | tf_op jit(solution)/shard_map/ppermute | solution.py:21
  133.8 14.2 collective-permute-start.3
  139.1 24.9 %collective-permute-start.4 = (bf16[256,512]{0,1:T(8,128)(2,1)S(1)}, bf16[256,512]{0,1:T(8,128)(2,1)S(1)}, u32[]{:S(2)}, u32[]{:S(2)}) collective-permute-start(bf16[256,512]{0,1:T(8,128)(2,1)S(1)} %bitcast.353), channel_id=1, source_target_pairs={{0,4},{1,5},{2,6},{3,7},{4,8},{5,9},{6,10},{7,11},{8,12},{9,13},{1... | collective-permute-start | bytes 786440 | tf_op jit(solution)/shard_map/ppermute | solution.py:21
  144.2 21.8 collective-permute-start.5
  148.0 20.1 collective-permute-start.6
  164.0 14.7 collective-permute-start.7
  166.0 33.2 %collective-permute-start.10 = (bf16[256,512]{1,0:T(8,128)(2,1)S(1)}, bf16[256,512]{1,0:T(8,128)(2,1)S(1)}, u32[]{:S(2)}, u32[]{:S(2)}) collective-permute-start(bf16[256,512]{1,0:T(8,128)(2,1)S(1)} %convolution_convert_fusion.1), channel_id=1, source_target_pairs={{0,6},{1,7},{2,8},{3,9},{4,10},{5,11},{6,12},{7,13},{8,14},{9,15},... | collective-permute-start | bytes 786440 | tf_op jit(solution)/shard_map/ppermute | solution.py:21
  168.0 21.7 collective-permute-start.8
  178.7 13.1 collective-permute-start.9
  189.7 25.3 %collective-permute-start.11 = (bf16[256,512]{1,0:T(8,128)(2,1)S(1)}, bf16[256,512]{1,0:T(8,128)(2,1)S(1)}, u32[]{:S(2)}, u32[]{:S(2)}) collective-permute-start(bf16[256,512]{1,0:T(8,128)(2,1)S(1)} %convolution_convert_fusion.1), channel_id=1, source_target_pairs={{0,5},{1,6},{2,7},{3,8},{4,9},{5,10},{6,11},{7,12},{8,13},{9,14},{... | collective-permute-start | bytes 786440 | tf_op jit(solution)/shard_map/ppermute | solution.py:21
  191.7 24.0 collective-permute-start.12
  199.2 19.6 collective-permute-start.13
  336.7 36.3 %copy-start.46 = (f32[256]{0:T(256)}, f32[256]{0:T(256)S(1)}, u32[]{:S(2)}) copy-start(f32[256]{0:T(256)S(1)} %get-tuple-element.347) | copy-start | bytes 3076
  337.4 35.6 %copy-start.14 = (bf16[256,1536]{1,0:T(8,128)(2,1)}, bf16[256,1536]{1,0:T(8,128)(2,1)S(1)}, u32[]{:S(2)}) copy-start(bf16[256,1536]{1,0:T(8,128)(2,1)S(1)} %multiply_convert_fusion.4) | copy-start | bytes 2359300
  373.0 165.9 %copy-start.52 = (bf16[1536,512]{1,0:T(8,128)(2,1)S(1)}, bf16[1536,512]{1,0:T(8,128)(2,1)}, u32[]{:S(2)}) copy-start(bf16[1536,512]{1,0:T(8,128)(2,1)} %param.32) | copy-start | bytes 4718596
  555.9 318.6 %all-to-all-start.1 = ((f32[32,72,1536]{2,1,0:T(8,128)}), f32[32,72,1536]{2,1,0:T(8,128)}, u32[]{:S(2)}, u32[]{:S(2)}) async-start(f32[32,72,1536]{2,1,0:T(8,128)} %bitcast.325), calls=%async_computation.1 | async-start | bytes 28311552 | tf_op jit(solution)/shard_map/all_to_all | solution.py:113
  1145.1 318.1 %all-to-all-start.3 = ((f32[32,72,1536]{2,1,0:T(8,128)}), f32[32,72,1536]{2,1,0:T(8,128)}, u32[]{:S(2)}, u32[]{:S(2)}) async-start(f32[32,72,1536]{2,1,0:T(8,128)} %bitcast.320), calls=%async_computation.3 | async-start | bytes 28311552 | tf_op jit(solution)/shard_map/all_to_all | solution.py:113
  1149.1 797.0 %reduce-scatter.16.cloned.1.call-start = ((), (), s32[]{:S(2)}) async-start(), calls=%async_computation.17 | async-start | bytes 811008
  1149.2 356.5 %copy-start.37 = (bf16[256,32]{0,1:T(8,128)(2,1)}, bf16[256,32]{0,1:T(8,128)(2,1)S(1)}, u32[]{:S(2)}) copy-start(bf16[256,32]{0,1:T(8,128)(2,1)S(1)} %select_reduce_fusion) | copy-start | bytes 49156
  1482.9 22.7 copy-start.7
  1482.9 22.7 copy-start.29
  1482.9 22.8 copy-start.40
  1482.9 22.8 copy-start.47
  1482.9 24.1 copy-start.18
  1819.1 10.3 collective-permute-start.31
  1820.4 10.3 collective-permute-start.24
  1821.7 10.3 collective-permute-start.30
  1823.0 12.9 collective-permute-start.29
  1824.3 20.0 collective-permute-start.28
  1829.4 15.0 collective-permute-start.27
  1830.7 13.7 collective-permute-start.26
  1832.1 12.7 collective-permute-start.25
  1834.7 218.1 %reduce-scatter.12.cloned.1.call-start = ((), (), s32[]{:S(2)}) async-start(), calls=%async_computation.15 | async-start | bytes 3244032 | tf_op jit(solution)/shard_map/reduce_scatter | solution.py:357
  1849.3 310.0 %reduce-scatter.10.cloned.1.call-start = ((), (), s32[]{:S(2)}) async-start(), calls=%async_computation.14 | async-start | bytes 3244032 | tf_op jit(solution)/shard_map/reduce_scatter | solution.py:356
  1852.2 49.1 %copy-start.31 = (f32[256,32]{0,1:T(8,128)S(1)}, f32[256,32]{0,1:T(8,128)}, u32[]{:S(2)}) copy-start(f32[256,32]{0,1:T(8,128)} %copy-done.30) | copy-start | bytes 98308
  1852.2 49.1 %copy-start.35 = (f32[256,32]{0,1:T(8,128)S(1)}, f32[256,32]{0,1:T(8,128)}, u32[]{:S(2)}) copy-start(f32[256,32]{0,1:T(8,128)} %get-tuple-element.341) | copy-start | bytes 98308
  1852.2 26.5 %collective-permute-start.23 = (bf16[256,512]{0,1:T(8,128)(2,1)S(1)}, bf16[256,512]{0,1:T(8,128)(2,1)S(1)}, u32[]{:S(2)}, u32[]{:S(2)}) collective-permute-start(bf16[256,512]{0,1:T(8,128)(2,1)S(1)} %bitcast.375), channel_id=1, source_target_pairs={{8,0},{9,1},{10,2},{11,3},{12,4},{13,5},{14,6},{15,7},{16,8},{17,9... | collective-permute-start | bytes 786440 | tf_op jit(solution)/shard_map/ppermute | solution.py:21
  1853.5 26.5 %collective-permute-start.16 = (bf16[256,512]{0,1:T(8,128)(2,1)S(1)}, bf16[256,512]{0,1:T(8,128)(2,1)S(1)}, u32[]{:S(2)}, u32[]{:S(2)}) collective-permute-start(bf16[256,512]{0,1:T(8,128)(2,1)S(1)} %bitcast.373), channel_id=1, source_target_pairs={{1,0},{2,1},{3,2},{4,3},{5,4},{6,5},{7,6},{8,7},{9,8},{10,9},{11,1... | collective-permute-start | bytes 786440 | tf_op jit(solution)/shard_map/ppermute | solution.py:21
  1854.8 32.7 %collective-permute-start.22 = (bf16[256,512]{0,1:T(8,128)(2,1)S(1)}, bf16[256,512]{0,1:T(8,128)(2,1)S(1)}, u32[]{:S(2)}, u32[]{:S(2)}) collective-permute-start(bf16[256,512]{0,1:T(8,128)(2,1)S(1)} %bitcast.371), channel_id=1, source_target_pairs={{7,0},{8,1},{9,2},{10,3},{11,4},{12,5},{13,6},{14,7},{15,8},{16,9}... | collective-permute-start | bytes 786440 | tf_op jit(solution)/shard_map/ppermute | solution.py:21
  1856.1 33.8 %collective-permute-start.21 = (bf16[256,512]{0,1:T(8,128)(2,1)S(1)}, bf16[256,512]{0,1:T(8,128)(2,1)S(1)}, u32[]{:S(2)}, u32[]{:S(2)}) collective-permute-start(bf16[256,512]{0,1:T(8,128)(2,1)S(1)} %bitcast.369), channel_id=1, source_target_pairs={{6,0},{7,1},{8,2},{9,3},{10,4},{11,5},{12,6},{13,7},{14,8},{15,9},... | collective-permute-start | bytes 786440 | tf_op jit(solution)/shard_map/ppermute | solution.py:21
  1857.4 32.5 %collective-permute-start.20 = (bf16[256,512]{0,1:T(8,128)(2,1)S(1)}, bf16[256,512]{0,1:T(8,128)(2,1)S(1)}, u32[]{:S(2)}, u32[]{:S(2)}) collective-permute-start(bf16[256,512]{0,1:T(8,128)(2,1)S(1)} %bitcast.368), channel_id=1, source_target_pairs={{5,0},{6,1},{7,2},{8,3},{9,4},{10,5},{11,6},{12,7},{13,8},{14,9},{... | collective-permute-start | bytes 786440 | tf_op jit(solution)/shard_map/ppermute | solution.py:21
  1878.7 22.3 collective-permute-start.19
  1880.0 21.0 collective-permute-start.18
  1887.5 13.5 collective-permute-start.17
  1903.9 396.3 %reduce-scatter.14.cloned.1.call-start = ((), (), s32[]{:S(2)}) async-start(), calls=%async_computation.16 | async-start | bytes 9732096 | tf_op jit(solution)/shard_map/reduce_scatter | solution.py:358
  1910.6 531.7 %reduce-scatter.8.cloned.1.call-start = ((), (), s32[]{:S(2)}) async-start(), calls=%async_computation.13 | async-start | bytes 9732096 | tf_op jit(solution)/shard_map/reduce_scatter | solution.py:355
  1947.5 18.3 slice-start.2
  1956.9 14.6 slice-start.4
  1974.8 43.9 %copy-start.50 = (f32[256]{0:T(256)S(1)}, f32[256]{0:T(256)}, u32[]{:S(2)}) copy-start(f32[256]{0:T(256)} %get-tuple-element.344) | copy-start | bytes 3076
  2018.6 423.6 %copy-start.1 = (bf16[512,1536]{1,0:T(8,128)(2,1)S(1)}, bf16[512,1536]{1,0:T(8,128)(2,1)}, u32[]{:S(2)}) copy-start(bf16[512,1536]{1,0:T(8,128)(2,1)} %param.34) | copy-start | bytes 4718596
  (56 other events, 286.9 us)
Sparse Core Ops, SparseCore 0:
  10.9 57.6 all-gather.7
  71.5 54.6 all-gather.9
  129.1 71.4 all-gather.5
  203.4 68.6 all-gather.11
  1834.9 111.1 reduce-scatter.15
  1952.0 100.8 reduce-scatter.11
  2058.8 100.4 reduce-scatter.9
  2165.8 134.3 reduce-scatter.13
  2307.7 134.4 reduce-scatter.7
where the time goes:
time: 2460 us; the launch traced here: 2450 us
  waiting for transfers between devices  861 us (35%)
  blocking collectives  730 us (30%)
  matrix products  305 us (12%)
  other arithmetic  236 us (10%)
  local copies, waits for them, and re-layouts  205 us (8%)
  starting transfers between devices  96.2 us (4%)
    all_to_all x2, blocking collectives, to_experts(): lax.all_to_all(copied, 'dev', split_axis=0, concat_axis=0, tiled=True)  370 us
    all_to_all x2, waiting for transfers between devices, from_experts(): lax.all_to_all(partial_rows.reshape(devices, capacity, model_width), 'dev...  331 us
    all_gather x1, blocking collectives, on_device(): lax.all_gather(router_weight, 'dev', axis=0, tiled=True)  277 us
    dot_general x32, matrix products, contract_last(): lax.dot_general(first_operand, second_operand, (((1,), (1,)), ((), ())),...  151 us
    reduce_scatter x1, waiting for transfers between devices, on_device(): lax.psum_scatter(query_gradient, 'dev', scatter_dimension=0, tiled=True)  142 us
    reduce_scatter x1, waiting for transfers between devices, on_device(): lax.psum_scatter(output_gradient, 'dev', scatter_dimension=0, tiled=True)  141 us
    sub x8, other arithmetic, attend_back(): probability_grad - row_delta  118 us
    reduce_scatter x1, waiting for transfers between devices, on_device(): lax.psum_scatter(key_gradient, 'dev', scatter_dimension=0, tiled=True)  106 us
  transfers between devices with their start and end apart: 43, of which 18 were waited for; matrix products, arithmetic and copies ran while one was open for 11% of the time, Pallas kernels for 0%

commit v1 on v0

v1 whole, which is shorter than its diff:
```python
import functools
import jax, jax.numpy as jnp
from jax import lax
from jax.experimental import pallas as pl
from jax.experimental.pallas import tpu as pltpu

MESH = pl.DeviceIdType.MESH


def place():
    me = lax.axis_index("dev")
    return lax.rem(me // 8, 4), lax.rem(me // 4, 2), lax.rem(me // 2, 2), lax.rem(me, 2)


def number(z, y, x, c):
    return ((z * 2 + y) * 2 + x) * 2 + c


def greet(partners):
    barrier = pltpu.get_barrier_semaphore()
    for partner in partners:
        pl.semaphore_signal(barrier, inc=1, device_id=(partner,), device_id_type=MESH)
    pl.semaphore_wait(barrier, len(partners))


def partners_of(z, y, x, c):
    return [
        number(z, y, x, 1 - c),
        number(z, y, 1 - x, c),
        number(z, 1 - y, x, c),
        number(lax.rem(z + 1, 4), y, x, c),
        number(lax.rem(z + 2, 4), y, x, c),
        number(lax.rem(z + 3, 4), y, x, c),
    ]


def gather_kernel(rows, pieces, x_ref, o_ref, local_sem, ss, rs):
    z, y, x, c = place()
    greet(partners_of(z, y, x, c))
    sibling = number(z, y, x, 1 - c)
    me = number(z, y, x, c)
    around = (number(z, 1 - y, x, c), number(z, y, 1 - x, c))

    def part(ref, block, p):
        r0, nr, c0, nc = pieces[p]
        return ref.at[pl.ds(pl.multiple_of(block * rows + r0, 16), nr), pl.ds(c0, nc)]

    def copy(block, p, slot, target, own=False):
        source = part(x_ref, 0, p) if own else part(o_ref, block, p)
        return pltpu.make_async_remote_copy(
            src_ref=source, dst_ref=part(o_ref, block, p),
            send_sem=ss.at[p * 31 + slot], recv_sem=rs.at[p * 31 + slot],
            device_id=(target,), device_id_type=MESH)

    pending = []

    def send(*args, **kw):
        cp = copy(*args, **kw)
        cp.start()
        pending.append(cp)

    def at(k, fy, fx):
        return number(lax.rem(z + 4 - k, 4), (1 - y) if fy else y, (1 - x) if fx else x, c)

    local = pltpu.make_async_copy(x_ref, o_ref.at[pl.ds(pl.multiple_of(me * rows, 16), rows), :], local_sem)
    local.start()
    order = (0, 1, 3, 2)
    far = ((1, 0), (0, 1))
    for k in (1, 3, 2):
        for p in range(2):
            send(me, p, k - 1, number(lax.rem(z + k, 4), y, x, c), own=True)
    for k in order:
        for p in range(2):
            block = at(k, 0, 0)
            if k:
                copy(block, p, k - 1, sibling).wait_recv()
            own = k == 0
            send(block, p, 3 + k, around[p], own=own)
            send(block, p, 7 + k, around[1 - p], own=own)
            send(block, p, 15 + k, sibling, own=own)
    for k in order:
        for p in range(2):
            fy, fx = far[p]
            block = at(k, fy, fx)
            copy(block, p, 3 + k, sibling).wait_recv()
            send(block, p, 11 + k, around[1 - p])
            send(block, p, 19 + k, sibling)
    for j, slot in ((0, 7), (1, 11)):
        for k in order:
            for p in range(2):
                fy, fx = (1, 1) if j else (1 - far[p][0], 1 - far[p][1])
                block = at(k, fy, fx)
                copy(block, p, slot + k, sibling).wait_recv()
                send(block, p, 23 + 4 * j + k, sibling)
    for k in range(4):
        for p in range(2):
            for s in (15, 19, 23, 27):
                copy(me, p, s + k, sibling).wait_recv()
    for cp in pending:
        cp.wait_send()
    local.wait()


def gather_all(block, cid, by_rows):
    rows, cols = block.shape
    if by_rows:
        pieces = ((0, rows // 2, 0, cols), (rows // 2, rows // 2, 0, cols))
    else:
        half = (cols // 256) * 128
        pieces = ((0, rows, 0, half), (0, rows, half, cols - half))
    return pl.pallas_call(
        functools.partial(gather_kernel, rows, pieces),
        out_shape=jax.ShapeDtypeStruct((32 * rows, cols), block.dtype),
        in_specs=[pl.BlockSpec(memory_space=pl.ANY)],
        out_specs=pl.BlockSpec(memory_space=pl.ANY),
        scratch_shapes=[pltpu.SemaphoreType.DMA, pltpu.SemaphoreType.DMA((62,)), pltpu.SemaphoreType.DMA((62,))],
        compiler_params=pltpu.CompilerParams(collective_id=cid, has_side_effects=True),
        name="gather_all",
    )(block)


def reduce_kernel(rows, cols, pieces, g_ref, o_ref, acc, own, ra, rb, rz, own_sem, ssem, rsem, sa, ra_sem, sb, rb_sem, sz, rz_sem):
    z, y, x, c = place()
    greet(partners_of(z, y, x, c))
    sibling = number(z, y, x, 1 - c)
    around = (number(z, y, 1 - x, c), number(z, 1 - y, x, c))
    blocks = [(dy, dx, k) for dy, dx in ((1, 1), (1, 0), (0, 1), (0, 0)) for k in (2, 1, 3, 0)]

    def where(dy, dx, k):
        return lax.rem(z + k, 4), (1 - y) if dy else y, (1 - x) if dx else x

    def lane(dy, dx, k):
        zz, yy, xx = where(dy, dx, k)
        return (zz * 2 + yy) * 2 + xx

    def chip_rows(dy, dx, k, core):
        zz, yy, xx = where(dy, dx, k)
        return g_ref.at[pl.ds(pl.multiple_of(number(zz, yy, xx, core) * rows, 16), rows), :]

    def to_sibling(n):
        dy, dx, k = blocks[n]
        return pltpu.make_async_remote_copy(
            src_ref=chip_rows(dy, dx, k, 1 - c), dst_ref=acc.at[lane(dy, dx, k)],
            send_sem=ssem.at[n], recv_sem=rsem.at[n], device_id=(sibling,), device_id_type=MESH)

    def load(n):
        return pltpu.make_async_copy(chip_rows(*blocks[n], c), own.at[n % 2], own_sem.at[n % 2])

    def part(ref, p):
        r0, nr, c0, nc = pieces[p]
        return ref.at[pl.ds(r0, nr), pl.ds(c0, nc)]

    def first(p, d2, k, dy, dx):
        return pltpu.make_async_remote_copy(
            src_ref=part(acc.at[lane(dy, dx, k)], p), dst_ref=ra.at[p, d2, k],
            send_sem=sa.at[p, d2, k], recv_sem=ra_sem.at[p, d2, k], device_id=(around[p],), device_id_type=MESH)

    def second(p, k):
        dy, dx = (1, 0) if p == 0 else (0, 1)
        return pltpu.make_async_remote_copy(
            src_ref=part(acc.at[lane(dy, dx, k)], p), dst_ref=rb.at[p, k],
            send_sem=sb.at[p, k], recv_sem=rb_sem.at[p, k], device_id=(around[1 - p],), device_id_type=MESH)

    def third(p, k):
        return pltpu.make_async_remote_copy(
            src_ref=part(acc.at[lane(0, 0, k)], p), dst_ref=rz.at[p, k - 1],
            send_sem=sz.at[p, k - 1], recv_sem=rz_sem.at[p, k - 1],
            device_id=(number(lax.rem(z + k, 4), y, x, c),), device_id_type=MESH)

    step = 16

    def add(out, terms, nr):
        def chunk(i, _):
            at = pl.ds(pl.multiple_of(i * step, step), step)
            total = terms[0][at, :].astype(jnp.float32)
            for t in terms[1:]:
                total = total + t[at, :].astype(jnp.float32)
            out[at, :] = total.astype(out.dtype)
            return 0
        lax.fori_loop(0, nr // step, chunk, 0)

    for n in range(16):
        to_sibling(n).start()
    load(0).start()
    for n in range(16):
        dy, dx, k = blocks[n]
        if n + 1 < 16:
            load(n + 1).start()
        load(n).wait()
        to_sibling(n).wait_recv()
        block = acc.at[lane(dy, dx, k)]
        add(block, [block, own.at[n % 2]], rows)
        if dx:
            first(0, dy, k, dy, dx).start()
        if dy:
            first(1, dx, k, dy, dx).start()
    for k in (2, 1, 3, 0):
        for p in range(2):
            dy, dx = (1, 0) if p == 0 else (0, 1)
            first(p, 1, k, 1, 1).wait_recv()
            block = part(acc.at[lane(dy, dx, k)], p)
            add(block, [block, ra.at[p, 1, k]], pieces[p][1])
            second(p, k).start()
    for k in (2, 1, 3, 0):
        for p in range(2):
            first(p, 0, k, 1 - p, p).wait_recv()
            second(p, k).wait_recv()
            block = part(acc.at[lane(0, 0, k)], p)
            if k:
                add(block, [block, ra.at[p, 0, k], rb.at[p, k]], pieces[p][1])
                third(p, k).start()
    for p in range(2):
        for k in range(1, 4):
            third(p, k).wait_recv()
        block = part(acc.at[lane(0, 0, 0)], p)
        add(part(o_ref, p), [block, ra.at[p, 0, 0], rb.at[p, 0]] + [rz.at[p, j] for j in range(3)], pieces[p][1])
    for n in range(16):
        to_sibling(n).wait_send()
    for p in range(2):
        for k in range(4):
            first(p, 0, k, 1 - p, p).wait_send()
            first(p, 1, k, 1, 1).wait_send()
            second(p, k).wait_send()
            if k:
                third(p, k).wait_send()


def reduce_all(dense, cid, by_rows, out_dtype=jnp.float32):
    rows, cols = dense.shape[0] // 32, dense.shape[1]
    if by_rows:
        pieces = ((0, rows // 2, 0, cols), (rows // 2, rows // 2, 0, cols))
    else:
        half = (cols // 256) * 128
        assert cols == 2 * half
        pieces = ((0, rows, 0, half), (0, rows, half, cols - half))
    pr, pc = pieces[0][1], pieces[0][3]
    dma = pltpu.SemaphoreType.DMA
    return pl.pallas_call(
        functools.partial(reduce_kernel, rows, cols, pieces),
        out_shape=jax.ShapeDtypeStruct((rows, cols), out_dtype),
        in_specs=[pl.BlockSpec(memory_space=pl.ANY)],
        out_specs=pl.BlockSpec(memory_space=pltpu.VMEM),
        scratch_shapes=[
            pltpu.VMEM((16, rows, cols), dense.dtype),
            pltpu.VMEM((2, rows, cols), dense.dtype),
            pltpu.VMEM((2, 2, 4, pr, pc), dense.dtype),
            pltpu.VMEM((2, 4, pr, pc), dense.dtype),
            pltpu.VMEM((2, 3, pr, pc), dense.dtype),
            dma((2,)), dma((16,)), dma((16,)), dma((2, 2, 4)), dma((2, 2, 4)), dma((2, 4)), dma((2, 4)), dma((2, 3)), dma((2, 3)),
        ],
        compiler_params=pltpu.CompilerParams(collective_id=cid, has_side_effects=True, vmem_limit_bytes=56 * 2**20),
        name="reduce_all",
    )(dense)


from jax.sharding import PartitionSpec as P

QUERY_HEADS = 24
KEY_HEADS = 8
HEAD_DIM = 64
GROUP = QUERY_HEADS // KEY_HEADS
TOP = 8
EXPERTS = 32
MAXDOC = 2000
EPSILON = 1e-06
MASKED = -1e30
QKV = (QUERY_HEADS + 2 * KEY_HEADS) * HEAD_DIM
F32 = jnp.float32
BF16 = jnp.bfloat16


def meshed():
    return lax.axis_size("dev") == 32


def dims(a, b, ca, cb):
    return lax.dot_general(a, b, (((ca,), (cb,)), ((), ())), preferred_element_type=F32)


def window_kernel(rows, kv_ref, o_ref, lsem, ss, rs):
    z, y, x, c = place()
    p = y * 2 + x
    sibling = number(z, y, x, 1 - c)
    up = number(lax.rem(z + 1, 4), y, x, c)
    down = number(lax.rem(z + 3, 4), y, x, c)

    def chip(q):
        return (z * 4 + q) * 2 + c

    near = [chip(lax.rem(p + d, 4)) for d in (1, 2, 3)]
    greet([sibling, up, down] + near)

    def slot(s, core):
        return o_ref.at[:, pl.ds(pl.multiple_of((2 * s + core) * rows, 16), rows), :]

    def copy(source, s, n, target):
        return pltpu.make_async_remote_copy(
            src_ref=source, dst_ref=slot(s, c), send_sem=ss.at[n], recv_sem=rs.at[n],
            device_id=(target,), device_id_type=MESH)

    own_in = pltpu.make_async_copy(kv_ref, slot(4, c), lsem.at[0])
    own_in.start()
    to_up = copy(kv_ref, 0, 0, up)

    @pl.when(z < 3)
    def _():
        to_up.start()

    stand_in = pltpu.make_async_copy(kv_ref, slot(0, c), lsem.at[1])

    @pl.when(z == 0)
    def _():
        stand_in.start()

    for d in (1, 3, 2):
        @pl.when(p + d < 4)
        def _(d=d):
            copy(kv_ref, 4 - d, d, near[d - 1]).start()

    to_sibling = {4: copy(kv_ref, 4, 4, sibling)}
    to_sibling[4].start()

    @pl.when(z == 0)
    def _():
        stand_in.wait()

    @pl.when(z > 0)
    def _():
        to_up.wait_recv()

    for d in (3, 1, 2):
        @pl.when(p + d >= 4)
        def _(d=d):
            copy(slot(0, c), 4 - d, d, near[d - 1]).start()

    to_sibling[0] = copy(slot(0, c), 0, 5, sibling)
    to_sibling[0].start()
    for d in (1, 3, 2):
        copy(kv_ref, 4 - d, d, near[d - 1]).wait_recv()
        to_sibling[4 - d] = copy(slot(4 - d, c), 4 - d, 5 + d, sibling)
        to_sibling[4 - d].start()
    for s in range(5):
        pltpu.make_async_remote_copy(
            src_ref=kv_ref, dst_ref=slot(s, 1 - c), send_sem=ss.at[0],
            recv_sem=rs.at[{4: 4, 0: 5}.get(s, 9 - s)], device_id=(sibling,), device_id_type=MESH).wait_recv()
    own_in.wait()

    @pl.when(z < 3)
    def _():
        to_up.wait_send()

    for d in (1, 2, 3):
        copy(kv_ref, 4 - d, d, near[d - 1]).wait_send()
    for s in range(5):
        to_sibling[s].wait_send()


def window_of(kv):
    rows, width = kv.shape[1:]
    if meshed():
        dma = pltpu.SemaphoreType.DMA
        full = pl.pallas_call(
            functools.partial(window_kernel, rows),
            out_shape=jax.ShapeDtypeStruct((2, 10 * rows, width), kv.dtype),
            in_specs=[pl.BlockSpec(memory_space=pl.ANY)],
            out_specs=pl.BlockSpec(memory_space=pl.ANY),
            scratch_shapes=[dma((2,)), dma((9,)), dma((9,))],
            compiler_params=pltpu.CompilerParams(collective_id=11, has_side_effects=True),
            name="window",
        )(kv)
        return full, lax.rem(lax.axis_index("dev"), 2)
    devices = lax.axis_size("dev")
    back = (MAXDOC + rows - 2) // rows
    parts = [
        lax.ppermute(kv, "dev", [(i - d, i) for i in range(d, devices)]) for d in range(back, 0, -1)
    ]
    return jnp.concatenate(parts + [kv, jnp.zeros_like(kv)], axis=1), jnp.int32(0)


def unwindow_kernel(rows, g_ref, o_ref, mine, got, near_got, far, lsem, ss, rs):
    z, y, x, c = place()
    p = y * 2 + x
    sibling = number(z, y, x, 1 - c)
    up = number(lax.rem(z + 1, 4), y, x, c)
    down = number(lax.rem(z + 3, 4), y, x, c)

    def chip(q):
        return (z * 4 + q) * 2 + c

    ahead = [chip(lax.rem(p + d, 4)) for d in (1, 2, 3)]
    behind = [chip(lax.rem(p + 4 - d, 4)) for d in (1, 2, 3)]
    greet([sibling, up, down] + ahead)

    def slot(s, core):
        return g_ref.at[:, pl.ds(pl.multiple_of((2 * s + core) * rows, 16), rows), :]

    def to_sibling(s):
        return pltpu.make_async_remote_copy(
            src_ref=slot(s, 1 - c), dst_ref=got.at[s], send_sem=ss.at[s], recv_sem=rs.at[s],
            device_id=(sibling,), device_id_type=MESH)

    def load(s):
        return pltpu.make_async_copy(slot(s, c), mine.at[s], lsem.at[s])

    def to_owner(d):
        return pltpu.make_async_remote_copy(
            src_ref=got.at[4 - d], dst_ref=near_got.at[d - 1], send_sem=ss.at[4 + d], recv_sem=rs.at[4 + d],
            device_id=(behind[d - 1],), device_id_type=MESH)

    to_down = pltpu.make_async_remote_copy(
        src_ref=got.at[0], dst_ref=far, send_sem=ss.at[8], recv_sem=rs.at[8],
        device_id=(down,), device_id_type=MESH)
    order = (3, 1, 2, 0, 4)
    for s in order:
        to_sibling(s).start()
        load(s).start()

    def rowwise(body):
        for h in range(2):
            def step(i, _, h=h):
                body(h, pl.ds(pl.multiple_of(i * 32, 32), 32))
                return 0
            lax.fori_loop(0, rows // 32, step, 0)

    for s in order:
        load(s).wait()
        to_sibling(s).wait_recv()

        def both(h, at, s=s):
            total = got[s, h, at, :].astype(F32) + mine[s, h, at, :].astype(F32)
            if s == 4:
                o_ref[h, at, :] = total
            else:
                got[s, h, at, :] = total.astype(BF16)
        rowwise(both)
        if 0 < s < 4:
            to_owner(4 - s).start()
    for d in (1, 3, 2):
        to_owner(d).wait_recv()

        @pl.when(p + d < 4)
        def _(d=d):
            def body(h, at):
                o_ref[h, at, :] += near_got[d - 1, h, at, :].astype(F32)
            rowwise(body)

        @pl.when(p + d >= 4)
        def _(d=d):
            def body(h, at):
                total = got[0, h, at, :].astype(F32) + near_got[d - 1, h, at, :].astype(F32)
                got[0, h, at, :] = total.astype(BF16)
            rowwise(body)

    @pl.when(z > 0)
    def _():
        to_down.start()

    @pl.when(z < 3)
    def _():
        to_down.wait_recv()

        def body(h, at):
            o_ref[h, at, :] += far[h, at, :].astype(F32)
        rowwise(body)

    @pl.when(z > 0)
    def _():
        to_down.wait_send()

    for s in range(5):
        to_sibling(s).wait_send()
    for d in (1, 2, 3):
        to_owner(d).wait_send()


def unwindow(grads):
    rows, width = grads.shape[1] // 10, grads.shape[2]
    if meshed():
        dma = pltpu.SemaphoreType.DMA
        return pl.pallas_call(
            functools.partial(unwindow_kernel, rows),
            out_shape=jax.ShapeDtypeStruct((2, rows, width), F32),
            in_specs=[pl.BlockSpec(memory_space=pl.ANY)],
            out_specs=pl.BlockSpec(memory_space=pltpu.VMEM),
            scratch_shapes=[
                pltpu.VMEM((5, 2, rows, width), BF16),
                pltpu.VMEM((5, 2, rows, width), BF16),
                pltpu.VMEM((3, 2, rows, width), BF16),
                pltpu.VMEM((2, rows, width), BF16),
                dma((5,)), dma((9,)), dma((9,)),
            ],
            compiler_params=pltpu.CompilerParams(collective_id=12, has_side_effects=True, vmem_limit_bytes=40 * 2**20),
            name="unwindow",
        )(grads)
    devices = lax.axis_size("dev")
    back = (MAXDOC + rows - 2) // rows
    total = grads[:, back * rows : (back + 1) * rows].astype(F32)
    for d in range(1, back + 1):
        piece = grads[:, (back - d) * rows : (back - d + 1) * rows]
        moved = lax.ppermute(piece, "dev", [(i, i - d) for i in range(d, devices)])
        total = total + moved.astype(F32)
    return total


def make_bias(bias, lo_ref, chunks, rows):
    def fill(ch, _):
        at = pl.ds(pl.multiple_of(ch * rows, rows), rows)
        relative = lax.broadcasted_iota(jnp.int32, (rows, rows), 0) + (ch - (chunks - 1)) * rows
        query = lax.broadcasted_iota(jnp.int32, (rows, rows), 1)
        allowed = (relative <= query) & (relative >= lo_ref[...])
        bias[at, :] = jnp.where(allowed, 0.0, MASKED)
        return 0
    lax.fori_loop(0, chunks, fill, 0)


def attend_kernel(chunks, rows, off_ref, lo_ref, q_ref, kv_ref, o_ref, lse_ref, bias):
    @pl.when(pl.program_id(0) == 0)
    def _():
        make_bias(bias, lo_ref, chunks, rows)

    off = off_ref[0]
    lse_ref[...] = jnp.zeros_like(lse_ref)
    for half in range(2):
        lanes = slice(half * HEAD_DIM, (half + 1) * HEAD_DIM)
        queries = [q_ref[(half * GROUP + g) * HEAD_DIM : (half * GROUP + g + 1) * HEAD_DIM, :] for g in range(GROUP)]

        def chunk(i, carry, lanes=lanes, queries=queries):
            ch = chunks - 1 - i
            at = pl.ds(pl.multiple_of((ch + off) * rows, rows), rows)
            key, value = kv_ref[0, at, lanes], kv_ref[1, at, lanes]
            shift = bias[pl.ds(pl.multiple_of(ch * rows, rows), rows), :]
            out = []
            for g in range(GROUP):
                top, total, mixed = carry[g]
                score = dims(key, queries[g], 1, 0) + shift
                new_top = jnp.maximum(top, jnp.max(score, axis=0, keepdims=True))
                weight = jnp.exp(score - new_top)
                fade = jnp.exp(top - new_top)
                total = total * fade + jnp.sum(weight, axis=0, keepdims=True)
                mixed = mixed * fade + dims(value, weight.astype(BF16), 0, 0)
                out.append((new_top, total, mixed))
            return tuple(out)

        start = tuple(
            (jnp.full((1, rows), MASKED, F32), jnp.zeros((1, rows), F32), jnp.zeros((HEAD_DIM, rows), F32))
            for _ in range(GROUP)
        )
        done = lax.fori_loop(0, chunks, chunk, start)
        for g in range(GROUP):
            top, total, mixed = done[g]
            n = half * GROUP + g
            o_ref[n * HEAD_DIM : (n + 1) * HEAD_DIM, :] = (mixed / total).astype(BF16)
            lse_ref[0, n : n + 1, :] = top + jnp.log(total)


def attend_back_kernel(
    chunks, rows, off_ref, lo_ref, cos_ref, sin_ref, q_ref, kv_ref, g_ref, lse_ref, delta_ref, dq_ref, dkv_ref, bias
):
    @pl.when(pl.program_id(0) == 0)
    def _():
        make_bias(bias, lo_ref, chunks, rows)

    off = off_ref[0]
    unused = pl.ds(pl.multiple_of((1 - off) * chunks * rows, rows), rows)
    dkv_ref[:, unused, :] = jnp.zeros((2, rows, 2 * HEAD_DIM), BF16)
    cosine, sine = cos_ref[...], sin_ref[...]
    for half in range(2):
        lanes = slice(half * HEAD_DIM, (half + 1) * HEAD_DIM)
        own = [slice((half * GROUP + g) * HEAD_DIM, (half * GROUP + g + 1) * HEAD_DIM) for g in range(GROUP)]
        queries = [q_ref[s, :] for s in own]
        grads = [g_ref[s, :] for s in own]
        lses = [lse_ref[0, half * GROUP + g : half * GROUP + g + 1, :] for g in range(GROUP)]
        deltas = [delta_ref[0, half * GROUP + g : half * GROUP + g + 1, :] for g in range(GROUP)]

        def chunk(ch, carry, lanes=lanes, queries=queries, grads=grads, lses=lses, deltas=deltas):
            at = pl.ds(pl.multiple_of((ch + off) * rows, rows), rows)
            key, value = kv_ref[0, at, lanes], kv_ref[1, at, lanes]
            shift = bias[pl.ds(pl.multiple_of(ch * rows, rows), rows), :]
            dk = jnp.zeros((rows, HEAD_DIM), F32)
            dv = jnp.zeros((rows, HEAD_DIM), F32)
            out = []
            for g in range(GROUP):
                weight = jnp.exp(dims(key, queries[g], 1, 0) + shift - lses[g])
                back = dims(value, grads[g], 1, 0)
                score_grad = (weight * (back - deltas[g])).astype(BF16)
                dv = dv + dims(weight.astype(BF16), grads[g], 1, 1)
                dk = dk + dims(score_grad, queries[g], 1, 1)
                out.append(carry[g] + dims(key, score_grad, 0, 0))
            dkv_ref[0, at, lanes] = dk.astype(BF16)
            dkv_ref[1, at, lanes] = dv.astype(BF16)
            return tuple(out)

        done = lax.fori_loop(0, chunks, chunk, tuple(jnp.zeros((HEAD_DIM, rows), F32) for _ in range(GROUP)))
        for g in range(GROUP):
            grad = done[g] * (HEAD_DIM**-0.5)
            u, w = grad[: HEAD_DIM // 2], grad[HEAD_DIM // 2 :]
            n = (half * GROUP + g) * HEAD_DIM
            dq_ref[n : n + HEAD_DIM // 2, :] = (u * cosine + w * sine).astype(BF16)
            dq_ref[n + HEAD_DIM // 2 : n + HEAD_DIM, :] = (w * cosine - u * sine).astype(BF16)


def attention_specs(rows, span):
    width = 2 * GROUP * HEAD_DIM
    return dict(
        smem=pl.BlockSpec(memory_space=pltpu.SMEM),
        row=pl.BlockSpec((1, rows), lambda j: (0, 0)),
        table=pl.BlockSpec((HEAD_DIM // 2, rows), lambda j: (0, 0)),
        query=pl.BlockSpec((width, rows), lambda j: (j, 0)),
        kv=pl.BlockSpec((2, span, 2 * HEAD_DIM), lambda j: (0, 0, j)),
        stat=pl.BlockSpec((1, 8, rows), lambda j: (j, 0, 0)),
    )


def attend(query_t, window, offset, lo):
    rows, span = query_t.shape[1], window.shape[1]
    chunks = span // rows - 1
    s = attention_specs(rows, span)
    return pl.pallas_call(
        functools.partial(attend_kernel, chunks, rows),
        grid=(KEY_HEADS // 2,),
        in_specs=[s["smem"], s["row"], s["query"], s["kv"]],
        out_specs=[s["query"], s["stat"]],
        out_shape=[
            jax.ShapeDtypeStruct(query_t.shape, BF16),
            jax.ShapeDtypeStruct((KEY_HEADS // 2, 8, rows), F32),
        ],
        scratch_shapes=[pltpu.VMEM((chunks * rows, rows), F32)],
        compiler_params=pltpu.CompilerParams(vmem_limit_bytes=40 * 2**20),
        cost_estimate=pl.CostEstimate(flops=7 * 10**9, bytes_accessed=8 * 10**6, transcendentals=15 * 10**6),
        name="attend",
    )(offset.reshape(1), lo, query_t, window)


def attend_back(query_t, window, offset, lo, grad_t, lse, delta, cos_t, sin_t):
    rows, span = query_t.shape[1], window.shape[1]
    chunks = span // rows - 1
    s = attention_specs(rows, span)
    return pl.pallas_call(
        functools.partial(attend_back_kernel, chunks, rows),
        grid=(KEY_HEADS // 2,),
        in_specs=[s["smem"], s["row"], s["table"], s["table"], s["query"], s["kv"], s["query"], s["stat"], s["stat"]],
        out_specs=[s["query"], s["kv"]],
        out_shape=[
            jax.ShapeDtypeStruct(query_t.shape, BF16),
            jax.ShapeDtypeStruct(window.shape, BF16),
        ],
        scratch_shapes=[pltpu.VMEM((chunks * rows, rows), F32)],
        compiler_params=pltpu.CompilerParams(vmem_limit_bytes=40 * 2**20),
        cost_estimate=pl.CostEstimate(flops=18 * 10**9, bytes_accessed=16 * 10**6, transcendentals=15 * 10**6),
        name="attend_back",
    )(offset.reshape(1), lo, cos_t, sin_t, query_t, window, grad_t, lse, delta)


def swap_kernel(x_ref, o_ref, lsem, ss, rs):
    me = lax.axis_index("dev")
    n = x_ref.shape[0]
    greet([lax.rem(me + d, n) for d in range(1, n)])

    def copy(d):
        target = lax.rem(me + d, n)
        return pltpu.make_async_remote_copy(
            src_ref=x_ref.at[target], dst_ref=o_ref.at[me], send_sem=ss.at[d], recv_sem=rs.at[d],
            device_id=(target,), device_id_type=MESH)

    own = pltpu.make_async_copy(x_ref.at[me], o_ref.at[me], lsem)
    own.start()

    def start(d, _):
        copy(d).start()
        return 0
    lax.fori_loop(1, n, start, 0)

    def end(d, _):
        copy(d).wait_recv()
        copy(d).wait_send()
        return 0
    lax.fori_loop(1, n, end, 0)
    own.wait()


def swap(values, cid):
    if not meshed():
        return lax.all_to_all(values, "dev", split_axis=0, concat_axis=0, tiled=True)
    n = values.shape[0]
    dma = pltpu.SemaphoreType.DMA
    return pl.pallas_call(
        swap_kernel,
        out_shape=jax.ShapeDtypeStruct(values.shape, values.dtype),
        in_specs=[pl.BlockSpec(memory_space=pltpu.VMEM)],
        out_specs=pl.BlockSpec(memory_space=pltpu.VMEM),
        scratch_shapes=[dma, dma((n,)), dma((n,))],
        compiler_params=pltpu.CompilerParams(collective_id=cid, has_side_effects=True),
        name="swap",
    )(values)


def swap_rows(values, cid):
    n, width = values.shape
    padded = jnp.pad(values.reshape(n, width // 128, 128), ((0, 0), (0, 8 - width // 128), (0, 0)))
    return swap(padded, cid)[:, : width // 128].reshape(n, width)


def hits(slot_ref, slots):
    width = slot_ref.shape[-1]
    return slot_ref[0] == lax.broadcasted_iota(jnp.int32, (slots, width), 0)


def dispatch_kernel(slot_ref, x_ref, u_ref, xo_ref, uo_ref):
    chosen = jnp.where(hits(slot_ref, xo_ref.shape[0]), 1.0, 0.0).astype(BF16)
    xo_ref[...] = dims(chosen, x_ref[...], 1, 0).astype(BF16)
    uo_ref[...] = dims(chosen, u_ref[...], 1, 0).astype(BF16)


def dispatch(slot, normed, upstream, slots):
    pairs, _, width = slot.shape
    model = normed.shape[1]
    return pl.pallas_call(
        dispatch_kernel,
        grid=(pairs,),
        in_specs=[
            pl.BlockSpec((1, 1, width), lambda i: (i, 0, 0)),
            pl.BlockSpec((width, model), lambda i: (i, 0)),
            pl.BlockSpec((width, model), lambda i: (i, 0)),
        ],
        out_specs=[pl.BlockSpec((slots, model), lambda i: (i, 0))] * 2,
        out_shape=[jax.ShapeDtypeStruct((pairs * slots, model), BF16)] * 2,
        compiler_params=pltpu.CompilerParams(vmem_limit_bytes=40 * 2**20),
        cost_estimate=pl.CostEstimate(flops=2 * 10**9, bytes_accessed=65 * 10**6, transcendentals=0),
        name="dispatch",
    )(slot, normed, upstream)


def combine_kernel(slot_ref, r_ref, o_ref):
    chosen = jnp.where(hits(slot_ref, r_ref.shape[0]), 1.0, 0.0).astype(BF16)
    o_ref[...] = dims(chosen, r_ref[...], 0, 0).astype(BF16)


def combine(slot, rows, slots):
    pairs, _, width = slot.shape
    model = rows.shape[1]
    return pl.pallas_call(
        combine_kernel,
        grid=(pairs,),
        in_specs=[
            pl.BlockSpec((1, 1, width), lambda i: (i, 0, 0)),
            pl.BlockSpec((slots, model), lambda i: (i, 0)),
        ],
        out_specs=pl.BlockSpec((width, model), lambda i: (i, 0)),
        out_shape=jax.ShapeDtypeStruct((pairs * width, model), BF16),
        compiler_params=pltpu.CompilerParams(vmem_limit_bytes=40 * 2**20),
        cost_estimate=pl.CostEstimate(flops=10**9, bytes_accessed=33 * 10**6, transcendentals=0),
        name="combine",
    )(slot, rows)


def rms_scale(values):
    return lax.rsqrt(jnp.mean(values * values, axis=-1, keepdims=True) + EPSILON)


def rotate_t(values, cosine, sine):
    half = cosine.shape[0]
    shaped = values.reshape(-1, 2, half, values.shape[1])
    u, w = shaped[:, 0], shaped[:, 1]
    turned = jnp.stack([u * cosine - w * sine, w * cosine + u * sine], axis=1)
    return turned.reshape(values.shape)


def gathered(block, cid, by_rows):
    if meshed():
        return gather_all(block, cid, by_rows)
    return lax.all_gather(block, "dev", axis=0, tiled=True)


def reduced(dense, cid, by_rows):
    if meshed():
        return reduce_all(dense, cid, by_rows)
    return lax.psum_scatter(dense, "dev", scatter_dimension=0, tiled=True).astype(F32)


def on_device(
    tokens,
    positions,
    expert_picks,
    priority,
    first_gain,
    query_weight,
    key_projection_matrix,
    value_projection_matrix,
    output_weight,
    second_gain,
    router_weight,
    gate_weight,
    up_weight,
    down_weight,
    cotangent,
):
    devices = lax.axis_size("dev")
    rows, model = tokens.shape
    split = devices // EXPERTS
    capacity = split * ((9 * rows * TOP + 8 * EXPERTS * split - 1) // (8 * EXPERTS * split))
    my_expert = lax.axis_index("dev") // split
    weight_rows = query_weight.shape[0]

    all_upstream = lax.all_gather(cotangent, "dev", axis=0, tiled=True)
    output_matrix = lax.all_gather(output_weight, "dev", axis=0, tiled=True)
    all_claims = lax.all_gather(jnp.concatenate([expert_picks, priority], axis=1), "dev", axis=0, tiled=True)

    extra = jnp.concatenate([router_weight, first_gain[:, None], second_gain[:, None]], axis=1)
    pad = (-extra.shape[1]) % 128
    packed = jnp.concatenate(
        [query_weight, key_projection_matrix, value_projection_matrix, extra, jnp.zeros((weight_rows, pad), BF16)],
        axis=1,
    )
    matrices = gathered(packed, 1, False)
    qkv_matrix = matrices[:, :QKV]
    router_matrix = matrices[:, QKV : QKV + EXPERTS]
    gain_first = matrices[:, QKV + EXPERTS].astype(F32)
    gain_second = matrices[:, QKV + EXPERTS + 1].astype(F32)

    claims = all_claims.reshape(devices, rows, 2 * TOP)
    mine = claims[:, :, :TOP] == my_expert
    picked_mine = jnp.any(mine, axis=2)
    turn = jnp.sum(jnp.where(mine, claims[:, :, TOP:], 0), axis=2)
    turn = jnp.where(picked_mine, turn, jnp.int32(2**30))
    rank = jnp.sum((turn[:, None, :] < turn[:, :, None]).astype(jnp.int32), axis=2)
    kept = picked_mine & (rank < capacity)
    slot = jnp.where(kept, rank, -1)
    pair_slot = jnp.where(
        slot.reshape(devices // 2, 2, rows) >= 0,
        slot.reshape(devices // 2, 2, rows) + jnp.array([[0], [capacity]], jnp.int32),
        -1,
    ).reshape(devices // 2, 1, 2 * rows)

    inputs = tokens.astype(F32)
    scale_one = rms_scale(inputs)
    normed_one = (inputs * scale_one * gain_first).astype(BF16)
    half_dim = HEAD_DIM // 2
    frequency = jnp.power(10000.0, -(jnp.arange(half_dim, dtype=F32) * 2.0) / HEAD_DIM)
    angle = positions.astype(F32)[None, :] * frequency[:, None]
    cos_t, sin_t = jnp.cos(angle), jnp.sin(angle)
    qkv_t = dims(qkv_matrix, normed_one, 0, 1)
    q_width, k_width = QUERY_HEADS * HEAD_DIM, KEY_HEADS * HEAD_DIM
    query_t = rotate_t(qkv_t[:q_width], cos_t, sin_t).astype(BF16) * BF16(HEAD_DIM**-0.5)
    key = rotate_t(qkv_t[q_width : q_width + k_width], cos_t, sin_t).astype(BF16).T
    value = qkv_t[q_width + k_width :].astype(BF16).T
    window, offset = window_of(jnp.stack([key, value]))
    lo = (jnp.arange(rows, dtype=jnp.int32) - positions)[None, :]
    attended_t, lse = attend(query_t, window, offset, lo)
    residual = inputs + dims(attended_t, output_matrix, 0, 0)
    scale_two = rms_scale(residual)
    normed_two = (residual * scale_two * gain_second).astype(BF16)

    logits = dims(normed_two, router_matrix, 1, 0)
    one_hot = expert_picks[:, :, None] == jnp.arange(EXPERTS, dtype=jnp.int32)
    picked_any = jnp.any(one_hot, axis=1)
    logits = jnp.where(picked_any, logits, MASKED)
    picked_exp = jnp.exp(logits - jnp.max(logits, axis=1, keepdims=True))
    gates = picked_exp / jnp.sum(picked_exp, axis=1, keepdims=True)
    gate_rows = swap_rows(jnp.repeat(gates.T, split, axis=0), 5)

    all_normed = gathered(normed_two, 2, True)
    expert_in, expert_up = dispatch(pair_slot, all_normed, all_upstream, 2 * capacity)
    slot_hit = slot[:, None, :] == jnp.arange(capacity, dtype=jnp.int32)[None, :, None]
    gate_of_slot = jnp.sum(jnp.where(slot_hit, gate_rows[:, None, :], 0.0), axis=2).reshape(-1, 1)
    gate_in = dims(expert_in, gate_weight, 1, 0)
    up_in = dims(expert_in, up_weight, 1, 0)
    sigmoid_gate = 1.0 / (1.0 + jnp.exp(-gate_in))
    silu_gate = gate_in * sigmoid_gate
    hidden = (silu_gate * up_in).astype(BF16)
    gated_hidden = (hidden.astype(F32) * gate_of_slot).astype(BF16)
    hidden_up = dims(expert_up, down_weight, 1, 1)
    hidden_grad = hidden_up * gate_of_slot
    gate_grad_slot = jnp.sum(hidden.astype(F32) * hidden_up, axis=1).reshape(devices, capacity)
    gate_in_grad = (hidden_grad * up_in * sigmoid_gate * (1.0 + gate_in * (1.0 - sigmoid_gate))).astype(BF16)
    up_in_grad = (hidden_grad * silu_gate).astype(BF16)
    partial_in = (dims(gate_in_grad, gate_weight, 1, 1) + dims(up_in_grad, up_weight, 1, 1)).astype(BF16)
    gate_grad_rows = jnp.sum(jnp.where(slot_hit, gate_grad_slot[:, :, None], 0.0), axis=1)
    returned_grad = reduced(combine(pair_slot, partial_in, 2 * capacity), 3, True)
    gate_grad = swap_rows(gate_grad_rows, 6)
    gate_grad = jnp.sum(gate_grad.reshape(EXPERTS, split, rows), axis=1).T

    partial_out = dims(gated_hidden, down_weight, 1, 0).astype(BF16)
    dense_out = combine(pair_slot, partial_out, 2 * capacity)
    mixture = lax.psum_scatter(dense_out, "dev", scatter_dimension=0, tiled=True)
    layer_output = (residual + mixture.astype(F32)).astype(BF16)
    down_gradient = dims(gated_hidden, expert_up, 0, 0)
    gate_gradient = dims(expert_in, gate_in_grad, 0, 0)
    up_gradient = dims(expert_in, up_in_grad, 0, 0)

    upstream = cotangent.astype(F32)
    logit_grad = (gates * (gate_grad - jnp.sum(gates * gate_grad, axis=1, keepdims=True))).astype(BF16)
    router_gradient = dims(normed_two, logit_grad, 0, 0)
    normed_two_grad = returned_grad + dims(logit_grad, router_matrix, 1, 1)
    weighted_two = normed_two_grad * gain_second
    second_gain_grad = jnp.sum(normed_two_grad * residual * scale_two, axis=0)
    residual_grad = (
        upstream
        + scale_two * weighted_two
        - residual * scale_two**3 * jnp.mean(weighted_two * residual, axis=-1, keepdims=True)
    )
    branch_grad = residual_grad.astype(BF16)
    output_gradient = dims(attended_t, branch_grad, 1, 0).astype(BF16)
    output_gradient = lax.psum_scatter(output_gradient, "dev", scatter_dimension=0, tiled=True).astype(F32)
    grad_t = dims(output_matrix, branch_grad, 1, 1).astype(BF16)

    delta = jnp.sum((attended_t.astype(F32) * grad_t.astype(F32)).reshape(QUERY_HEADS, HEAD_DIM, rows), axis=1)
    delta = jnp.pad(delta.reshape(KEY_HEADS // 2, 2 * GROUP, rows), ((0, 0), (0, 8 - 2 * GROUP), (0, 0)))
    query_grad_t, window_grad = attend_back(query_t, window, offset, lo, grad_t, lse, delta, cos_t, sin_t)
    key_grad, value_grad = unwindow(window_grad)
    key_grad_t = rotate_t(key_grad.T, cos_t, -sin_t).astype(BF16)
    qkv_grad_t = jnp.concatenate([query_grad_t, key_grad_t, value_grad.T.astype(BF16)], axis=0)
    qkv_gradient = dims(normed_one, qkv_grad_t, 0, 1)
    normed_one_grad = dims(qkv_grad_t, qkv_matrix, 0, 1)
    weighted_one = normed_one_grad * gain_first
    first_gain_grad = jnp.sum(normed_one_grad * inputs * scale_one, axis=0)
    tokens_gradient = (
        residual_grad
        + scale_one * weighted_one
        - inputs * scale_one**3 * jnp.mean(weighted_one * inputs, axis=-1, keepdims=True)
    )
    terms = jnp.concatenate(
        [qkv_gradient, router_gradient, first_gain_grad[:, None], second_gain_grad[:, None],
         jnp.zeros((model, (-(QKV + EXPERTS + 2)) % 256), F32)],
        axis=1,
    ).astype(BF16)
    sums = reduced(terms, 4, False)
    return (
        layer_output,
        tokens_gradient,
        sums[:, QKV + EXPERTS],
        sums[:, :q_width],
        sums[:, q_width : q_width + k_width],
        sums[:, q_width + k_width : QKV],
        output_gradient,
        sums[:, QKV + EXPERTS + 1],
        sums[:, QKV : QKV + EXPERTS],
        gate_gradient,
        up_gradient,
        down_gradient,
    )


def solution(mesh):
    rows, whole = P("dev", None), P("dev")
    columns = P(None, "dev")
    return jax.shard_map(
        on_device,
        mesh=mesh,
        in_specs=(rows, whole, rows, rows, whole, rows, rows, rows, rows, whole, rows, columns, columns, rows, rows),
        out_specs=(rows, rows, whole, rows, rows, rows, rows, whole, rows, columns, columns, rows),
        check_vma=False,
    )
```

time: 2460 us -> 1020 us (0.41)
  waiting for transfers between devices: 861 us -> 6.11 us
  Pallas kernels: 0 us -> 771 us
  blocking collectives: 730 us -> 40.4 us
  other arithmetic: 236 us -> 28.5 us
  matrix products: 305 us -> 105 us
  local copies, waits for them, and re-layouts: 205 us -> 44.7 us
  starting transfers between devices: 96.2 us -> 0.16 us
    pallas_call x0 -> x13, Pallas kernels: none -> 771 us  [the longest x2 276 us: reduce_all(): pl.pallas_call(functools.partial(reduce_kernel, rows, cols, pieces), out_...]
    all_to_all x2 -> x0, blocking collectives: 370 us -> none  [to_experts(): lax.all_to_all(copied, 'dev', split_axis=0, concat_axis=0, tiled=True)]
    all_to_all x2 -> x0, waiting for transfers between devices: 331 us -> none  [from_experts(): lax.all_to_all(partial_rows.reshape(devices, capacity, model_width), 'dev...]
    reduce_scatter x3 -> x1, waiting for transfers between devices: 279 us -> 4.68 us  [on_device(): lax.psum_scatter(dense_out, 'dev', scatter_dimension=0, tiled=True)]
    all_gather x1, blocking collectives: 277 us -> 40.4 us  [on_device(): lax.all_gather(jnp.concatenate([expert_picks, priority], axis=1), 'dev',...]
    dot_general x79 -> x18, matrix products: 304 us -> 105 us  [dims(): lax.dot_general(a, b, (((ca,), (cb,)), ((), ())), preferred_element_type=...]
    reduce_scatter x1, waiting for transfers between devices: 141 us -> 0.01 us  [on_device(): lax.psum_scatter(output_gradient, 'dev', scatter_dimension=0, tiled=True)]
    sub x11 -> x0, other arithmetic: 119 us -> none  [the longest x8 118 us: attend_back(): probability_grad - row_delta]
  transfers between devices with their start and end apart: 43 -> 4, of which waited for: 18 -> 1; matrix products, arithmetic and copies ran while one was open for 11% -> 13% of each run, Pallas kernels for 0% -> 73%
where the time goes in v1:
time: 1020 us; the launch traced here: 1010 us
  Pallas kernels  771 us (76%)
  matrix products  105 us (10%)
  local copies, waits for them, and re-layouts  44.7 us (4%)
  blocking collectives  40.4 us (4%)
  other arithmetic  28.5 us (3%)
  between operations  14.8 us (1%)
    pallas_call x2, Pallas kernels, reduce_all(): pl.pallas_call(functools.partial(reduce_kernel, rows, cols, pieces), out_...  276 us
    pallas_call x2, Pallas kernels, gather_all(): pl.pallas_call(functools.partial(gather_kernel, rows, pieces), out_shape=...  174 us
    dot_general x18, matrix products, dims(): lax.dot_general(a, b, (((ca,), (cb,)), ((), ())), preferred_element_type=...  105 us
    pallas_call x1, Pallas kernels, attend(): pl.pallas_call(functools.partial(attend_kernel, chunks, rows), grid=(KEY_...  70.1 us
    pallas_call x1, Pallas kernels, attend_back(): pl.pallas_call(functools.partial(attend_back_kernel, chunks, rows), grid=...  69.1 us
    pallas_call x1, Pallas kernels, window_of(): pl.pallas_call(functools.partial(window_kernel, rows), out_shape=jax.Shap...  65.2 us
    pallas_call x1, Pallas kernels, unwindow(): pl.pallas_call(functools.partial(unwindow_kernel, rows), out_shape=jax.Sh...  44 us
    all_gather x1, blocking collectives, on_device(): lax.all_gather(jnp.concatenate([expert_picks, priority], axis=1), 'dev',...  40.4 us
  transfers between devices with their start and end apart: 4, of which 1 were waited for; matrix products, arithmetic and copies ran while one was open for 13% of the time, Pallas kernels for 73%

profile of v1, /device:TPU:0, one launch (start us, length us, event | category | flops | bytes accessed | tf_op | source)
XLA Modules:
  0.0 1010.0 jit_solution(18066790444117434191)
XLA Ops:
  8.7 0.8 copy.70
  11.0 1.7 concatenate.13.x_ref
  12.8 54.7 %gather_all.2 = bf16[1536,2688]{1,0:T(8,128)(2,1)} custom-call(bf16[48,2688]{1,0:T(8,128)(2,1)} %concatenate.13.x_ref), custom_call_target="tpu_custom_call" | custom-call | tf_op jit(solution)/shard_map/gather_all/pallas_call | solution.py:111
  67.5 1.9 convert_reduce_fusion.1
  70.3 5.6 fusion.2
  75.9 1.2 slice.93
  77.4 0.8 fusion.35
  78.5 0.8 pad_maximum_fusion.3.kv_ref
  79.3 65.2 %window.1.kv_ref = bf16[2,2560,512]{2,1,0:T(8,128)(2,1)} custom-call(bf16[2,256,512]{2,1,0:T(8,128)(2,1)} %pad_maximum_fusion.3.kv_ref), custom_call_target="tpu_custom_call" | custom-call | tf_op jit(solution)/shard_map/window/pallas_call | solution.py:362
  144.6 40.4 %all_gather.10 = s32[8192,16]{0,1:T(8,128)S(1)} all-gather(s32[256,16]{0,1:T(8,128)S(1)} %pad_add_fusion), channel_id=1, replica_groups=mesh['dev'=32] {'dev'}, dimensions={0}, use_global_device_ids=true | all-gather | bytes 540672 | tf_op jit(solution)/shard_map/all_gather | solution.py:806
  185.3 2.8 convert_reduce_fusion
  188.2 1.6 subtract_convert_fusion
  190.1 2.6 copy-done.2
  192.6 70.1 %attend.1 = (bf16[1536,256]{1,0:T(8,128)(2,1)S(1)}, f32[4,8,256]{2,1,0:T(8,128)S(1)}) custom-call(s32[1]{0:T(128)} %bitcast.off_ref, s32[1,256]{1,0:T(1,128)S(1)} %bitcast.93, bf16[1536,256]{1,0:T(8,128)(2,1)S(1)} %bitcast.91, bf16[2,2560,512]{2,1,0:T(8,128)(2,1)S(1)} %copy-done.2), custom_call_target="tpu_custom_call" | custom-call | flops 7000000000 | bytes 8000000 | tf_op jit(solution)/shard_map/attend/pallas_call | solution.py:618
  262.8 0.9 copy-done.4
  263.7 3.8 multiply_reduce_fusion.2
  267.5 1.1 copy-done.13
  268.6 1.1 multiply_convert_fusion.3.x_ref
  269.7 119.1 %gather_all.3.x_ref = bf16[8192,1536]{1,0:T(8,128)(2,1)} custom-call(bf16[256,1536]{1,0:T(8,128)(2,1)} %multiply_convert_fusion.3.x_ref), custom_call_target="tpu_custom_call" | custom-call | tf_op jit(solution)/shard_map/gather_all/pallas_call | solution.py:111
  388.8 1.4 fusion.41
  390.9 9.8 swap.2
  400.7 0.9 slice.83
  401.7 22.5 %dispatch.1 = (bf16[2304,1536]{1,0:T(8,128)(2,1)S(1)}, bf16[2304,1536]{1,0:T(8,128)(2,1)S(1)}) custom-call(s32[16,1,512]{2,1,0:T(1,128)S(1)} %compare_select_fusion.slot_ref, bf16[8192,1536]{1,0:T(8,128)(2,1)} %gather_all.3.x_ref, bf16[8192,1536]{1,0:T(8,128)(2,1)} %all-gather.5.cloned.1.call-done.u_ref), custom_call_target="tpu_custom_call" | custom-call | flops 2000000000 | bytes 65000000 | tf_op jit(solution)/shard_map/dispatch/pallas_call | solution.py:717
  424.2 7.0 fusion.43
  431.2 5.9 fusion.42
  437.1 8.4 fusion.5
  445.6 1.5 select_reduce_fusion
  447.2 5.8 convolution_convert_fusion.1.r_ref
  453.0 15.0 %combine.2 = bf16[8192,1536]{1,0:T(8,128)(2,1)} custom-call(s32[16,1,512]{2,1,0:T(1,128)S(1)} %compare_select_fusion.slot_ref, bf16[2304,1536]{1,0:T(8,128)(2,1)S(1)} %convolution_convert_fusion.1.r_ref), custom_call_target="tpu_custom_call" | custom-call | flops 1000000000 | bytes 33000000 | tf_op jit(solution)/shard_map/combine/pallas_call | solution.py:741
  468.1 6.9 multiply_convert_fusion
  475.0 7.9 fusion.44
  483.0 9.3 add_convert_fusion.r_ref
  492.2 15.0 %combine.3.g_ref = bf16[8192,1536]{1,0:T(8,128)(2,1)} custom-call(s32[16,1,512]{2,1,0:T(1,128)S(1)} %compare_select_fusion.slot_ref, bf16[2304,1536]{1,0:T(8,128)(2,1)S(1)} %add_convert_fusion.r_ref), custom_call_target="tpu_custom_call" | custom-call | flops 1000000000 | bytes 33000000 | tf_op jit(solution)/shard_map/combine/pallas_call | solution.py:741
  507.3 218.7 %reduce_all.2 = f32[256,1536]{1,0:T(8,128)} custom-call(bf16[8192,1536]{1,0:T(8,128)(2,1)} %combine.3.g_ref), custom_call_target="tpu_custom_call" | custom-call | tf_op jit(solution)/shard_map/reduce_all/pallas_call | solution.py:238
  726.7 10.2 %swap.3 = f32[32,8,128]{2,1,0:T(8,128)} custom-call(f32[32,8,128]{2,1,0:T(8,128)} %pad.12.x_ref), custom_call_target="tpu_custom_call" | custom-call | tf_op jit(solution)/shard_map/swap/pallas_call | solution.py:686
  736.8 0.9 slice.84
  738.0 1.0 copy.79
  739.0 3.4 multiply_reduce_fusion
  742.5 1.1 broadcast_in_dim.119
  743.5 9.4 fusion.45
  753.0 5.5 fusion.8
  758.4 4.7 reduce-scatter.3.cloned.1.call-done
  763.1 3.1 multiply_subtract_fusion
  766.2 1.1 copy-done.15
  767.3 3.6 convolution_convert_fusion.2
  770.9 9.6 fusion.46
  780.5 5.4 convert_multiply_fusion.7
  786.0 1.6 reduce_sum.146
  787.6 2.6 copy-done.3
  790.2 1.1 copy-done.12
  791.4 69.1 %attend_back.1 = (bf16[1536,256]{1,0:T(8,128)(2,1)S(1)}, bf16[2,2560,512]{2,1,0:T(8,128)(2,1)S(1)}) custom-call(s32[1]{0:T(128)} %bitcast.off_ref, s32[1,256]{1,0:T(1,128)S(1)} %bitcast.94, f32[32,256]{1,0:T(8,128)S(1)} %copy-done.7, f32[32,256]{1,0:T(8,128)S(1)} %copy-done.9, bf16[1536,256]{1,0:T(8,128)(2,1)S(1)} %bitcast.92, ...), custom_call_target="tpu_custom_call" | custom-call | flops 17999998976 | bytes 16000000 | tf_op jit(solution)/shard_map/attend_back/pallas_call | solution.py:638
  860.5 44.0 %unwindow.1 = f32[2,256,512]{2,1,0:T(8,128)S(1)} custom-call(bf16[2,2560,512]{2,1,0:T(8,128)(2,1)S(1)} %get-tuple-element.23.g_ref), custom_call_target="tpu_custom_call" | custom-call | tf_op jit(solution)/shard_map/unwindow/pallas_call | solution.py:480
  904.6 0.8 copy.78
  905.4 0.9 slice_bitcast_fusion
  906.3 1.3 copy.77
  907.7 6.8 fusion.18
  914.8 5.5 convolution_convert_fusion
  920.4 14.2 %concatenate.16.g_ref = bf16[1536,2816]{1,0:T(8,128)(2,1)} concatenate(bf16[1536,2560]{1,0:T(8,128)(2,1)} %convolution_convert_fusion, bf16[1536,32]{1,0:T(8,128)(2,1)S(1)} %copy-done.26, bf16[1536,1]{1,0:T(8,128)(2,1)S(1)} %broadcast_in_dim.118, bf16[1536,1]{1,0:T(8,128)(2,1)S(1)} %copy-done.25, bf16[1536,222]{1,0:T(8,128)(2,1)S(1)} %broadcast_in_dim.117), dimensions={1} | concatenate | bytes 17301504 | tf_op jit(solution)/shard_map/concatenate | solution.py:921
  934.6 57.4 %reduce_all.3 = f32[48,2816]{1,0:T(8,128)} custom-call(bf16[1536,2816]{1,0:T(8,128)(2,1)} %concatenate.16.g_ref), custom_call_target="tpu_custom_call" | custom-call | tf_op jit(solution)/shard_map/reduce_all/pallas_call | solution.py:238
  992.0 1.7 slice.88
  995.1 1.5 slice_reduce_fusion
  996.6 1.6 fusion.39
  998.2 3.4 fusion.15
  1001.6 1.6 convert_element_type.143
  (141 shorter events, 9.0 us)
Async XLA Ops:
  7.2 430.0 %copy-start = (bf16[512,1536]{1,0:T(8,128)(2,1)S(1)}, bf16[512,1536]{1,0:T(8,128)(2,1)}, u32[]{:S(2)}) copy-start(bf16[512,1536]{1,0:T(8,128)(2,1)} %param.29) | copy-start | bytes 4718596
  7.2 256.5 %all-gather.3.cloned.1.call-start = ((), (), s32[]{:S(2)}) async-start(), calls=%async_computation.2 | async-start | bytes 4866048 | tf_op jit(solution)/shard_map/all_gather | solution.py:805
  7.9 393.8 %all-gather.5.cloned.1.call-start = ((), (), s32[]{:S(2)}) async-start(), calls=%async_computation.3 | async-start | bytes 25952256 | tf_op jit(solution)/shard_map/all_gather | solution.py:804
  8.7 754.4 %reduce-scatter.3.cloned.1.call-start = ((), (), s32[]{:S(2)}) async-start(), calls=%async_computation.4 | async-start | bytes 25952256 | tf_op jit(solution)/shard_map/reduce_scatter | solution.py:884
  12.8 56.6 %copy-start.18 = (bf16[256,1536]{1,0:T(8,128)(2,1)S(1)}, bf16[256,1536]{1,0:T(8,128)(2,1)}, u32[]{:S(2)}) copy-start(bf16[256,1536]{1,0:T(8,128)(2,1)} %param.16) | copy-start | bytes 2359300
  69.4 6.4 copy-start.28
  70.2 5.6 copy-start.32
  75.9 1.5 copy-start.36
  78.2 110.0 %copy-start.6 = (f32[32,256]{1,0:T(8,128)}, f32[32,256]{1,0:T(8,128)S(1)}, u32[]{:S(2)}) copy-start(f32[32,256]{1,0:T(8,128)S(1)} %get-tuple-element.100.cos_ref) | copy-start | bytes 98308
  78.2 110.0 %copy-start.8 = (f32[32,256]{1,0:T(8,128)}, f32[32,256]{1,0:T(8,128)S(1)}, u32[]{:S(2)}) copy-start(f32[32,256]{1,0:T(8,128)S(1)} %get-tuple-element.99.sin_ref) | copy-start | bytes 98308
  79.3 65.3 %copy-start.31 = (s32[256,8]{0,1:T(8,128)S(1)}, s32[256,8]{0,1:T(8,128)}, u32[]{:S(2)}) copy-start(s32[256,8]{0,1:T(8,128)} %param.18) | copy-start | bytes 24580
  79.3 65.3 %copy-start.34 = (s32[256,8]{0,1:T(8,128)S(1)}, s32[256,8]{0,1:T(8,128)}, u32[]{:S(2)}) copy-start(s32[256,8]{0,1:T(8,128)} %param.19) | copy-start | bytes 24580
  190.1 2.6 copy-start.2
  262.8 0.9 copy-start.4
  267.5 1.1 copy-start.13
  269.7 119.1 %copy-start.20 = (bf16[256,1536]{1,0:T(8,128)(2,1)S(1)}, bf16[256,1536]{1,0:T(8,128)(2,1)}, u32[]{:S(2)}) copy-start(bf16[256,1536]{1,0:T(8,128)(2,1)} %multiply_convert_fusion.3.x_ref) | copy-start | bytes 2359300
  424.2 7.1 copy-start.10
  424.2 13.0 %copy-start.11 = (bf16[2304,1536]{1,0:T(8,128)(2,1)}, bf16[2304,1536]{1,0:T(8,128)(2,1)S(1)}, u32[]{:S(2)}) copy-start(bf16[2304,1536]{1,0:T(8,128)(2,1)S(1)} %get-tuple-element.20) | copy-start | bytes 21233668
  424.2 7.0 copy-start.37
  431.2 5.9 copy-start.21
  468.0 533.6 %reduce-scatter.5.cloned.1.call-start = ((), (), s32[]{:S(2)}) async-start(), calls=%async_computation.5 | async-start | bytes 4866048 | tf_op jit(solution)/shard_map/reduce_scatter | solution.py:903
  468.1 6.9 copy-start.38
  475.0 7.9 copy-start.24
  475.0 8.0 copy-start.23
  726.0 13.1 %copy-start.14 = (f32[256,1536]{1,0:T(8,128)S(1)}, f32[256,1536]{1,0:T(8,128)}, u32[]{:S(2)}) copy-start(f32[256,1536]{1,0:T(8,128)} %copy-done.13) | copy-start | bytes 4718596
  739.0 13.9 %slice-start = ((s8[7077888]{0:T(1024)(128)(4,1)}), s8[4194304]{0:T(1024)(128)(4,1)S(1)}, s32[]{:S(2)}) async-start(s8[7077888]{0:T(1024)(128)(4,1)} %bitcast.95), calls=%async_computation.6 | async-start | bytes 8388608
  743.5 9.4 slice-start.1
  743.5 9.4 copy-start.39
  752.9 10.2 %copy-start.22 = (bf16[256,1536]{1,0:T(8,128)(2,1)S(1)}, bf16[256,1536]{1,0:T(8,128)(2,1)}, u32[]{:S(2)}) copy-start(bf16[256,1536]{1,0:T(8,128)(2,1)} %param.30) | copy-start | bytes 2359300
  766.2 1.1 copy-start.15
  770.9 9.6 copy-start.16
  780.5 7.1 copy-start.5
  780.5 7.1 copy-start.7
  780.5 7.1 copy-start.9
  787.6 2.6 copy-start.3
  790.2 1.1 copy-start.12
  904.5 3.1 copy-start.30
  904.5 3.2 copy-start.19
  904.5 3.2 copy-start.29
  904.5 3.2 copy-start.33
  906.3 1.4 copy-start.27
  914.8 5.6 copy-start.25
  914.8 5.6 copy-start.26
  934.6 63.6 %copy-start.17 = (f32[256,1536]{1,0:T(8,128)S(1)}, f32[256,1536]{1,0:T(8,128)}, u32[]{:S(2)}) copy-start(f32[256,1536]{1,0:T(8,128)} %copy-done.15) | copy-start | bytes 4718596
  934.6 63.6 %copy-start.35 = (f32[256]{0:T(256)S(1)}, f32[256]{0:T(256)}, u32[]{:S(2)}) copy-start(f32[256]{0:T(256)} %get-tuple-element.101) | copy-start | bytes 3076
  998.2 5.0 copy-start.1
Sparse Core Ops, SparseCore 0:
  10.9 78.1 all-gather.2
  92.0 168.4 all-gather.4
  468.2 294.9 reduce-scatter.2
  771.0 106.6 reduce-scatter.4

commit v2 on v1

--- a/solution.py
+++ b/solution.py
@@ -277,7 +277,7 @@
     return lax.dot_general(a, b, (((ca,), (cb,)), ((), ())), preferred_element_type=F32)
 
 
-def window_kernel(rows, kv_ref, o_ref, lsem, ss, rs):
+def window_kernel(rows, kv_ref, mine_ref, o_ref, slots_ref, lsem, ss, rs, gs, gr):
     z, y, x, c = place()
     p = y * 2 + x
     sibling = number(z, y, x, 1 - c)
@@ -288,7 +288,8 @@
         return (z * 4 + q) * 2 + c
 
     near = [chip(lax.rem(p + d, 4)) for d in (1, 2, 3)]
-    greet([sibling, up, down] + near)
+    greet_all()
+    swap = Swap(lambda t: mine_ref.at[t // 8], slots_ref, gs, gr)
 
     def slot(s, core):
         return o_ref.at[:, pl.ds(pl.multiple_of((2 * s + core) * rows, 16), rows), :]
@@ -319,6 +320,7 @@
 
     to_sibling = {4: copy(kv_ref, 4, 4, sibling)}
     to_sibling[4].start()
+    swap.start()
 
     @pl.when(z == 0)
     def _():
@@ -353,28 +355,33 @@
         copy(kv_ref, 4 - d, d, near[d - 1]).wait_send()
     for s in range(5):
         to_sibling[s].wait_send()
-
-
-def window_of(kv):
+    swap.wait_recv()
+    swap.wait_send()
+
+
+def window_of(kv, slots):
     rows, width = kv.shape[1:]
     if meshed():
         dma = pltpu.SemaphoreType.DMA
-        full = pl.pallas_call(
+        full, plane_slots = pl.pallas_call(
             functools.partial(window_kernel, rows),
-            out_shape=jax.ShapeDtypeStruct((2, 10 * rows, width), kv.dtype),
-            in_specs=[pl.BlockSpec(memory_space=pl.ANY)],
-            out_specs=pl.BlockSpec(memory_space=pl.ANY),
-            scratch_shapes=[dma((2,)), dma((9,)), dma((9,))],
+            out_shape=[
+                jax.ShapeDtypeStruct((2, 10 * rows, width), kv.dtype),
+                jax.ShapeDtypeStruct((32, 8, rows), F32),
+            ],
+            in_specs=[pl.BlockSpec(memory_space=pl.ANY), pl.BlockSpec(memory_space=pltpu.VMEM)],
+            out_specs=[pl.BlockSpec(memory_space=pl.ANY), pl.BlockSpec(memory_space=pltpu.VMEM)],
+            scratch_shapes=[dma((2,)), dma((9,)), dma((9,)), dma((32,)), dma((32,))],
             compiler_params=pltpu.CompilerParams(collective_id=11, has_side_effects=True),
             name="window",
-        )(kv)
-        return full, lax.rem(lax.axis_index("dev"), 2)
+        )(kv, slots)
+        return full, lax.rem(lax.axis_index("dev"), 2), plane_slots
     devices = lax.axis_size("dev")
     back = (MAXDOC + rows - 2) // rows
     parts = [
         lax.ppermute(kv, "dev", [(i - d, i) for i in range(d, devices)]) for d in range(back, 0, -1)
     ]
-    return jnp.concatenate(parts + [kv, jnp.zeros_like(kv)], axis=1), jnp.int32(0)
+    return jnp.concatenate(parts + [kv, jnp.zeros_like(kv)], axis=1), jnp.int32(0), None
 
 
 def unwindow_kernel(rows, g_ref, o_ref, mine, got, near_got, far, lsem, ss, rs):
@@ -553,17 +560,11 @@
             lse_ref[0, n : n + 1, :] = top + jnp.log(total)
 
 
-def attend_back_kernel(
-    chunks, rows, off_ref, lo_ref, cos_ref, sin_ref, q_ref, kv_ref, g_ref, lse_ref, delta_ref, dq_ref, dkv_ref, bias
+def attend_back_pair(
+    chunks, rows, off, cos_ref, sin_ref, q_ref, kv_ref, g_ref, lse_ref, delta_ref, dq_ref, dkv_ref, bias, between
 ):
-    @pl.when(pl.program_id(0) == 0)
-    def _():
-        make_bias(bias, lo_ref, chunks, rows)
-
-    off = off_ref[0]
     unused = pl.ds(pl.multiple_of((1 - off) * chunks * rows, rows), rows)
     dkv_ref[:, unused, :] = jnp.zeros((2, rows, 2 * HEAD_DIM), BF16)
-    cosine, sine = cos_ref[...], sin_ref[...]
     for half in range(2):
         lanes = slice(half * HEAD_DIM, (half + 1) * HEAD_DIM)
         own = [slice((half * GROUP + g) * HEAD_DIM, (half * GROUP + g + 1) * HEAD_DIM) for g in range(GROUP)]
@@ -591,12 +592,27 @@
             return tuple(out)
 
         done = lax.fori_loop(0, chunks, chunk, tuple(jnp.zeros((HEAD_DIM, rows), F32) for _ in range(GROUP)))
+        cosine, sine = cos_ref[...], sin_ref[...]
         for g in range(GROUP):
             grad = done[g] * (HEAD_DIM**-0.5)
             u, w = grad[: HEAD_DIM // 2], grad[HEAD_DIM // 2 :]
             n = (half * GROUP + g) * HEAD_DIM
             dq_ref[n : n + HEAD_DIM // 2, :] = (u * cosine + w * sine).astype(BF16)
             dq_ref[n + HEAD_DIM // 2 : n + HEAD_DIM, :] = (w * cosine - u * sine).astype(BF16)
+        between(half)
+
+
+def attend_back_kernel(
+    chunks, rows, off_ref, lo_ref, cos_ref, sin_ref, q_ref, kv_ref, g_ref, lse_ref, delta_ref, dq_ref, dkv_ref, bias
+):
+    @pl.when(pl.program_id(0) == 0)
+    def _():
+        make_bias(bias, lo_ref, chunks, rows)
+
+    attend_back_pair(
+        chunks, rows, off_ref[0], cos_ref, sin_ref, q_ref, kv_ref, g_ref, lse_ref, delta_ref, dq_ref, dkv_ref, bias,
+        lambda half: None,
+    )
 
 
 def attention_specs(rows, span):
@@ -651,55 +667,6 @@
     )(offset.reshape(1), lo, cos_t, sin_t, query_t, window, grad_t, lse, delta)
 
 
-def swap_kernel(x_ref, o_ref, lsem, ss, rs):
-    me = lax.axis_index("dev")
-    n = x_ref.shape[0]
-    greet([lax.rem(me + d, n) for d in range(1, n)])
-
-    def copy(d):
-        target = lax.rem(me + d, n)
-        return pltpu.make_async_remote_copy(
-            src_ref=x_ref.at[target], dst_ref=o_ref.at[me], send_sem=ss.at[d], recv_sem=rs.at[d],
-            device_id=(target,), device_id_type=MESH)
-
-    own = pltpu.make_async_copy(x_ref.at[me], o_ref.at[me], lsem)
-    own.start()
-
-    def start(d, _):
-        copy(d).start()
-        return 0
-    lax.fori_loop(1, n, start, 0)
-
-    def end(d, _):
-        copy(d).wait_recv()
-        copy(d).wait_send()
-        return 0
-    lax.fori_loop(1, n, end, 0)
-    own.wait()
-
-
-def swap(values, cid):
-    if not meshed():
-        return lax.all_to_all(values, "dev", split_axis=0, concat_axis=0, tiled=True)
-    n = values.shape[0]
-    dma = pltpu.SemaphoreType.DMA
-    return pl.pallas_call(
-        swap_kernel,
-        out_shape=jax.ShapeDtypeStruct(values.shape, values.dtype),
-        in_specs=[pl.BlockSpec(memory_space=pltpu.VMEM)],
-        out_specs=pl.BlockSpec(memory_space=pltpu.VMEM),
-        scratch_shapes=[dma, dma((n,)), dma((n,))],
-        compiler_params=pltpu.CompilerParams(collective_id=cid, has_side_effects=True),
-        name="swap",
-    )(values)
-
-
-def swap_rows(values, cid):
-    n, width = values.shape
-    padded = jnp.pad(values.reshape(n, width // 128, 128), ((0, 0), (0, 8 - width // 128), (0, 0)))
-    return swap(padded, cid)[:, : width // 128].reshape(n, width)
-
-
 def hits(slot_ref, slots):
     width = slot_ref.shape[-1]
     return slot_ref[0] == lax.broadcasted_iota(jnp.int32, (slots, width), 0)
@@ -751,6 +718,584 @@
         cost_estimate=pl.CostEstimate(flops=10**9, bytes_accessed=33 * 10**6, transcendentals=0),
         name="combine",
     )(slot, rows)
+
+
+SLOTS = 80
+
+
+def order_of(i):
+    return jnp.where(i < 2, i, 5 - i)
+
+
+def far_first(i):
+    return jnp.where(i == 0, 2, jnp.where(i == 3, 0, 2 * i - 1))
+
+
+def greet_all():
+    me = lax.axis_index("dev")
+    barrier = pltpu.get_barrier_semaphore()
+
+    def signal(d, _):
+        pl.semaphore_signal(barrier, inc=1, device_id=(lax.rem(me + d, 32),), device_id_type=MESH)
+        return 0
+    lax.fori_loop(1, 32, signal, 0)
+    pl.semaphore_wait(barrier, 31)
+
+
+class Swap:
+    def __init__(self, source, into, ss, rs):
+        self.me = lax.axis_index("dev")
+        self.source, self.into, self.ss, self.rs = source, into, ss, rs
+
+    def copy(self, d):
+        target = lax.rem(self.me + d, 32)
+        return pltpu.make_async_remote_copy(
+            src_ref=self.source(target), dst_ref=self.into.at[self.me], send_sem=self.ss.at[d], recv_sem=self.rs.at[d],
+            device_id=(target,), device_id_type=MESH)
+
+    def start(self):
+        def one(d, _):
+            self.copy(d).start()
+            return 0
+        lax.fori_loop(1, 32, one, 0)
+        self.into[self.me] = self.source(self.me)[...]
+
+    def wait_recv(self):
+        def one(d, _):
+            self.copy(d).wait_recv()
+            return 0
+        lax.fori_loop(1, 32, one, 0)
+
+    def wait_send(self):
+        def one(d, _):
+            self.copy(d).wait_send()
+            return 0
+        lax.fori_loop(1, 32, one, 0)
+
+
+def in_plane(y, x, c):
+    return (y * 2 + x) * 2 + c
+
+
+def chosen_rows(slots_ref, block, expert):
+    row = slots_ref[block, pl.ds(expert, 1), :]
+    return row == lax.broadcasted_iota(jnp.int32, (SLOTS, row.shape[1]), 0).astype(F32)
+
+
+def experts_kernel(
+    x_ref, gates_ref, slots_ref, u_ref, wg_ref, wu_ref, wd_ref,
+    xi_out, ui_out, dx_out, y_out, hg_ref, dg_ref, du_ref, gg_ref,
+    gates, land, stage, xi, ubuf, ui_buf, dx_buf, y_buf,
+    gs, gr, zs, zr, fs, fr, cs, cr, own_sem, usem, xsem, osem,
+):
+    z, y, x, c = place()
+    rows, model = x_ref.shape
+    half = model // 2
+    sibling = number(z, y, x, 1 - c)
+    greet_all()
+    swap = Swap(lambda t: gates_ref.at[t], gates, gs, gr)
+    cols = [pl.ds(0, half), pl.ds(half, half)]
+    beside = [number(z, 1 - y, x, c), number(z, y, 1 - x, c)]
+    across = [(y, 1 - x), (1 - y, x)]
+
+    def to_z(p, d):
+        return pltpu.make_async_remote_copy(
+            src_ref=x_ref.at[:, cols[p]], dst_ref=land.at[p, 0, d], send_sem=zs.at[p, d], recv_sem=zr.at[p, d],
+            device_id=(number(lax.rem(z + d, 4), y, x, c),), device_id_type=MESH)
+
+    def hop(p, k):
+        return pltpu.make_async_remote_copy(
+            src_ref=land.at[p, 0, k], dst_ref=land.at[p, 1, k], send_sem=fs.at[p, k], recv_sem=fr.at[p, k],
+            device_id=(beside[p],), device_id_type=MESH)
+
+    def block_of(p, h, k, yy, xx, cc):
+        zz = lax.rem(z + 4 - k, 4)
+        if p == 0:
+            return number(zz, (1 - yy) if h else yy, xx, cc)
+        return number(zz, yy, (1 - xx) if h else xx, cc)
+
+    def served(p, h, k, t):
+        block = block_of(p, h, k, y, x, c)
+        ay, ax = across[p]
+        target = [number(z, y, x, 1 - c), number(z, ay, ax, c), number(z, ay, ax, 1 - c)][t]
+        return pltpu.make_async_remote_copy(
+            src_ref=stage.at[p, h, k, t],
+            dst_ref=xi.at[pl.ds(pl.multiple_of(block * SLOTS, 16), SLOTS), cols[p]],
+            send_sem=cs.at[p, h, k, t], recv_sem=cr.at[p, h, k, t], device_id=(target,), device_id_type=MESH)
+
+    def serve(p, h, k):
+        block = block_of(p, h, k, y, x, c)
+        source = land[p, h, k]
+        ay, ax = across[p]
+        for t, expert in enumerate([in_plane(y, x, 1 - c), in_plane(ay, ax, c), in_plane(ay, ax, 1 - c), in_plane(y, x, c)]):
+            chosen = jnp.where(chosen_rows(slots_ref, block, expert), 1.0, 0.0).astype(BF16)
+            got = dims(chosen, source, 1, 0).astype(BF16)
+            if t < 3:
+                stage[p, h, k, t] = got
+                served(p, h, k, t).start()
+            else:
+                xi[pl.ds(pl.multiple_of(block * SLOTS, 16), SLOTS), cols[p]] = got
+
+    own = [pltpu.make_async_copy(x_ref.at[:, cols[p]], land.at[p, 0, 0], own_sem.at[p]) for p in range(2)]
+    for p in range(2):
+        own[p].start()
+    for d in (1, 3, 2):
+        for p in range(2):
+            to_z(p, d).start()
+
+    def chip_of(u):
+        group, k = u // 4, order_of(lax.rem(u, 4))
+        dy, dx = lax.rem(group, 2), group // 2
+        zz = lax.rem(z + 4 - k, 4)
+        yy = jnp.where(dy == 1, 1 - y, y)
+        xx = jnp.where(dx == 1, 1 - x, x)
+        return (zz * 2 + yy) * 2 + xx
+
+    def load_up(u):
+        at = pl.ds(pl.multiple_of(chip_of(u) * 2 * rows, 16), 2 * rows)
+        return pltpu.make_async_copy(u_ref.at[at, :], ubuf.at[lax.rem(u, 2)], usem.at[lax.rem(u, 2)])
+
+    load_up(0).start()
+    swap.start()
+    for p in range(2):
+        own[p].wait()
+        hop(p, 0).start()
+
+    def first_stage(i, _):
+        k = order_of(i)
+        for p in range(2):
+            @pl.when(i > 0)
+            def _(p=p):
+                to_z(p, k).wait_recv()
+                hop(p, k).start()
+            serve(p, 0, k)
+        return 0
+    lax.fori_loop(0, 4, first_stage, 0)
+    swap.wait_recv()
+
+    def store(n, buf, out, u):
+        at = pl.ds(pl.multiple_of(chip_of(u) * 2 * SLOTS, 16), 2 * SLOTS)
+        return pltpu.make_async_copy(buf.at[lax.rem(u, 2)], out.at[at, :], osem.at[n, lax.rem(u, 2)])
+
+    def stores(u):
+        return [store(0, ui_buf, ui_out, u), store(1, dx_buf, dx_out, u), store(2, y_buf, y_out, u)]
+
+    def keep(u):
+        at = pl.ds(pl.multiple_of(chip_of(u) * 2 * SLOTS, 16), 2 * SLOTS)
+        return pltpu.make_async_copy(xi.at[at, :], xi_out.at[at, :], xsem.at[u])
+
+    def unit(u, _):
+        group, k = u // 4, order_of(lax.rem(u, 4))
+        slot = lax.rem(u, 2)
+        chip = chip_of(u)
+
+        @pl.when(u < 15)
+        def _():
+            load_up(u + 1).start()
+
+        @pl.when(group == 0)
+        def _():
+            for p in range(2):
+                hop(p, k).wait_recv()
+                serve(p, 1, k)
+            for p in range(2):
+                served(p, 0, k, 0).wait_recv()
+
+        @pl.when(group == 1)
+        def _():
+            served(0, 1, k, 0).wait_recv()
+            served(1, 0, k, 1).wait_recv()
+            served(1, 0, k, 2).wait_recv()
+
+        @pl.when(group == 2)
+        def _():
+            served(1, 1, k, 0).wait_recv()
+            served(0, 0, k, 1).wait_recv()
+            served(0, 0, k, 2).wait_recv()
+
+        @pl.when(group == 3)
+        def _():
+            for p in range(2):
+                served(p, 1, k, 1).wait_recv()
+                served(p, 1, k, 2).wait_recv()
+
+        @pl.when(u >= 2)
+        def _():
+            for s in stores(u - 2):
+                s.wait()
+
+        load_up(u).wait()
+        at = pl.ds(pl.multiple_of(chip * 2 * SLOTS, 16), 2 * SLOTS)
+        expert = in_plane(y, x, c)
+        picks, gate, up_rows = [], [], []
+        for core in range(2):
+            block = chip * 2 + core
+            hit = chosen_rows(slots_ref, block, expert)
+            picks.append(hit)
+            gate_row = jnp.concatenate([gates[block, 0:1, :], gates[block, 1:2, :]], axis=1)
+            gate.append(jnp.sum(jnp.where(hit, gate_row, 0.0), axis=1, keepdims=True))
+            up_rows.append(
+                dims(jnp.where(hit, 1.0, 0.0).astype(BF16), ubuf[slot, core * rows : (core + 1) * rows, :], 1, 0).astype(BF16)
+            )
+        gate_of_slot = jnp.concatenate(gate, axis=0)
+        ui = jnp.concatenate(up_rows, axis=0)
+        ui_buf[slot] = ui
+        hidden_up = dims(ui, wd_ref[...], 1, 1)
+        rows_in = xi[at, :]
+        gate_in = dims(rows_in, wg_ref[...], 1, 0)
+        up_in = dims(rows_in, wu_ref[...], 1, 0)
+        sig = 1.0 / (1.0 + jnp.exp(-gate_in))
+        silu = gate_in * sig
+        hidden = (silu * up_in).astype(BF16).astype(F32)
+        gated = (hidden * gate_of_slot).astype(BF16)
+        hidden_grad = hidden_up * gate_of_slot
+        gate_back = (hidden_grad * up_in * sig * (1.0 + gate_in * (1.0 - sig))).astype(BF16)
+        up_back = (hidden_grad * silu).astype(BF16)
+        hg_ref[at, :] = gated
+        dg_ref[at, :] = gate_back
+        du_ref[at, :] = up_back
+        dx_buf[slot] = (dims(gate_back, wg_ref[...], 1, 1) + dims(up_back, wu_ref[...], 1, 1)).astype(BF16)
+        y_buf[slot] = dims(gated, wd_ref[...], 1, 0).astype(BF16)
+        gate_grad = jnp.sum(hidden * hidden_up, axis=1, keepdims=True)
+        for core in range(2):
+            block = chip * 2 + core
+            row = jnp.sum(jnp.where(picks[core], gate_grad[core * SLOTS : (core + 1) * SLOTS], 0.0), axis=0, keepdims=True)
+            gg_ref[block, 0:1, :] = row[:, :128]
+            gg_ref[block, 1:2, :] = row[:, 128:]
+        for s in stores(u):
+            s.start()
+        keep(u).start()
+        return 0
+
+    lax.fori_loop(0, 16, unit, 0)
+    for u in (14, 15):
+        for s in stores(u):
+            s.wait()
+
+    def last(u, _):
+        keep(u).wait()
+        return 0
+    lax.fori_loop(0, 16, last, 0)
+
+    def sent(k, _):
+        for p in range(2):
+            hop(p, k).wait_send()
+
+            @pl.when(k > 0)
+            def _(p=p):
+                to_z(p, k).wait_send()
+            for h in range(2):
+                for t in range(3):
+                    served(p, h, k, t).wait_send()
+        return 0
+    lax.fori_loop(0, 4, sent, 0)
+    swap.wait_send()
+
+
+def run_experts(normed, gates, slots, upstream, gate_weight, up_weight, down_weight):
+    rows, model = normed.shape
+    ff = gate_weight.shape[1]
+    half = model // 2
+    n = 32 * SLOTS
+    hbm, vmem = pl.BlockSpec(memory_space=pl.ANY), pl.BlockSpec(memory_space=pltpu.VMEM)
+    dma = pltpu.SemaphoreType.DMA
+    long = jax.ShapeDtypeStruct((n, model), BF16)
+    short = jax.ShapeDtypeStruct((n, ff), BF16)
+    return pl.pallas_call(
+        experts_kernel,
+        in_specs=[hbm, vmem, vmem, hbm, vmem, vmem, vmem],
+        out_specs=[hbm] * 4 + [vmem] * 4,
+        out_shape=[long] * 4 + [short] * 3 + [jax.ShapeDtypeStruct((32, 8, 128), F32)],
+        scratch_shapes=[
+            pltpu.VMEM((32, 8, 128), F32),
+            pltpu.VMEM((2, 2, 4, rows, half), BF16),
+            pltpu.VMEM((2, 2, 4, 3, SLOTS, half), BF16),
+            pltpu.VMEM((n, model), BF16),
+            pltpu.VMEM((2, 2 * rows, model), BF16),
+            pltpu.VMEM((2, 2 * SLOTS, model), BF16),
+            pltpu.VMEM((2, 2 * SLOTS, model), BF16),
+            pltpu.VMEM((2, 2 * SLOTS, model), BF16),
+            dma((32,)), dma((32,)), dma((2, 4)), dma((2, 4)), dma((2, 4)), dma((2, 4)),
+            dma((2, 2, 4, 3)), dma((2, 2, 4, 3)), dma((2,)), dma((2,)), dma((16,)), dma((3, 2)),
+        ],
+        compiler_params=pltpu.CompilerParams(collective_id=13, has_side_effects=True, vmem_limit_bytes=56 * 2**20),
+        name="experts",
+    )(normed, gates, slots, upstream, gate_weight, up_weight, down_weight)
+
+
+class Back:
+    scratch = staticmethod(lambda rows, half: [
+        pltpu.VMEM((2, 2, 4, SLOTS, half), BF16),
+        pltpu.VMEM((2, 3, 2, 4, SLOTS, half), BF16),
+        pltpu.VMEM((2, 4, rows, half), BF16),
+        pltpu.VMEM((2, 4, rows, half), BF16),
+        pltpu.VMEM((2, 4, rows, half), BF16),
+        pltpu.VMEM((2, 4, rows, half), BF16),
+        pltpu.SemaphoreType.DMA((2, 2, 4)),
+        pltpu.SemaphoreType.DMA((2, 3, 2, 4)), pltpu.SemaphoreType.DMA((2, 3, 2, 4)),
+        pltpu.SemaphoreType.DMA((2, 4)), pltpu.SemaphoreType.DMA((2, 4)),
+        pltpu.SemaphoreType.DMA((2, 4)), pltpu.SemaphoreType.DMA((2, 4)),
+    ])
+    n_scratch = 13
+
+    def __init__(self, rows_ref, slots_ref, o_ref, scratch):
+        self.rows_ref, self.slots_ref, self.o_ref = rows_ref, slots_ref, o_ref
+        (self.own, self.rin, self.sout, self.rb, self.zout, self.rz,
+         self.own_sem, self.ts, self.tr, self.bs, self.br, self.zs, self.zr) = scratch
+        self.z, self.y, self.x, self.c = place()
+        half = rows_ref.shape[1] // 2
+        self.cols = [pl.ds(0, half), pl.ds(half, half)]
+
+    def block(self, p, h, k, yy, xx, cc):
+        zz = lax.rem(self.z + k, 4)
+        if p == 0:
+            return number(zz, (1 - yy) if h else yy, xx, cc)
+        return number(zz, yy, (1 - xx) if h else xx, cc)
+
+    def sources(self, p):
+        y, x, c = self.y, self.x, self.c
+        ay, ax = (y, 1 - x) if p == 0 else (1 - y, x)
+        return [(y, x, 1 - c), (ay, ax, c), (ay, ax, 1 - c)]
+
+    def slot_rows(self, block, p):
+        return self.rows_ref.at[pl.ds(pl.multiple_of(block * SLOTS, 16), SLOTS), self.cols[p]]
+
+    def to(self, p, t, h, k):
+        place_of = self.sources(p)[t]
+        return pltpu.make_async_remote_copy(
+            src_ref=self.slot_rows(self.block(p, h, k, *place_of), p), dst_ref=self.rin.at[p, t, h, k],
+            send_sem=self.ts.at[p, t, h, k], recv_sem=self.tr.at[p, t, h, k],
+            device_id=(number(self.z, *place_of),), device_id_type=MESH)
+
+    def mine(self, p, h, k):
+        return pltpu.make_async_copy(
+            self.slot_rows(self.block(p, h, k, self.y, self.x, self.c), p), self.own.at[p, h, k], self.own_sem.at[p, h, k])
+
+    def second(self, p, k):
+        z, y, x, c = self.z, self.y, self.x, self.c
+        target = number(z, 1 - y, x, c) if p == 0 else number(z, y, 1 - x, c)
+        return pltpu.make_async_remote_copy(
+            src_ref=self.sout.at[p, k], dst_ref=self.rb.at[p, k], send_sem=self.bs.at[p, k], recv_sem=self.br.at[p, k],
+            device_id=(target,), device_id_type=MESH)
+
+    def third(self, p, k):
+        target = number(lax.rem(self.z + k, 4), self.y, self.x, self.c)
+        return pltpu.make_async_remote_copy(
+            src_ref=self.zout.at[p, k], dst_ref=self.rz.at[p, k], send_sem=self.zs.at[p, k], recv_sem=self.zr.at[p, k],
+            device_id=(target,), device_id_type=MESH)
+
+    def start(self):
+        for h in (1, 0):
+            def one(i, _, h=h):
+                k = far_first(i)
+                for p in range(2):
+                    for t in (1, 2, 0):
+                        self.to(p, t, h, k).start()
+                    self.mine(p, h, k).start()
+                return 0
+            lax.fori_loop(0, 4, one, 0)
+
+    def dense(self, p, h, k):
+        self.mine(p, h, k).wait()
+        for t in range(3):
+            self.to(p, t, h, k).wait_recv()
+        block = self.block(p, h, k, self.y, self.x, self.c)
+        total = None
+        for t, who in enumerate([(self.y, self.x, self.c)] + self.sources(p)):
+            hit = chosen_rows(self.slots_ref, block, in_plane(*who))
+            chosen = jnp.where(hit, 1.0, 0.0).astype(BF16)
+            values = self.own[p, h, k] if t == 0 else self.rin[p, t - 1, h, k]
+            term = dims(chosen, values, 0, 0)
+            total = term if total is None else total + term
+        return total
+
+    def step(self, u):
+        k = far_first(lax.rem(u, 4))
+
+        @pl.when(u < 4)
+        def _():
+            for p in range(2):
+                self.sout[p, k] = self.dense(p, 1, k).astype(BF16)
+                self.second(p, k).start()
+
+        @pl.when(u >= 4)
+        def _():
+            for p in range(2):
+                total = self.dense(p, 0, k)
+                self.second(p, k).wait_recv()
+                total = total + self.rb[p, k].astype(F32)
+
+                @pl.when(k > 0)
+                def _(p=p, total=total):
+                    self.zout[p, k] = total.astype(BF16)
+                    self.third(p, k).start()
+
+                @pl.when(k == 0)
+                def _(p=p, total=total):
+                    self.o_ref[:, self.cols[p]] = total
+
+    def finish(self):
+        for p in range(2):
+            for k in range(1, 4):
+                self.third(p, k).wait_recv()
+            self.o_ref[:, self.cols[p]] += (
+                self.rz[p, 1].astype(F32) + self.rz[p, 2].astype(F32) + self.rz[p, 3].astype(F32)
+            )
+
+        def one(k, _):
+            for p in range(2):
+                self.second(p, k).wait_send()
+
+                @pl.when(k > 0)
+                def _(p=p):
+                    self.third(p, k).wait_send()
+                for t in range(3):
+                    for h in range(2):
+                        self.to(p, t, h, k).wait_send()
+            return 0
+        lax.fori_loop(0, 4, one, 0)
+
+
+def grads_kernel(
+    dx_ref, slots_ref, gg_ref, xi_ref, ui_ref, hg_ref, dg_ref, du_ref,
+    o_ref, back_ref, wg_out, wu_out, wd_out, xcol, ucol, gout, uout, dout, gs, gr, isem, osem, *scratch,
+):
+    greet_all()
+    swap = Swap(lambda t: gg_ref.at[t], back_ref, gs, gr)
+    rs = Back(dx_ref, slots_ref, o_ref, scratch)
+    rs.start()
+    swap.start()
+
+    def col(i):
+        return pl.ds(pl.multiple_of(i * 256, 256), 256)
+
+    def loads(i):
+        s = lax.rem(i, 2)
+        return [
+            pltpu.make_async_copy(xi_ref.at[:, col(i)], xcol.at[s], isem.at[0, s]),
+            pltpu.make_async_copy(ui_ref.at[:, col(i)], ucol.at[s], isem.at[1, s]),
+        ]
+
+    def stores(i):
+        s = lax.rem(i, 2)
+        return [
+            pltpu.make_async_copy(gout.at[s], wg_out.at[col(i), :], osem.at[0, s]),
+            pltpu.make_async_copy(uout.at[s], wu_out.at[col(i), :], osem.at[1, s]),
+            pltpu.make_async_copy(dout.at[s], wd_out.at[:, col(i)], osem.at[2, s]),
+        ]
+
+    for cp in loads(0):
+        cp.start()
+
+    def one(u, _):
+        @pl.when(u < 6)
+        def _():
+            s = lax.rem(u, 2)
+
+            @pl.when(u < 5)
+            def _():
+                for cp in loads(u + 1):
+                    cp.start()
+
+            for cp in loads(u):
+                cp.wait()
+
+            @pl.when(u >= 2)
+            def _():
+                for cp in stores(u - 2):
+                    cp.wait()
+
+            rows_in = xcol[s]
+            gout[s] = dims(rows_in, dg_ref[...], 0, 0)
+            uout[s] = dims(rows_in, du_ref[...], 0, 0)
+            dout[s] = dims(hg_ref[...], ucol[s], 0, 0)
+            for cp in stores(u):
+                cp.start()
+
+        rs.step(u)
+        return 0
+
+    lax.fori_loop(0, 8, one, 0)
+    for i in (4, 5):
+        for cp in stores(i):
+            cp.wait()
+    swap.wait_recv()
+    rs.finish()
+    swap.wait_send()
+
+
+def run_grads(dx, slots, gg, xi, ui, hg, dg, du):
+    rows, model = slots.shape[2], dx.shape[1]
+    ff = hg.shape[1]
+    n = dx.shape[0]
+    hbm, vmem = pl.BlockSpec(memory_space=pl.ANY), pl.BlockSpec(memory_space=pltpu.VMEM)
+    dma = pltpu.SemaphoreType.DMA
+    return pl.pallas_call(
+        grads_kernel,
+        in_specs=[hbm, vmem, vmem, hbm, hbm, vmem, vmem, vmem],
+        out_specs=[vmem, vmem, hbm, hbm, hbm],
+        out_shape=[
+            jax.ShapeDtypeStruct((rows, model), F32),
+            jax.ShapeDtypeStruct((32, 8, 128), F32),
+            jax.ShapeDtypeStruct((model, ff), F32),
+            jax.ShapeDtypeStruct((model, ff), F32),
+            jax.ShapeDtypeStruct((ff, model), F32),
+        ],
+        scratch_shapes=[
+            pltpu.VMEM((2, n, 256), BF16), pltpu.VMEM((2, n, 256), BF16),
+            pltpu.VMEM((2, 256, ff), F32), pltpu.VMEM((2, 256, ff), F32), pltpu.VMEM((2, ff, 256), F32),
+            dma((32,)), dma((32,)), dma((2, 2)), dma((3, 2)),
+        ] + Back.scratch(rows, model // 2),
+        compiler_params=pltpu.CompilerParams(collective_id=14, has_side_effects=True, vmem_limit_bytes=56 * 2**20),
+        name="grads",
+    )(dx, slots, gg, xi, ui, hg, dg, du)
+
+
+def attend_back_mesh_kernel(
+    chunks, rows, lo_ref, cos_ref, sin_ref, q_ref, kv_ref, g_ref, lse_ref, delta_ref, y_ref, slots_ref,
+    dq_ref, dkv_ref, o_ref, bias, *scratch,
+):
+    greet_all()
+    rs = Back(y_ref, slots_ref, o_ref, scratch)
+    rs.start()
+    make_bias(bias, lo_ref, chunks, rows)
+    width = 2 * GROUP * HEAD_DIM
+
+    def pair(j, _):
+        lanes = pl.ds(pl.multiple_of(j * 2 * HEAD_DIM, 2 * HEAD_DIM), 2 * HEAD_DIM)
+        head = pl.ds(pl.multiple_of(j * width, width), width)
+
+        def between(half):
+            rs.step(2 * j + half)
+
+        attend_back_pair(
+            chunks, rows, lax.rem(lax.axis_index("dev"), 2), cos_ref, sin_ref, q_ref.at[head, :], kv_ref.at[:, :, lanes], g_ref.at[head, :],
+            lse_ref.at[pl.ds(j, 1)], delta_ref.at[pl.ds(j, 1)], dq_ref.at[head, :], dkv_ref.at[:, :, lanes], bias, between,
+        )
+        return 0
+
+    lax.fori_loop(0, KEY_HEADS // 2, pair, 0)
+    rs.finish()
+
+
+def attend_back_mesh(query_t, window, lo, grad_t, lse, delta, cos_t, sin_t, y, slots):
+    rows, span = query_t.shape[1], window.shape[1]
+    chunks = span // rows - 1
+    model = y.shape[1]
+    hbm, vmem = pl.BlockSpec(memory_space=pl.ANY), pl.BlockSpec(memory_space=pltpu.VMEM)
+    return pl.pallas_call(
+        functools.partial(attend_back_mesh_kernel, chunks, rows),
+        in_specs=[vmem] * 8 + [hbm, vmem],
+        out_specs=[vmem] * 3,
+        out_shape=[
+            jax.ShapeDtypeStruct(query_t.shape, BF16),
+            jax.ShapeDtypeStruct(window.shape, BF16),
+            jax.ShapeDtypeStruct((rows, model), F32),
+        ],
+        scratch_shapes=[pltpu.VMEM((chunks * rows, rows), F32)] + Back.scratch(rows, model // 2),
+        compiler_params=pltpu.CompilerParams(collective_id=15, has_side_effects=True, vmem_limit_bytes=56 * 2**20),
+        name="attend_back",
+    )(lo, cos_t, sin_t, query_t, window, grad_t, lse, delta, y, slots)
 
 
 def rms_scale(values):
@@ -798,12 +1343,10 @@
     rows, model = tokens.shape
     split = devices // EXPERTS
     capacity = split * ((9 * rows * TOP + 8 * EXPERTS * split - 1) // (8 * EXPERTS * split))
-    my_expert = lax.axis_index("dev") // split
     weight_rows = query_weight.shape[0]
 
     all_upstream = lax.all_gather(cotangent, "dev", axis=0, tiled=True)
     output_matrix = lax.all_gather(output_weight, "dev", axis=0, tiled=True)
-    all_claims = lax.all_gather(jnp.concatenate([expert_picks, priority], axis=1), "dev", axis=0, tiled=True)
 
     extra = jnp.concatenate([router_weight, first_gain[:, None], second_gain[:, None]], axis=1)
     pad = (-extra.shape[1]) % 128
@@ -817,19 +1360,12 @@
     gain_first = matrices[:, QKV + EXPERTS].astype(F32)
     gain_second = matrices[:, QKV + EXPERTS + 1].astype(F32)
 
-    claims = all_claims.reshape(devices, rows, 2 * TOP)
-    mine = claims[:, :, :TOP] == my_expert
-    picked_mine = jnp.any(mine, axis=2)
-    turn = jnp.sum(jnp.where(mine, claims[:, :, TOP:], 0), axis=2)
-    turn = jnp.where(picked_mine, turn, jnp.int32(2**30))
+    one_hot = expert_picks[:, :, None] == jnp.arange(EXPERTS, dtype=jnp.int32)
+    picked_any = jnp.any(one_hot, axis=1)
+    turn = jnp.sum(jnp.where(one_hot, priority[:, :, None], 0), axis=1)
+    turn = jnp.where(picked_any, turn, jnp.int32(2**30)).T
     rank = jnp.sum((turn[:, None, :] < turn[:, :, None]).astype(jnp.int32), axis=2)
-    kept = picked_mine & (rank < capacity)
-    slot = jnp.where(kept, rank, -1)
-    pair_slot = jnp.where(
-        slot.reshape(devices // 2, 2, rows) >= 0,
-        slot.reshape(devices // 2, 2, rows) + jnp.array([[0], [capacity]], jnp.int32),
-        -1,
-    ).reshape(devices // 2, 1, 2 * rows)
+    slot_rows = jnp.where(picked_any.T & (rank < capacity), rank, -1).astype(F32)
 
     inputs = tokens.astype(F32)
     scale_one = rms_scale(inputs)
@@ -843,7 +1379,7 @@
     query_t = rotate_t(qkv_t[:q_width], cos_t, sin_t).astype(BF16) * BF16(HEAD_DIM**-0.5)
     key = rotate_t(qkv_t[q_width : q_width + k_width], cos_t, sin_t).astype(BF16).T
     value = qkv_t[q_width + k_width :].astype(BF16).T
-    window, offset = window_of(jnp.stack([key, value]))
+    window, offset, plane_slots = window_of(jnp.stack([key, value]), slot_rows.reshape(-1, 8, rows))
     lo = (jnp.arange(rows, dtype=jnp.int32) - positions)[None, :]
     attended_t, lse = attend(query_t, window, offset, lo)
     residual = inputs + dims(attended_t, output_matrix, 0, 0)
@@ -851,41 +1387,57 @@
     normed_two = (residual * scale_two * gain_second).astype(BF16)
 
     logits = dims(normed_two, router_matrix, 1, 0)
-    one_hot = expert_picks[:, :, None] == jnp.arange(EXPERTS, dtype=jnp.int32)
-    picked_any = jnp.any(one_hot, axis=1)
     logits = jnp.where(picked_any, logits, MASKED)
     picked_exp = jnp.exp(logits - jnp.max(logits, axis=1, keepdims=True))
     gates = picked_exp / jnp.sum(picked_exp, axis=1, keepdims=True)
-    gate_rows = swap_rows(jnp.repeat(gates.T, split, axis=0), 5)
-
-    all_normed = gathered(normed_two, 2, True)
-    expert_in, expert_up = dispatch(pair_slot, all_normed, all_upstream, 2 * capacity)
-    slot_hit = slot[:, None, :] == jnp.arange(capacity, dtype=jnp.int32)[None, :, None]
-    gate_of_slot = jnp.sum(jnp.where(slot_hit, gate_rows[:, None, :], 0.0), axis=2).reshape(-1, 1)
-    gate_in = dims(expert_in, gate_weight, 1, 0)
-    up_in = dims(expert_in, up_weight, 1, 0)
-    sigmoid_gate = 1.0 / (1.0 + jnp.exp(-gate_in))
-    silu_gate = gate_in * sigmoid_gate
-    hidden = (silu_gate * up_in).astype(BF16)
-    gated_hidden = (hidden.astype(F32) * gate_of_slot).astype(BF16)
-    hidden_up = dims(expert_up, down_weight, 1, 1)
-    hidden_grad = hidden_up * gate_of_slot
-    gate_grad_slot = jnp.sum(hidden.astype(F32) * hidden_up, axis=1).reshape(devices, capacity)
-    gate_in_grad = (hidden_grad * up_in * sigmoid_gate * (1.0 + gate_in * (1.0 - sigmoid_gate))).astype(BF16)
-    up_in_grad = (hidden_grad * silu_gate).astype(BF16)
-    partial_in = (dims(gate_in_grad, gate_weight, 1, 1) + dims(up_in_grad, up_weight, 1, 1)).astype(BF16)
-    gate_grad_rows = jnp.sum(jnp.where(slot_hit, gate_grad_slot[:, :, None], 0.0), axis=1)
-    returned_grad = reduced(combine(pair_slot, partial_in, 2 * capacity), 3, True)
-    gate_grad = swap_rows(gate_grad_rows, 6)
-    gate_grad = jnp.sum(gate_grad.reshape(EXPERTS, split, rows), axis=1).T
-
-    partial_out = dims(gated_hidden, down_weight, 1, 0).astype(BF16)
-    dense_out = combine(pair_slot, partial_out, 2 * capacity)
-    mixture = lax.psum_scatter(dense_out, "dev", scatter_dimension=0, tiled=True)
-    layer_output = (residual + mixture.astype(F32)).astype(BF16)
-    down_gradient = dims(gated_hidden, expert_up, 0, 0)
-    gate_gradient = dims(expert_in, gate_in_grad, 0, 0)
-    up_gradient = dims(expert_in, up_in_grad, 0, 0)
+
+    if meshed():
+        gate_rows = jnp.pad(gates.T.reshape(EXPERTS, rows // 128, 128), ((0, 0), (0, 8 - rows // 128), (0, 0)))
+        expert_in, expert_up, grad_rows, out_rows, gated_hidden, gate_in_grad, up_in_grad, gate_grad_rows = run_experts(
+            normed_two, gate_rows, plane_slots, all_upstream, gate_weight, up_weight, down_weight
+        )
+        returned_grad, gate_grad, gate_gradient, up_gradient, down_gradient = run_grads(
+            grad_rows, plane_slots, gate_grad_rows, expert_in, expert_up, gated_hidden, gate_in_grad, up_in_grad
+        )
+        gate_grad = gate_grad[:, : rows // 128].reshape(EXPERTS, rows).T
+    else:
+        gate_rows, slot = (
+            lax.all_to_all(jnp.repeat(v, split, axis=0), "dev", split_axis=0, concat_axis=0, tiled=True)
+            for v in (gates.T, slot_rows)
+        )
+        pair_slot = jnp.where(
+            slot.reshape(devices // 2, 2, rows) >= 0,
+            slot.reshape(devices // 2, 2, rows) + jnp.array([[0], [capacity]], F32),
+            -1.0,
+        ).astype(jnp.int32).reshape(devices // 2, 1, 2 * rows)
+        all_normed = lax.all_gather(normed_two, "dev", axis=0, tiled=True)
+        expert_in, expert_up = dispatch(pair_slot, all_normed, all_upstream, 2 * capacity)
+        slot_hit = slot[:, None, :] == jnp.arange(capacity, dtype=F32)[None, :, None]
+        gate_of_slot = jnp.sum(jnp.where(slot_hit, gate_rows[:, None, :], 0.0), axis=2).reshape(-1, 1)
+        gate_in = dims(expert_in, gate_weight, 1, 0)
+        up_in = dims(expert_in, up_weight, 1, 0)
+        sigmoid_gate = 1.0 / (1.0 + jnp.exp(-gate_in))
+        silu_gate = gate_in * sigmoid_gate
+        hidden = (silu_gate * up_in).astype(BF16)
+        gated_hidden = (hidden.astype(F32) * gate_of_slot).astype(BF16)
+        hidden_up = dims(expert_up, down_weight, 1, 1)
+        hidden_grad = hidden_up * gate_of_slot
+        gate_grad_slot = jnp.sum(hidden.astype(F32) * hidden_up, axis=1).reshape(devices, capacity)
+        gate_in_grad = (hidden_grad * up_in * sigmoid_gate * (1.0 + gate_in * (1.0 - sigmoid_gate))).astype(BF16)
+        up_in_grad = (hidden_grad * silu_gate).astype(BF16)
+        partial_in = (dims(gate_in_grad, gate_weight, 1, 1) + dims(up_in_grad, up_weight, 1, 1)).astype(BF16)
+        gate_grad_rows = jnp.sum(jnp.where(slot_hit, gate_grad_slot[:, :, None], 0.0), axis=1)
+        returned_grad = lax.psum_scatter(
+            combine(pair_slot, partial_in, 2 * capacity), "dev", scatter_dimension=0, tiled=True
+        ).astype(F32)
+        gate_grad = lax.all_to_all(gate_grad_rows, "dev", split_axis=0, concat_axis=0, tiled=True)
+        gate_grad = jnp.sum(gate_grad.reshape(EXPERTS, split, rows), axis=1).T
+        partial_out = dims(gated_hidden, down_weight, 1, 0).astype(BF16)
+        dense_out = combine(pair_slot, partial_out, 2 * capacity)
+        mixture = lax.psum_scatter(dense_out, "dev", scatter_dimension=0, tiled=True).astype(F32)
+        down_gradient = dims(gated_hidden, expert_up, 0, 0)
+        gate_gradient = dims(expert_in, gate_in_grad, 0, 0)
+        up_gradient = dims(expert_in, up_in_grad, 0, 0)
 
     upstream = cotangent.astype(F32)
     logit_grad = (gates * (gate_grad - jnp.sum(gates * gate_grad, axis=1, keepdims=True))).astype(BF16)
@@ -905,7 +1457,13 @@
 
     delta = jnp.sum((attended_t.astype(F32) * grad_t.astype(F32)).reshape(QUERY_HEADS, HEAD_DIM, rows), axis=1)
     delta = jnp.pad(delta.reshape(KEY_HEADS // 2, 2 * GROUP, rows), ((0, 0), (0, 8 - 2 * GROUP), (0, 0)))
-    query_grad_t, window_grad = attend_back(query_t, window, offset, lo, grad_t, lse, delta, cos_t, sin_t)
+    if meshed():
+        query_grad_t, window_grad, mixture = attend_back_mesh(
+            query_t, window, lo, grad_t, lse, delta, cos_t, sin_t, out_rows, plane_slots
+        )
+    else:
+        query_grad_t, window_grad = attend_back(query_t, window, offset, lo, grad_t, lse, delta, cos_t, sin_t)
+    layer_output = (residual + mixture).astype(BF16)
     key_grad, value_grad = unwindow(window_grad)
     key_grad_t = rotate_t(key_grad.T, cos_t, -sin_t).astype(BF16)
     qkv_grad_t = jnp.concatenate([query_grad_t, key_grad_t, value_grad.T.astype(BF16)], axis=0)

time: 1020 us -> 867 us (0.85)
  matrix products: 105 us -> 36.3 us
  Pallas kernels: 771 us -> 716 us
  blocking collectives: 40.4 us -> 0 us
  waiting for transfers between devices: 6.11 us -> 26.8 us
  other arithmetic: 28.5 us -> 15.4 us
    pallas_call x7 -> x4, Pallas kernels: 207 us -> 491 us  [the longest x1 150 us: attend_back_mesh(): pl.pallas_call(functools.partial(attend_back_mesh_kernel, chunks, rows),...]
    pallas_call x2 -> x1, Pallas kernels: 276 us -> 56.7 us  [reduce_all(): pl.pallas_call(functools.partial(reduce_kernel, rows, cols, pieces), out_...]
    pallas_call x2 -> x1, Pallas kernels: 174 us -> 54.7 us  [gather_all(): pl.pallas_call(functools.partial(gather_kernel, rows, pieces), out_shape=...]
    dot_general x18 -> x9, matrix products: 105 us -> 36.3 us  [dims(): lax.dot_general(a, b, (((ca,), (cb,)), ((), ())), preferred_element_type=...]
    all_gather x1 -> x0, blocking collectives: 40.4 us -> none  [on_device(): lax.all_gather(jnp.concatenate([expert_picks, priority], axis=1), 'dev',...]
    all_gather x1, waiting for transfers between devices: 0.02 us -> 25.4 us  [on_device(): all_upstream = lax.all_gather(cotangent, 'dev', axis=0, tiled=True)]
  transfers between devices with their start and end apart: 4 -> 3, of which waited for: 1 -> 1; matrix products, arithmetic and copies ran while one was open for 13% -> 9% of each run, Pallas kernels for 73% -> 52%
where the time goes in v2:
time: 867 us; the launch traced here: 862 us
  Pallas kernels  716 us (83%)
  local copies, waits for them, and re-layouts  52.9 us (6%)
  matrix products  36.3 us (4%)
  waiting for transfers between devices  26.8 us (3%)
  other arithmetic  15.4 us (2%)
  between operations  14.5 us (2%)
    pallas_call x1, Pallas kernels, attend_back_mesh(): pl.pallas_call(functools.partial(attend_back_mesh_kernel, chunks, rows),...  150 us
    pallas_call x1, Pallas kernels, run_experts(): pl.pallas_call(experts_kernel, in_specs=[hbm, vmem, vmem, hbm, vmem, vmem...  137 us
    pallas_call x1, Pallas kernels, run_grads(): pl.pallas_call(grads_kernel, in_specs=[hbm, vmem, vmem, hbm, hbm, vmem, v...  132 us
    pallas_call x1, Pallas kernels, window_of(): pl.pallas_call(functools.partial(window_kernel, rows), out_shape=[jax.Sha...  71.9 us
    pallas_call x1, Pallas kernels, attend(): pl.pallas_call(functools.partial(attend_kernel, chunks, rows), grid=(KEY_...  70.1 us
    pallas_call x1, Pallas kernels, reduce_all(): pl.pallas_call(functools.partial(reduce_kernel, rows, cols, pieces), out_...  56.7 us
    pallas_call x1, Pallas kernels, gather_all(): pl.pallas_call(functools.partial(gather_kernel, rows, pieces), out_shape=...  54.7 us
    pallas_call x1, Pallas kernels, unwindow(): pl.pallas_call(functools.partial(unwindow_kernel, rows), out_shape=jax.Sh...  43.5 us
  transfers between devices with their start and end apart: 3, of which 1 were waited for; matrix products, arithmetic and copies ran while one was open for 9% of the time, Pallas kernels for 52%

profile of v2, /device:TPU:0, one launch (start us, length us, event | category | flops | bytes accessed | tf_op | source)
XLA Modules:
  0.0 861.7 jit_solution(10130525081582123041)
XLA Ops:
  7.2 0.7 all-gather.3.cloned.1.call-update
  8.0 0.7 all-gather.5.cloned.1.call-update
  8.7 0.8 copy.69
  9.5 0.8 copy.70
  10.3 0.8 copy.71
  11.0 1.7 concatenate.10.x_ref
  12.7 54.7 %gather_all.1 = bf16[1536,2688]{1,0:T(8,128)(2,1)} custom-call(bf16[48,2688]{1,0:T(8,128)(2,1)} %concatenate.10.x_ref), custom_call_target="tpu_custom_call" | custom-call | tf_op jit(solution)/shard_map/gather_all/pallas_call | solution.py:111
  67.5 1.8 convert_reduce_fusion.1
  69.3 0.2 fusion.5
  69.5 5.7 fusion.2
  75.3 1.4 copy-done.9
  76.8 0.2 fusion.33
  77.1 0.1 copy.72
  77.3 0.1 copy.82
  77.5 0.8 pad_maximum_fusion.3.kv_ref
  78.4 3.1 convert_reduce_fusion
  81.5 0.6 convert_bitcast_fusion.1.mine_ref
  82.1 71.9 %window.1 = (bf16[2,2560,512]{2,1,0:T(8,128)(2,1)}, f32[32,8,256]{2,1,0:T(8,128)}) custom-call(bf16[2,256,512]{2,1,0:T(8,128)(2,1)} %pad_maximum_fusion.3.kv_ref, f32[4,8,256]{2,1,0:T(8,128)} %convert_bitcast_fusion.1.mine_ref), custom_call_target="tpu_custom_call" | custom-call | tf_op jit(solution)/shard_map/window/pallas_call | solution.py:366
  154.1 0.3 subtract_convert_fusion
  154.5 2.8 copy-done.1
  157.3 70.1 %attend.1 = (bf16[1536,256]{1,0:T(8,128)(2,1)S(1)}, f32[4,8,256]{2,1,0:T(8,128)S(1)}) custom-call(s32[1]{0:T(128)} %bitcast.off_ref, s32[1,256]{1,0:T(1,128)S(1)} %bitcast.82, bf16[1536,256]{1,0:T(8,128)(2,1)S(1)} %bitcast.80, bf16[2,2560,512]{2,1,0:T(8,128)(2,1)S(1)} %copy-done.1), custom_call_target="tpu_custom_call" | custom-call | flops 7000000000 | bytes 8000000 | tf_op jit(solution)/shard_map/attend/pallas_call | solution.py:634
  227.4 0.6 copy-done.3
  228.0 3.8 multiply_reduce_fusion.2
  231.8 0.2 multiply_convert_fusion.x_ref
  232.1 0.9 copy-done.8
  232.9 1.4 fusion.32
  234.4 0.7 pad.8.gates_ref
  235.1 25.4 %all-gather.5.cloned.1.call-done.u_ref = bf16[8192,1536]{1,0:T(8,128)(2,1)} async-done(((bf16[256,1536]{1,0:T(8,128)(2,1)}), bf16[8192,1536]{1,0:T(8,128)(2,1)}) %all-gather.5.cloned.1.call-update) | async-done | bytes 25165840 | tf_op jit(solution)/shard_map/all_gather | solution.py:1348
  260.5 136.8 %experts.1 = (bf16[2560,1536]{1,0:T(8,128)(2,1)}, bf16[2560,1536]{1,0:T(8,128)(2,1)}, bf16[2560,1536]{1,0:T(8,128)(2,1)}, bf16[2560,1536]{1,0:T(8,128)(2,1)}, bf...) custom-call(bf16[256,1536]{1,0:T(8,128)(2,1)} %copy-done.8, ...), custom_call_target="tpu_custom_call" | custom-call | tf_op jit(solution)/shard_map/experts/pallas_call | solution.py:1004
  397.2 132.0 %grads.1 = (f32[256,1536]{1,0:T(8,128)}, f32[32,8,128]{2,1,0:T(8,128)}, f32[1536,512]{1,0:T(8,128)}, f32[1536,512]{1,0:T(8,128)}, f32[512,1536]{1,0:T(8,128)}) custom-call(bf16[2560,1536]{1,0:T(8,128)(2,1)} %get-tuple-element.35.dx_ref, f32[32,8,256]{2,1,0:T(8,128)} %get-tuple-element.34.slots_ref, f32[32,8,128]{2,1,0:T(8,128)} %get-tuple-element.36.gg_ref, ...), custom_call_target="tpu_custom_call" | custom-call | tf_op jit(solution)/shard_map/grads/pallas_call | solution.py:1233
  529.2 0.9 slice.72
  530.2 2.3 multiply_reduce_fusion
  532.5 0.5 multiply_subtract_fusion
  533.0 1.1 copy-done.5
  534.1 3.5 convolution_convert_fusion.1
  537.7 5.6 convert_multiply_fusion.5
  543.3 1.6 reduce_sum.109
  544.9 0.6 pad.9.delta_ref
  545.5 149.9 %attend_back.1 = (bf16[1536,256]{1,0:T(8,128)(2,1)}, bf16[2,2560,512]{2,1,0:T(8,128)(2,1)}, f32[256,1536]{1,0:T(8,128)}) custom-call(s32[1,256]{1,0:T(1,128)} %bitcast.83, f32[32,256]{1,0:T(8,128)} %copy-done.14, f32[32,256]{1,0:T(8,128)} %copy-done.17, bf16[1536,256]{1,0:T(8,128)(2,1)} %bitcast.81, bf16[2,2560,512]{2,1,0:T(8,128)(2,1)} %get-tuple-element.32.kv_ref, ...), custom_call_target="tpu_custom_call" | custom-call | tf_op jit(solution)/shard_map/attend_back/pallas_call | solution.py:1286
  695.5 2.5 copy-done
  698.0 43.5 %unwindow.1 = f32[2,256,512]{2,1,0:T(8,128)S(1)} custom-call(bf16[2,2560,512]{2,1,0:T(8,128)(2,1)S(1)} %copy-done), custom_call_target="tpu_custom_call" | custom-call | tf_op jit(solution)/shard_map/unwindow/pallas_call | solution.py:487
  741.5 0.8 slice_bitcast_fusion
  742.4 2.0 copy.75
  744.4 0.7 fusion.18
  745.1 1.1 copy.76
  746.3 1.4 convolution_convert_fusion.3
  747.7 0.9 copy.77
  748.7 7.1 fusion.12
  755.8 1.0 broadcast_in_dim.92
  756.8 1.0 broadcast_in_dim.93
  757.8 5.5 convolution_convert_fusion
  763.4 14.2 %concatenate.12.g_ref = bf16[1536,2816]{1,0:T(8,128)(2,1)} concatenate(bf16[1536,2560]{1,0:T(8,128)(2,1)} %convolution_convert_fusion, bf16[1536,32]{1,0:T(8,128)(2,1)} %copy.77, bf16[1536,1]{1,0:T(8,128)(2,1)} %broadcast_in_dim.92, bf16[1536,1]{1,0:T(8,128)(2,1)} %broadcast_in_dim.93, bf16[1536,222]{1,0:T(8,128)(2,1)S(1)} %broadcast_in_dim.91), dimensions={1} | concatenate | bytes 17301504 | tf_op jit(solution)/shard_map/concatenate | solution.py:1479
  777.6 56.7 %reduce_all.1 = f32[48,2816]{1,0:T(8,128)} custom-call(bf16[1536,2816]{1,0:T(8,128)(2,1)} %concatenate.12.g_ref), custom_call_target="tpu_custom_call" | custom-call | tf_op jit(solution)/shard_map/reduce_all/pallas_call | solution.py:238
  834.3 1.7 slice.76
  836.0 0.7 slice.80
  836.7 0.7 copy.80
  837.4 1.5 slice_reduce_fusion
  838.9 1.6 fusion.36
  840.6 4.0 fusion.9
  844.5 1.6 convert_element_type.113
  846.2 4.0 copy.89
  850.2 1.7 copy.90
  851.9 1.4 copy-done.10
  853.2 1.7 copy.91
  (67 shorter events, 0.9 us)
Async XLA Ops:
  7.2 220.8 %all-gather.3.cloned.1.call-start = ((), (), s32[]{:S(2)}) async-start(), calls=%async_computation.1 | async-start | bytes 4866048 | tf_op jit(solution)/shard_map/all_gather | solution.py:1349
  7.9 252.5 %all-gather.5.cloned.1.call-start = ((), (), s32[]{:S(2)}) async-start(), calls=%async_computation.2 | async-start | bytes 25952256 | tf_op jit(solution)/shard_map/all_gather | solution.py:1348
  8.7 835.9 %reduce-scatter.2.cloned.1.call-start = ((), (), s32[]{:S(2)}) async-start(), calls=%async_computation.3 | async-start | bytes 4866048 | tf_op jit(solution)/shard_map/reduce_scatter | solution.py:1455
  12.7 56.5 %copy-start.7 = (bf16[256,1536]{1,0:T(8,128)(2,1)S(1)}, bf16[256,1536]{1,0:T(8,128)(2,1)}, u32[]{:S(2)}) copy-start(bf16[256,1536]{1,0:T(8,128)(2,1)} %param.15) | copy-start | bytes 2359300
  75.2 1.5 copy-start.9
  75.3 1.4 copy-start.20
  76.7 0.7 copy-start.18
  76.7 0.8 copy-start.19
  76.8 77.7 %copy-start.4 = (s32[256]{0:T(256)}, s32[256]{0:T(256)S(1)}, u32[]{:S(2)}) copy-start(s32[256]{0:T(256)S(1)} %get-tuple-element.124) | copy-start | bytes 3076
  77.0 77.1 %copy-start.14 = (f32[32,256]{1,0:T(8,128)}, f32[32,256]{1,0:T(8,128)S(1)}, u32[]{:S(2)}) copy-start(f32[32,256]{1,0:T(8,128)S(1)} %get-tuple-element.118.cos_ref) | copy-start | bytes 98308
  77.0 77.1 %copy-start.17 = (f32[32,256]{1,0:T(8,128)}, f32[32,256]{1,0:T(8,128)S(1)}, u32[]{:S(2)}) copy-start(f32[32,256]{1,0:T(8,128)S(1)} %get-tuple-element.117.sin_ref) | copy-start | bytes 98308
  77.1 77.0 %slice-start = ((f32[2560,256]{1,0:T(8,128)}), f32[1536,256]{1,0:T(8,128)S(1)}, s32[]{:S(2)}) async-start(f32[2560,256]{1,0:T(8,128)} %copy-done.9), calls=%async_computation.4 | async-start | bytes 3145728 | tf_op jit(solution)/shard_map/slice | solution.py:1379
  154.5 72.9 %copy-start.2 = (bf16[24,2,32,256]{3,2,1,0:T(8,128)(2,1)}, bf16[24,2,32,256]{3,2,1,0:T(8,128)(2,1)S(1)}, u32[]{:S(2)}) copy-start(bf16[24,2,32,256]{3,2,1,0:T(8,128)(2,1)S(1)} %maximum_multiply_fusion) | copy-start | bytes 2359300
  154.5 2.8 copy-start.1
  227.4 0.6 copy-start.3
  232.1 0.9 copy-start.8
  530.2 2.3 copy-start.12
  533.0 1.1 copy-start.5
  695.5 2.5 copy-start
  742.4 6.2 copy-start.15
  745.1 3.5 copy-start.13
  748.7 9.1 %copy-start.16 = (bf16[1536,256]{1,0:T(8,128)(2,1)S(1)}, bf16[1536,256]{1,0:T(8,128)(2,1)}, u32[]{:S(2)}) copy-start(bf16[1536,256]{1,0:T(8,128)(2,1)} %get-tuple-element.47) | copy-start | bytes 2359300
  777.6 62.9 %copy-start.6 = (f32[256,1536]{1,0:T(8,128)S(1)}, f32[256,1536]{1,0:T(8,128)}, u32[]{:S(2)}) copy-start(f32[256,1536]{1,0:T(8,128)} %copy-done.5) | copy-start | bytes 4718596
  846.2 4.0 copy-start.11
  850.2 3.0 copy-start.10
Sparse Core Ops, SparseCore 0:
  10.9 78.5 all-gather.2
  92.4 168.0 all-gather.4
  537.8 152.9 reduce-scatter.1

commit v3 on v2

--- a/solution.py
+++ b/solution.py
@@ -119,7 +119,7 @@
     )(block)
 
 
-def reduce_kernel(rows, cols, pieces, g_ref, o_ref, acc, own, ra, rb, rz, own_sem, ssem, rsem, sa, ra_sem, sb, rb_sem, sz, rz_sem):
+def reduce_kernel(rows, cols, pieces, g_ref, more_ref, o_ref, acc, own, ra, rb, rz, own_sem, ssem, rsem, sa, ra_sem, sb, rb_sem, sz, rz_sem):
     z, y, x, c = place()
     greet(partners_of(z, y, x, c))
     sibling = number(z, y, x, 1 - c)
@@ -133,18 +133,26 @@
         zz, yy, xx = where(dy, dx, k)
         return (zz * 2 + yy) * 2 + xx
 
-    def chip_rows(dy, dx, k, core):
+    main = g_ref.shape[1]
+    sides = ((g_ref, pl.ds(0, main)), (more_ref, pl.ds(main, cols - main)))
+
+    def chip_rows(ref, dy, dx, k, core):
         zz, yy, xx = where(dy, dx, k)
-        return g_ref.at[pl.ds(pl.multiple_of(number(zz, yy, xx, core) * rows, 16), rows), :]
+        return ref.at[pl.ds(pl.multiple_of(number(zz, yy, xx, core) * rows, 16), rows), :]
 
     def to_sibling(n):
-        dy, dx, k = blocks[n]
-        return pltpu.make_async_remote_copy(
-            src_ref=chip_rows(dy, dx, k, 1 - c), dst_ref=acc.at[lane(dy, dx, k)],
-            send_sem=ssem.at[n], recv_sem=rsem.at[n], device_id=(sibling,), device_id_type=MESH)
+        return [
+            pltpu.make_async_remote_copy(
+                src_ref=chip_rows(ref, *blocks[n], 1 - c), dst_ref=acc.at[lane(*blocks[n]), :, at],
+                send_sem=ssem.at[n, i], recv_sem=rsem.at[n, i], device_id=(sibling,), device_id_type=MESH)
+            for i, (ref, at) in enumerate(sides)
+        ]
 
     def load(n):
-        return pltpu.make_async_copy(chip_rows(*blocks[n], c), own.at[n % 2], own_sem.at[n % 2])
+        return [
+            pltpu.make_async_copy(chip_rows(ref, *blocks[n], c), own.at[n % 2, :, at], own_sem.at[n % 2, i])
+            for i, (ref, at) in enumerate(sides)
+        ]
 
     def part(ref, p):
         r0, nr, c0, nc = pieces[p]
@@ -180,14 +188,19 @@
         lax.fori_loop(0, nr // step, chunk, 0)
 
     for n in range(16):
-        to_sibling(n).start()
-    load(0).start()
+        for cp in to_sibling(n):
+            cp.start()
+    for cp in load(0):
+        cp.start()
     for n in range(16):
         dy, dx, k = blocks[n]
         if n + 1 < 16:
-            load(n + 1).start()
-        load(n).wait()
-        to_sibling(n).wait_recv()
+            for cp in load(n + 1):
+                cp.start()
+        for cp in load(n):
+            cp.wait()
+        for cp in to_sibling(n):
+            cp.wait_recv()
         block = acc.at[lane(dy, dx, k)]
         add(block, [block, own.at[n % 2]], rows)
         if dx:
@@ -215,7 +228,8 @@
         block = part(acc.at[lane(0, 0, 0)], p)
         add(part(o_ref, p), [block, ra.at[p, 0, 0], rb.at[p, 0]] + [rz.at[p, j] for j in range(3)], pieces[p][1])
     for n in range(16):
-        to_sibling(n).wait_send()
+        for cp in to_sibling(n):
+            cp.wait_send()
     for p in range(2):
         for k in range(4):
             first(p, 0, k, 1 - p, p).wait_send()
@@ -225,32 +239,27 @@
                 third(p, k).wait_send()
 
 
-def reduce_all(dense, cid, by_rows, out_dtype=jnp.float32):
-    rows, cols = dense.shape[0] // 32, dense.shape[1]
-    if by_rows:
-        pieces = ((0, rows // 2, 0, cols), (rows // 2, rows // 2, 0, cols))
-    else:
-        half = (cols // 256) * 128
-        assert cols == 2 * half
-        pieces = ((0, rows, 0, half), (0, rows, half, cols - half))
-    pr, pc = pieces[0][1], pieces[0][3]
+def reduce_all(dense, more, cid):
+    rows, cols = dense.shape[0] // 32, dense.shape[1] + more.shape[1]
+    half = cols // 2
+    pieces = ((0, rows, 0, half), (0, rows, half, half))
     dma = pltpu.SemaphoreType.DMA
     return pl.pallas_call(
         functools.partial(reduce_kernel, rows, cols, pieces),
-        out_shape=jax.ShapeDtypeStruct((rows, cols), out_dtype),
-        in_specs=[pl.BlockSpec(memory_space=pl.ANY)],
+        out_shape=jax.ShapeDtypeStruct((rows, cols), jnp.float32),
+        in_specs=[pl.BlockSpec(memory_space=pl.ANY)] * 2,
         out_specs=pl.BlockSpec(memory_space=pltpu.VMEM),
         scratch_shapes=[
             pltpu.VMEM((16, rows, cols), dense.dtype),
             pltpu.VMEM((2, rows, cols), dense.dtype),
-            pltpu.VMEM((2, 2, 4, pr, pc), dense.dtype),
-            pltpu.VMEM((2, 4, pr, pc), dense.dtype),
-            pltpu.VMEM((2, 3, pr, pc), dense.dtype),
-            dma((2,)), dma((16,)), dma((16,)), dma((2, 2, 4)), dma((2, 2, 4)), dma((2, 4)), dma((2, 4)), dma((2, 3)), dma((2, 3)),
+            pltpu.VMEM((2, 2, 4, rows, half), dense.dtype),
+            pltpu.VMEM((2, 4, rows, half), dense.dtype),
+            pltpu.VMEM((2, 3, rows, half), dense.dtype),
+            dma((2, 2)), dma((16, 2)), dma((16, 2)), dma((2, 2, 4)), dma((2, 2, 4)), dma((2, 4)), dma((2, 4)), dma((2, 3)), dma((2, 3)),
         ],
         compiler_params=pltpu.CompilerParams(collective_id=cid, has_side_effects=True, vmem_limit_bytes=56 * 2**20),
         name="reduce_all",
-    )(dense)
+    )(dense, more)
 
 
 from jax.sharding import PartitionSpec as P
@@ -277,111 +286,98 @@
     return lax.dot_general(a, b, (((ca,), (cb,)), ((), ())), preferred_element_type=F32)
 
 
-def window_kernel(rows, kv_ref, mine_ref, o_ref, slots_ref, lsem, ss, rs, gs, gr):
-    z, y, x, c = place()
-    p = y * 2 + x
-    sibling = number(z, y, x, 1 - c)
-    up = number(lax.rem(z + 1, 4), y, x, c)
-    down = number(lax.rem(z + 3, 4), y, x, c)
-
-    def chip(q):
-        return (z * 4 + q) * 2 + c
-
-    near = [chip(lax.rem(p + d, 4)) for d in (1, 2, 3)]
-    greet_all()
-    swap = Swap(lambda t: mine_ref.at[t // 8], slots_ref, gs, gr)
-
-    def slot(s, core):
-        return o_ref.at[:, pl.ds(pl.multiple_of((2 * s + core) * rows, 16), rows), :]
-
-    def copy(source, s, n, target):
+class Window:
+    scratch = [pltpu.SemaphoreType.DMA((2,)), pltpu.SemaphoreType.DMA((9,)), pltpu.SemaphoreType.DMA((9,))]
+
+    def __init__(self, rows, kv_ref, out, scratch):
+        self.rows, self.kv_ref, self.out = rows, kv_ref, out
+        self.lsem, self.ss, self.rs = scratch
+        self.z, self.y, self.x, self.c = place()
+        self.p = self.y * 2 + self.x
+        self.sibling = number(self.z, self.y, self.x, 1 - self.c)
+        self.near = [(self.z * 4 + lax.rem(self.p + d, 4)) * 2 + self.c for d in (1, 2, 3)]
+        self.own_in = pltpu.make_async_copy(kv_ref, self.slot(4, self.c), self.lsem.at[0])
+        self.stand_in = pltpu.make_async_copy(kv_ref, self.slot(0, self.c), self.lsem.at[1])
+        self.to_up = self.copy(kv_ref, 0, 0, number(lax.rem(self.z + 1, 4), self.y, self.x, self.c))
+
+    def slot(self, s, core):
+        return self.out.at[:, pl.ds(pl.multiple_of((2 * s + core) * self.rows, 16), self.rows), :]
+
+    def copy(self, source, s, n, target):
         return pltpu.make_async_remote_copy(
-            src_ref=source, dst_ref=slot(s, c), send_sem=ss.at[n], recv_sem=rs.at[n],
+            src_ref=source, dst_ref=self.slot(s, self.c), send_sem=self.ss.at[n], recv_sem=self.rs.at[n],
             device_id=(target,), device_id_type=MESH)
 
-    own_in = pltpu.make_async_copy(kv_ref, slot(4, c), lsem.at[0])
-    own_in.start()
-    to_up = copy(kv_ref, 0, 0, up)
-
-    @pl.when(z < 3)
-    def _():
-        to_up.start()
-
-    stand_in = pltpu.make_async_copy(kv_ref, slot(0, c), lsem.at[1])
-
-    @pl.when(z == 0)
-    def _():
-        stand_in.start()
-
-    for d in (1, 3, 2):
-        @pl.when(p + d < 4)
-        def _(d=d):
-            copy(kv_ref, 4 - d, d, near[d - 1]).start()
-
-    to_sibling = {4: copy(kv_ref, 4, 4, sibling)}
-    to_sibling[4].start()
-    swap.start()
-
-    @pl.when(z == 0)
-    def _():
-        stand_in.wait()
-
-    @pl.when(z > 0)
-    def _():
-        to_up.wait_recv()
-
-    for d in (3, 1, 2):
-        @pl.when(p + d >= 4)
-        def _(d=d):
-            copy(slot(0, c), 4 - d, d, near[d - 1]).start()
-
-    to_sibling[0] = copy(slot(0, c), 0, 5, sibling)
-    to_sibling[0].start()
-    for d in (1, 3, 2):
-        copy(kv_ref, 4 - d, d, near[d - 1]).wait_recv()
-        to_sibling[4 - d] = copy(slot(4 - d, c), 4 - d, 5 + d, sibling)
-        to_sibling[4 - d].start()
-    for s in range(5):
-        pltpu.make_async_remote_copy(
-            src_ref=kv_ref, dst_ref=slot(s, 1 - c), send_sem=ss.at[0],
-            recv_sem=rs.at[{4: 4, 0: 5}.get(s, 9 - s)], device_id=(sibling,), device_id_type=MESH).wait_recv()
-    own_in.wait()
-
-    @pl.when(z < 3)
-    def _():
-        to_up.wait_send()
-
-    for d in (1, 2, 3):
-        copy(kv_ref, 4 - d, d, near[d - 1]).wait_send()
-    for s in range(5):
-        to_sibling[s].wait_send()
-    swap.wait_recv()
-    swap.wait_send()
-
-
-def window_of(kv, slots):
-    rows, width = kv.shape[1:]
-    if meshed():
-        dma = pltpu.SemaphoreType.DMA
-        full, plane_slots = pl.pallas_call(
-            functools.partial(window_kernel, rows),
-            out_shape=[
-                jax.ShapeDtypeStruct((2, 10 * rows, width), kv.dtype),
-                jax.ShapeDtypeStruct((32, 8, rows), F32),
-            ],
-            in_specs=[pl.BlockSpec(memory_space=pl.ANY), pl.BlockSpec(memory_space=pltpu.VMEM)],
-            out_specs=[pl.BlockSpec(memory_space=pl.ANY), pl.BlockSpec(memory_space=pltpu.VMEM)],
-            scratch_shapes=[dma((2,)), dma((9,)), dma((9,)), dma((32,)), dma((32,))],
-            compiler_params=pltpu.CompilerParams(collective_id=11, has_side_effects=True),
-            name="window",
-        )(kv, slots)
-        return full, lax.rem(lax.axis_index("dev"), 2), plane_slots
+    def own_near(self, d):
+        return self.copy(self.kv_ref, 4 - d, d, self.near[d - 1])
+
+    def across(self, s):
+        source = self.kv_ref if s == 4 else self.slot(s, self.c)
+        return self.copy(source, s, {4: 4, 0: 5}.get(s, 9 - s), self.sibling)
+
+    def start(self):
+        self.own_in.start()
+
+        @pl.when(self.z < 3)
+        def _():
+            self.to_up.start()
+
+        @pl.when(self.z == 0)
+        def _():
+            self.stand_in.start()
+
+        for d in (1, 3, 2):
+            @pl.when(self.p + d < 4)
+            def _(d=d):
+                self.own_near(d).start()
+        self.across(4).start()
+
+    def previous(self):
+        @pl.when(self.z == 0)
+        def _():
+            self.stand_in.wait()
+
+        @pl.when(self.z > 0)
+        def _():
+            self.to_up.wait_recv()
+
+        for d in (3, 1, 2):
+            @pl.when(self.p + d >= 4)
+            def _(d=d):
+                self.copy(self.slot(0, self.c), 4 - d, d, self.near[d - 1]).start()
+        self.across(0).start()
+
+    def pass_on(self):
+        for d in (1, 3, 2):
+            self.own_near(d).wait_recv()
+            self.across(4 - d).start()
+
+    def end(self):
+        for s in range(5):
+            pltpu.make_async_remote_copy(
+                src_ref=self.kv_ref, dst_ref=self.slot(s, 1 - self.c), send_sem=self.ss.at[0],
+                recv_sem=self.rs.at[{4: 4, 0: 5}.get(s, 9 - s)], device_id=(self.sibling,), device_id_type=MESH).wait_recv()
+        self.own_in.wait()
+
+    def sent(self):
+        @pl.when(self.z < 3)
+        def _():
+            self.to_up.wait_send()
+
+        for d in (1, 2, 3):
+            self.own_near(d).wait_send()
+        for s in range(5):
+            self.across(s).wait_send()
+
+
+def window_of(kv):
+    rows = kv.shape[1]
     devices = lax.axis_size("dev")
     back = (MAXDOC + rows - 2) // rows
     parts = [
         lax.ppermute(kv, "dev", [(i - d, i) for i in range(d, devices)]) for d in range(back, 0, -1)
     ]
-    return jnp.concatenate(parts + [kv, jnp.zeros_like(kv)], axis=1), jnp.int32(0), None
+    return jnp.concatenate(parts + [kv, jnp.zeros_like(kv)], axis=1)
 
 
 def unwindow_kernel(rows, g_ref, o_ref, mine, got, near_got, far, lsem, ss, rs):
@@ -520,44 +516,55 @@
     lax.fori_loop(0, chunks, fill, 0)
 
 
-def attend_kernel(chunks, rows, off_ref, lo_ref, q_ref, kv_ref, o_ref, lse_ref, bias):
-    @pl.when(pl.program_id(0) == 0)
-    def _():
-        make_bias(bias, lo_ref, chunks, rows)
-
-    off = off_ref[0]
+def side_by_side(ref, half):
+    first = half * GROUP
+    return jnp.concatenate(
+        [ref[(first + g) * HEAD_DIM : (first + g + 1) * HEAD_DIM, :] for g in range(GROUP)], axis=1
+    )
+
+
+def stats_of(ref, half):
+    return jnp.concatenate([ref[0, half * GROUP + g : half * GROUP + g + 1, :] for g in range(GROUP)], axis=1)
+
+
+def attend_pair(chunks, rows, off, q_ref, kv_ref, o_ref, lse_ref, bias, between):
     lse_ref[...] = jnp.zeros_like(lse_ref)
+    width = GROUP * rows
     for half in range(2):
         lanes = slice(half * HEAD_DIM, (half + 1) * HEAD_DIM)
-        queries = [q_ref[(half * GROUP + g) * HEAD_DIM : (half * GROUP + g + 1) * HEAD_DIM, :] for g in range(GROUP)]
+        queries = side_by_side(q_ref, half)
 
         def chunk(i, carry, lanes=lanes, queries=queries):
             ch = chunks - 1 - i
             at = pl.ds(pl.multiple_of((ch + off) * rows, rows), rows)
             key, value = kv_ref[0, at, lanes], kv_ref[1, at, lanes]
             shift = bias[pl.ds(pl.multiple_of(ch * rows, rows), rows), :]
-            out = []
-            for g in range(GROUP):
-                top, total, mixed = carry[g]
-                score = dims(key, queries[g], 1, 0) + shift
-                new_top = jnp.maximum(top, jnp.max(score, axis=0, keepdims=True))
-                weight = jnp.exp(score - new_top)
-                fade = jnp.exp(top - new_top)
-                total = total * fade + jnp.sum(weight, axis=0, keepdims=True)
-                mixed = mixed * fade + dims(value, weight.astype(BF16), 0, 0)
-                out.append((new_top, total, mixed))
-            return tuple(out)
-
-        start = tuple(
-            (jnp.full((1, rows), MASKED, F32), jnp.zeros((1, rows), F32), jnp.zeros((HEAD_DIM, rows), F32))
-            for _ in range(GROUP)
-        )
-        done = lax.fori_loop(0, chunks, chunk, start)
+            top, total, mixed = carry
+            score = dims(key, queries, 1, 0) + jnp.concatenate([shift] * GROUP, axis=1)
+            new_top = jnp.maximum(top, jnp.max(score, axis=0, keepdims=True))
+            weight = jnp.exp(score - new_top)
+            fade = jnp.exp(top - new_top)
+            total = total * fade + jnp.sum(weight, axis=0, keepdims=True)
+            mixed = mixed * fade + dims(value, weight.astype(BF16), 0, 0)
+            return new_top, total, mixed
+
+        start = (jnp.full((1, width), MASKED, F32), jnp.zeros((1, width), F32), jnp.zeros((HEAD_DIM, width), F32))
+        top, total, mixed = lax.fori_loop(0, chunks, chunk, start, unroll=3)
+        mixed = (mixed / total).astype(BF16)
+        lse = top + jnp.log(total)
         for g in range(GROUP):
-            top, total, mixed = done[g]
             n = half * GROUP + g
-            o_ref[n * HEAD_DIM : (n + 1) * HEAD_DIM, :] = (mixed / total).astype(BF16)
-            lse_ref[0, n : n + 1, :] = top + jnp.log(total)
+            o_ref[n * HEAD_DIM : (n + 1) * HEAD_DIM, :] = mixed[:, g * rows : (g + 1) * rows]
+            lse_ref[0, n : n + 1, :] = lse[:, g * rows : (g + 1) * rows]
+        between(half)
+
+
+def attend_kernel(chunks, rows, off_ref, lo_ref, q_ref, kv_ref, o_ref, lse_ref, bias):
+    @pl.when(pl.program_id(0) == 0)
+    def _():
+        make_bias(bias, lo_ref, chunks, rows)
+
+    attend_pair(chunks, rows, off_ref[0], q_ref, kv_ref, o_ref, lse_ref, bias, lambda half: None)
 
 
 def attend_back_pair(
@@ -567,34 +574,25 @@
     dkv_ref[:, unused, :] = jnp.zeros((2, rows, 2 * HEAD_DIM), BF16)
     for half in range(2):
         lanes = slice(half * HEAD_DIM, (half + 1) * HEAD_DIM)
-        own = [slice((half * GROUP + g) * HEAD_DIM, (half * GROUP + g + 1) * HEAD_DIM) for g in range(GROUP)]
-        queries = [q_ref[s, :] for s in own]
-        grads = [g_ref[s, :] for s in own]
-        lses = [lse_ref[0, half * GROUP + g : half * GROUP + g + 1, :] for g in range(GROUP)]
-        deltas = [delta_ref[0, half * GROUP + g : half * GROUP + g + 1, :] for g in range(GROUP)]
-
-        def chunk(ch, carry, lanes=lanes, queries=queries, grads=grads, lses=lses, deltas=deltas):
+        queries, grads = side_by_side(q_ref, half), side_by_side(g_ref, half)
+        lse, delta = stats_of(lse_ref, half), stats_of(delta_ref, half)
+
+        def chunk(ch, query_grad, lanes=lanes, queries=queries, grads=grads, lse=lse, delta=delta):
             at = pl.ds(pl.multiple_of((ch + off) * rows, rows), rows)
             key, value = kv_ref[0, at, lanes], kv_ref[1, at, lanes]
             shift = bias[pl.ds(pl.multiple_of(ch * rows, rows), rows), :]
-            dk = jnp.zeros((rows, HEAD_DIM), F32)
-            dv = jnp.zeros((rows, HEAD_DIM), F32)
-            out = []
-            for g in range(GROUP):
-                weight = jnp.exp(dims(key, queries[g], 1, 0) + shift - lses[g])
-                back = dims(value, grads[g], 1, 0)
-                score_grad = (weight * (back - deltas[g])).astype(BF16)
-                dv = dv + dims(weight.astype(BF16), grads[g], 1, 1)
-                dk = dk + dims(score_grad, queries[g], 1, 1)
-                out.append(carry[g] + dims(key, score_grad, 0, 0))
-            dkv_ref[0, at, lanes] = dk.astype(BF16)
-            dkv_ref[1, at, lanes] = dv.astype(BF16)
-            return tuple(out)
-
-        done = lax.fori_loop(0, chunks, chunk, tuple(jnp.zeros((HEAD_DIM, rows), F32) for _ in range(GROUP)))
+            score = dims(key, queries, 1, 0) + jnp.concatenate([shift] * GROUP, axis=1)
+            weight = jnp.exp(score - lse)
+            score_grad = (weight * (dims(value, grads, 1, 0) - delta)).astype(BF16)
+            dkv_ref[0, at, lanes] = dims(score_grad, queries, 1, 1).astype(BF16)
+            dkv_ref[1, at, lanes] = dims(weight.astype(BF16), grads, 1, 1).astype(BF16)
+            return query_grad + dims(key, score_grad, 0, 0)
+
+        done = lax.fori_loop(0, chunks, chunk, jnp.zeros((HEAD_DIM, GROUP * rows), F32), unroll=3)
+        done = done * (HEAD_DIM**-0.5)
         cosine, sine = cos_ref[...], sin_ref[...]
         for g in range(GROUP):
-            grad = done[g] * (HEAD_DIM**-0.5)
+            grad = done[:, g * rows : (g + 1) * rows]
             u, w = grad[: HEAD_DIM // 2], grad[HEAD_DIM // 2 :]
             n = (half * GROUP + g) * HEAD_DIM
             dq_ref[n : n + HEAD_DIM // 2, :] = (u * cosine + w * sine).astype(BF16)
@@ -723,10 +721,6 @@
 SLOTS = 80
 
 
-def order_of(i):
-    return jnp.where(i < 2, i, 5 - i)
-
-
 def far_first(i):
     return jnp.where(i == 0, 2, jnp.where(i == 3, 0, 2 * i - 1))
 
@@ -782,110 +776,229 @@
     return row == lax.broadcasted_iota(jnp.int32, (SLOTS, row.shape[1]), 0).astype(F32)
 
 
+def greet_near():
+    z, y, x, c = place()
+    greet(
+        [number(z, y, x, 1 - c)]
+        + [number(z, 1 - y, x, cc) for cc in (c, 1 - c)]
+        + [number(z, y, 1 - x, cc) for cc in (c, 1 - c)]
+        + [number(lax.rem(z + d, 4), y, x, c) for d in (1, 2, 3)]
+    )
+
+
+class Forth:
+    scratch = staticmethod(lambda rows, half: [
+        pltpu.VMEM((2, 2, 4, rows, half), BF16),
+        pltpu.VMEM((2, 2, 4, 4, SLOTS, half), BF16),
+        pltpu.SemaphoreType.DMA((2, 2, 4)), pltpu.SemaphoreType.DMA((2, 4)),
+        pltpu.SemaphoreType.DMA((2, 4)), pltpu.SemaphoreType.DMA((2, 4)),
+        pltpu.SemaphoreType.DMA((2, 2, 4, 4)), pltpu.SemaphoreType.DMA((2, 2, 4, 3)), pltpu.SemaphoreType.DMA((2,)),
+    ])
+    n_scratch = 9
+
+    def __init__(self, x_ref, slots_ref, xi, scratch):
+        self.x_ref, self.slots_ref, self.xi = x_ref, slots_ref, xi
+        self.land, self.stage, self.zs, self.zr, self.fs, self.fr, self.cs, self.cr, self.own_sem = scratch
+        self.z, self.y, self.x, self.c = place()
+        half = x_ref.shape[1] // 2
+        self.cols = [pl.ds(0, half), pl.ds(half, half)]
+
+    def turn(self, i):
+        middle = jnp.where(i < 2, i, 5 - i)
+        return jnp.where(self.z == 0, lax.rem(4 - i, 4), jnp.where(self.z == 3, i, middle))
+
+    def to_z(self, p, up, k, own=False):
+        step = 1 if up else 3
+        source = self.x_ref.at[:, self.cols[p]] if own else self.land.at[p, 0, k]
+        there = lax.rem(k + step, 4)
+        return pltpu.make_async_remote_copy(
+            src_ref=source, dst_ref=self.land.at[p, 0, there],
+            send_sem=self.zs.at[p, int(up), k], recv_sem=self.zr.at[p, there],
+            device_id=(number(lax.rem(self.z + step, 4), self.y, self.x, self.c),), device_id_type=MESH)
+
+    def hop(self, p, k):
+        z, y, x, c = self.z, self.y, self.x, self.c
+        beside = number(z, 1 - y, x, c) if p == 0 else number(z, y, 1 - x, c)
+        return pltpu.make_async_remote_copy(
+            src_ref=self.land.at[p, 0, k], dst_ref=self.land.at[p, 1, k],
+            send_sem=self.fs.at[p, k], recv_sem=self.fr.at[p, k], device_id=(beside,), device_id_type=MESH)
+
+    def block(self, p, h, k):
+        zz = lax.rem(self.z + 4 - k, 4)
+        if p == 0:
+            return number(zz, (1 - self.y) if h else self.y, self.x, self.c)
+        return number(zz, self.y, (1 - self.x) if h else self.x, self.c)
+
+    def who(self, p):
+        y, x, c = self.y, self.x, self.c
+        ay, ax = (y, 1 - x) if p == 0 else (1 - y, x)
+        return [(y, x, 1 - c), (ay, ax, c), (ay, ax, 1 - c), (y, x, c)]
+
+    def slots_at(self, p, h, k):
+        return self.xi.at[pl.ds(pl.multiple_of(self.block(p, h, k) * SLOTS, 16), SLOTS), self.cols[p]]
+
+    def served(self, p, h, k, t):
+        return pltpu.make_async_remote_copy(
+            src_ref=self.stage.at[p, h, k, t], dst_ref=self.slots_at(p, h, k),
+            send_sem=self.cs.at[p, h, k, t], recv_sem=self.cr.at[p, h, k, t],
+            device_id=(number(self.z, *self.who(p)[t]),), device_id_type=MESH)
+
+    def kept(self, p, h, k):
+        return pltpu.make_async_copy(self.stage.at[p, h, k, 3], self.slots_at(p, h, k), self.cs.at[p, h, k, 3])
+
+    def serve(self, p, h, k):
+        block = self.block(p, h, k)
+        source = self.land[p, h, k]
+        for t, to in enumerate(self.who(p)):
+            chosen = jnp.where(chosen_rows(self.slots_ref, block, in_plane(*to)), 1.0, 0.0).astype(BF16)
+            self.stage[p, h, k, t] = dims(chosen, source, 1, 0).astype(BF16)
+            if t < 3:
+                self.served(p, h, k, t).start()
+            else:
+                self.kept(p, h, k).start()
+
+    def own(self, p):
+        return pltpu.make_async_copy(self.x_ref.at[:, self.cols[p]], self.land.at[p, 0, 0], self.own_sem.at[p])
+
+    def along(self, i, use):
+        k = self.turn(i)
+        zz = lax.rem(self.z + 4 - k, 4)
+        for p in range(2):
+            @pl.when((zz < self.z) & (self.z < 3))
+            def _(p=p):
+                use(self.to_z(p, True, k))
+
+            @pl.when((zz > self.z) & (self.z > 0))
+            def _(p=p):
+                use(self.to_z(p, False, k))
+
+    def along_own(self, use):
+        for p in range(2):
+            @pl.when(self.z < 3)
+            def _(p=p):
+                use(self.to_z(p, True, 0, own=True))
+
+            @pl.when(self.z > 0)
+            def _(p=p):
+                use(self.to_z(p, False, 0, own=True))
+
+    def start(self):
+        for p in range(2):
+            self.own(p).start()
+        self.along_own(lambda cp: cp.start())
+
+    def one(self, i):
+        k = self.turn(i)
+
+        @pl.when(i == 0)
+        def _():
+            for p in range(2):
+                self.own(p).wait()
+
+        @pl.when(i > 0)
+        def _():
+            for p in range(2):
+                self.to_z(p, True, lax.rem(k + 3, 4)).wait_recv()
+
+        self.along(i, lambda cp: cp.start())
+        for p in range(2):
+            self.hop(p, k).start()
+        for p in range(2):
+            self.serve(p, 0, k)
+
+    def two(self, i):
+        k = self.turn(i)
+        for p in range(2):
+            self.hop(p, k).wait_recv()
+            self.serve(p, 1, k)
+
+    def arrived(self, group, i):
+        k = self.turn(i)
+
+        @pl.when(group == 0)
+        def _():
+            for p in range(2):
+                self.served(p, 0, k, 0).wait_recv()
+                self.kept(p, 0, k).wait()
+
+        @pl.when(group == 1)
+        def _():
+            self.kept(0, 1, k).wait()
+            self.served(0, 1, k, 0).wait_recv()
+            self.served(1, 0, k, 1).wait_recv()
+            self.served(1, 0, k, 2).wait_recv()
+
+        @pl.when(group == 2)
+        def _():
+            self.kept(1, 1, k).wait()
+            self.served(1, 1, k, 0).wait_recv()
+            self.served(0, 0, k, 1).wait_recv()
+            self.served(0, 0, k, 2).wait_recv()
+
+        @pl.when(group == 3)
+        def _():
+            for p in range(2):
+                self.served(p, 1, k, 1).wait_recv()
+                self.served(p, 1, k, 2).wait_recv()
+
+    def chip(self, group, i):
+        dy, dx = lax.rem(group, 2), group // 2
+        zz = lax.rem(self.z + 4 - self.turn(i), 4)
+        yy = jnp.where(dy == 1, 1 - self.y, self.y)
+        xx = jnp.where(dx == 1, 1 - self.x, self.x)
+        return (zz * 2 + yy) * 2 + xx
+
+    def sent(self):
+        self.along_own(lambda cp: cp.wait_send())
+
+        def each(i, _):
+            k = self.turn(i)
+            self.along(i, lambda cp: cp.wait_send())
+            for p in range(2):
+                self.hop(p, k).wait_send()
+                for h in range(2):
+                    for t in range(3):
+                        self.served(p, h, k, t).wait_send()
+            return 0
+        lax.fori_loop(0, 4, each, 0)
+
+
 def experts_kernel(
-    x_ref, gates_ref, slots_ref, u_ref, wg_ref, wu_ref, wd_ref,
-    xi_out, ui_out, dx_out, y_out, hg_ref, dg_ref, du_ref, gg_ref,
-    gates, land, stage, xi, ubuf, ui_buf, dx_buf, y_buf,
-    gs, gr, zs, zr, fs, fr, cs, cr, own_sem, usem, xsem, osem,
+    x_ref, gates_ref, slots_ref, ui_ref, wg_ref, wu_ref, wd_ref,
+    xi_out, dx_out, y_out, hg_ref, dg_ref, du_ref, gg_ref,
+    gates, xi, ubuf, dx_buf, y_buf, gs, gr, usem, xsem, osem, *scratch,
 ):
     z, y, x, c = place()
-    rows, model = x_ref.shape
-    half = model // 2
-    sibling = number(z, y, x, 1 - c)
+    rows = x_ref.shape[0]
     greet_all()
     swap = Swap(lambda t: gates_ref.at[t], gates, gs, gr)
-    cols = [pl.ds(0, half), pl.ds(half, half)]
-    beside = [number(z, 1 - y, x, c), number(z, y, 1 - x, c)]
-    across = [(y, 1 - x), (1 - y, x)]
-
-    def to_z(p, d):
-        return pltpu.make_async_remote_copy(
-            src_ref=x_ref.at[:, cols[p]], dst_ref=land.at[p, 0, d], send_sem=zs.at[p, d], recv_sem=zr.at[p, d],
-            device_id=(number(lax.rem(z + d, 4), y, x, c),), device_id_type=MESH)
-
-    def hop(p, k):
-        return pltpu.make_async_remote_copy(
-            src_ref=land.at[p, 0, k], dst_ref=land.at[p, 1, k], send_sem=fs.at[p, k], recv_sem=fr.at[p, k],
-            device_id=(beside[p],), device_id_type=MESH)
-
-    def block_of(p, h, k, yy, xx, cc):
-        zz = lax.rem(z + 4 - k, 4)
-        if p == 0:
-            return number(zz, (1 - yy) if h else yy, xx, cc)
-        return number(zz, yy, (1 - xx) if h else xx, cc)
-
-    def served(p, h, k, t):
-        block = block_of(p, h, k, y, x, c)
-        ay, ax = across[p]
-        target = [number(z, y, x, 1 - c), number(z, ay, ax, c), number(z, ay, ax, 1 - c)][t]
-        return pltpu.make_async_remote_copy(
-            src_ref=stage.at[p, h, k, t],
-            dst_ref=xi.at[pl.ds(pl.multiple_of(block * SLOTS, 16), SLOTS), cols[p]],
-            send_sem=cs.at[p, h, k, t], recv_sem=cr.at[p, h, k, t], device_id=(target,), device_id_type=MESH)
-
-    def serve(p, h, k):
-        block = block_of(p, h, k, y, x, c)
-        source = land[p, h, k]
-        ay, ax = across[p]
-        for t, expert in enumerate([in_plane(y, x, 1 - c), in_plane(ay, ax, c), in_plane(ay, ax, 1 - c), in_plane(y, x, c)]):
-            chosen = jnp.where(chosen_rows(slots_ref, block, expert), 1.0, 0.0).astype(BF16)
-            got = dims(chosen, source, 1, 0).astype(BF16)
-            if t < 3:
-                stage[p, h, k, t] = got
-                served(p, h, k, t).start()
-            else:
-                xi[pl.ds(pl.multiple_of(block * SLOTS, 16), SLOTS), cols[p]] = got
-
-    own = [pltpu.make_async_copy(x_ref.at[:, cols[p]], land.at[p, 0, 0], own_sem.at[p]) for p in range(2)]
-    for p in range(2):
-        own[p].start()
-    for d in (1, 3, 2):
-        for p in range(2):
-            to_z(p, d).start()
+    ag = Forth(x_ref, slots_ref, xi, scratch)
+    ag.start()
 
     def chip_of(u):
-        group, k = u // 4, order_of(lax.rem(u, 4))
-        dy, dx = lax.rem(group, 2), group // 2
-        zz = lax.rem(z + 4 - k, 4)
-        yy = jnp.where(dy == 1, 1 - y, y)
-        xx = jnp.where(dx == 1, 1 - x, x)
-        return (zz * 2 + yy) * 2 + xx
+        return ag.chip(lax.rem(u, 4), u // 4)
+
+    def at_chip(u):
+        return pl.ds(pl.multiple_of(chip_of(u) * 2 * SLOTS, 16), 2 * SLOTS)
 
     def load_up(u):
-        at = pl.ds(pl.multiple_of(chip_of(u) * 2 * rows, 16), 2 * rows)
-        return pltpu.make_async_copy(u_ref.at[at, :], ubuf.at[lax.rem(u, 2)], usem.at[lax.rem(u, 2)])
+        return pltpu.make_async_copy(ui_ref.at[at_chip(u), :], ubuf.at[lax.rem(u, 2)], usem.at[lax.rem(u, 2)])
 
     load_up(0).start()
     swap.start()
-    for p in range(2):
-        own[p].wait()
-        hop(p, 0).start()
-
-    def first_stage(i, _):
-        k = order_of(i)
-        for p in range(2):
-            @pl.when(i > 0)
-            def _(p=p):
-                to_z(p, k).wait_recv()
-                hop(p, k).start()
-            serve(p, 0, k)
-        return 0
-    lax.fori_loop(0, 4, first_stage, 0)
+    ag.one(0)
     swap.wait_recv()
 
     def store(n, buf, out, u):
-        at = pl.ds(pl.multiple_of(chip_of(u) * 2 * SLOTS, 16), 2 * SLOTS)
-        return pltpu.make_async_copy(buf.at[lax.rem(u, 2)], out.at[at, :], osem.at[n, lax.rem(u, 2)])
+        return pltpu.make_async_copy(buf.at[lax.rem(u, 2)], out.at[at_chip(u), :], osem.at[n, lax.rem(u, 2)])
 
     def stores(u):
-        return [store(0, ui_buf, ui_out, u), store(1, dx_buf, dx_out, u), store(2, y_buf, y_out, u)]
+        return [store(0, dx_buf, dx_out, u), store(1, y_buf, y_out, u)]
 
     def keep(u):
-        at = pl.ds(pl.multiple_of(chip_of(u) * 2 * SLOTS, 16), 2 * SLOTS)
-        return pltpu.make_async_copy(xi.at[at, :], xi_out.at[at, :], xsem.at[u])
-
-    def unit(u, _):
-        group, k = u // 4, order_of(lax.rem(u, 4))
+        return pltpu.make_async_copy(xi.at[at_chip(u), :], xi_out.at[at_chip(u), :], xsem.at[u])
+
+    def unit(u):
         slot = lax.rem(u, 2)
         chip = chip_of(u)
 
@@ -893,31 +1006,7 @@
         def _():
             load_up(u + 1).start()
 
-        @pl.when(group == 0)
-        def _():
-            for p in range(2):
-                hop(p, k).wait_recv()
-                serve(p, 1, k)
-            for p in range(2):
-                served(p, 0, k, 0).wait_recv()
-
-        @pl.when(group == 1)
-        def _():
-            served(0, 1, k, 0).wait_recv()
-            served(1, 0, k, 1).wait_recv()
-            served(1, 0, k, 2).wait_recv()
-
-        @pl.when(group == 2)
-        def _():
-            served(1, 1, k, 0).wait_recv()
-            served(0, 0, k, 1).wait_recv()
-            served(0, 0, k, 2).wait_recv()
-
-        @pl.when(group == 3)
-        def _():
-            for p in range(2):
-                served(p, 1, k, 1).wait_recv()
-                served(p, 1, k, 2).wait_recv()
+        ag.arrived(lax.rem(u, 4), u // 4)
 
         @pl.when(u >= 2)
         def _():
@@ -925,22 +1014,17 @@
                 s.wait()
 
         load_up(u).wait()
-        at = pl.ds(pl.multiple_of(chip * 2 * SLOTS, 16), 2 * SLOTS)
+        at = at_chip(u)
         expert = in_plane(y, x, c)
-        picks, gate, up_rows = [], [], []
+        picks, gate = [], []
         for core in range(2):
             block = chip * 2 + core
             hit = chosen_rows(slots_ref, block, expert)
             picks.append(hit)
             gate_row = jnp.concatenate([gates[block, 0:1, :], gates[block, 1:2, :]], axis=1)
             gate.append(jnp.sum(jnp.where(hit, gate_row, 0.0), axis=1, keepdims=True))
-            up_rows.append(
-                dims(jnp.where(hit, 1.0, 0.0).astype(BF16), ubuf[slot, core * rows : (core + 1) * rows, :], 1, 0).astype(BF16)
-            )
         gate_of_slot = jnp.concatenate(gate, axis=0)
-        ui = jnp.concatenate(up_rows, axis=0)
-        ui_buf[slot] = ui
-        hidden_up = dims(ui, wd_ref[...], 1, 1)
+        hidden_up = dims(ubuf[slot], wd_ref[...], 1, 1)
         rows_in = xi[at, :]
         gate_in = dims(rows_in, wg_ref[...], 1, 0)
         up_in = dims(rows_in, wu_ref[...], 1, 0)
@@ -965,9 +1049,24 @@
         for s in stores(u):
             s.start()
         keep(u).start()
+
+    def each(v, _):
+        i, group = v // 4, lax.rem(v, 4)
+
+        @pl.when((group == 0) & (i < 3))
+        def _():
+            ag.one(i + 1)
+
+        @pl.when((group == 0) & (i < 4))
+        def _():
+            ag.two(i)
+
+        @pl.when(v >= 4)
+        def _():
+            unit(v - 4)
         return 0
 
-    lax.fori_loop(0, 16, unit, 0)
+    lax.fori_loop(0, 20, each, 0)
     for u in (14, 15):
         for s in stores(u):
             s.wait()
@@ -976,26 +1075,13 @@
         keep(u).wait()
         return 0
     lax.fori_loop(0, 16, last, 0)
-
-    def sent(k, _):
-        for p in range(2):
-            hop(p, k).wait_send()
-
-            @pl.when(k > 0)
-            def _(p=p):
-                to_z(p, k).wait_send()
-            for h in range(2):
-                for t in range(3):
-                    served(p, h, k, t).wait_send()
-        return 0
-    lax.fori_loop(0, 4, sent, 0)
+    ag.sent()
     swap.wait_send()
 
 
-def run_experts(normed, gates, slots, upstream, gate_weight, up_weight, down_weight):
+def run_experts(normed, gates, slots, ui, gate_weight, up_weight, down_weight):
     rows, model = normed.shape
     ff = gate_weight.shape[1]
-    half = model // 2
     n = 32 * SLOTS
     hbm, vmem = pl.BlockSpec(memory_space=pl.ANY), pl.BlockSpec(memory_space=pltpu.VMEM)
     dma = pltpu.SemaphoreType.DMA
@@ -1004,23 +1090,19 @@
     return pl.pallas_call(
         experts_kernel,
         in_specs=[hbm, vmem, vmem, hbm, vmem, vmem, vmem],
-        out_specs=[hbm] * 4 + [vmem] * 4,
-        out_shape=[long] * 4 + [short] * 3 + [jax.ShapeDtypeStruct((32, 8, 128), F32)],
+        out_specs=[hbm] * 3 + [vmem] * 4,
+        out_shape=[long] * 3 + [short] * 3 + [jax.ShapeDtypeStruct((32, 8, 128), F32)],
         scratch_shapes=[
             pltpu.VMEM((32, 8, 128), F32),
-            pltpu.VMEM((2, 2, 4, rows, half), BF16),
-            pltpu.VMEM((2, 2, 4, 3, SLOTS, half), BF16),
             pltpu.VMEM((n, model), BF16),
-            pltpu.VMEM((2, 2 * rows, model), BF16),
             pltpu.VMEM((2, 2 * SLOTS, model), BF16),
             pltpu.VMEM((2, 2 * SLOTS, model), BF16),
             pltpu.VMEM((2, 2 * SLOTS, model), BF16),
-            dma((32,)), dma((32,)), dma((2, 4)), dma((2, 4)), dma((2, 4)), dma((2, 4)),
-            dma((2, 2, 4, 3)), dma((2, 2, 4, 3)), dma((2,)), dma((2,)), dma((16,)), dma((3, 2)),
-        ],
+            dma((32,)), dma((32,)), dma((2,)), dma((16,)), dma((2, 2)),
+        ] + Forth.scratch(rows, model // 2),
         compiler_params=pltpu.CompilerParams(collective_id=13, has_side_effects=True, vmem_limit_bytes=56 * 2**20),
         name="experts",
-    )(normed, gates, slots, upstream, gate_weight, up_weight, down_weight)
+    )(normed, gates, slots, ui, gate_weight, up_weight, down_weight)
 
 
 class Back:
@@ -1084,16 +1166,16 @@
             src_ref=self.zout.at[p, k], dst_ref=self.rz.at[p, k], send_sem=self.zs.at[p, k], recv_sem=self.zr.at[p, k],
             device_id=(target,), device_id_type=MESH)
 
+    def issue(self, h, i):
+        k = far_first(i)
+        for p in range(2):
+            for t in (1, 2, 0):
+                self.to(p, t, h, k).start()
+            self.mine(p, h, k).start()
+
     def start(self):
-        for h in (1, 0):
-            def one(i, _, h=h):
-                k = far_first(i)
-                for p in range(2):
-                    for t in (1, 2, 0):
-                        self.to(p, t, h, k).start()
-                    self.mine(p, h, k).start()
-                return 0
-            lax.fori_loop(0, 4, one, 0)
+        self.issue(1, 0)
+        self.issue(0, 0)
 
     def dense(self, p, h, k):
         self.mine(p, h, k).wait()
@@ -1110,15 +1192,21 @@
         return total
 
     def step(self, u):
-        k = far_first(lax.rem(u, 4))
-
-        @pl.when(u < 4)
+        i = u // 2
+        k = far_first(i)
+        early = lax.rem(u, 2) == 0
+
+        @pl.when(early)
         def _():
             for p in range(2):
                 self.sout[p, k] = self.dense(p, 1, k).astype(BF16)
                 self.second(p, k).start()
 
-        @pl.when(u >= 4)
+            @pl.when(i < 3)
+            def _():
+                self.issue(1, i + 1)
+
+        @pl.when(jnp.logical_not(early))
         def _():
             for p in range(2):
                 total = self.dense(p, 0, k)
@@ -1133,6 +1221,10 @@
                 @pl.when(k == 0)
                 def _(p=p, total=total):
                     self.o_ref[:, self.cols[p]] = total
+
+            @pl.when(i < 3)
+            def _():
+                self.issue(0, i + 1)
 
     def finish(self):
         for p in range(2):
@@ -1251,11 +1343,87 @@
     )(dx, slots, gg, xi, ui, hg, dg, du)
 
 
+def attend_mesh_kernel(
+    chunks, rows, lo_ref, q_ref, kv_ref, u_ref, mine_ref, o_ref, lse_ref, window, slots_ref, ui_ref,
+    bias, gs, gr, lsem, ws, wr, *scratch,
+):
+    greet_all()
+    swap = Swap(lambda t: mine_ref.at[t // 8], slots_ref, gs, gr)
+    keys = Window(rows, kv_ref, window, (lsem, ws, wr))
+    ag = Forth(u_ref, slots_ref, ui_ref, scratch)
+    keys.start()
+    swap.start()
+    ag.start()
+    make_bias(bias, lo_ref, chunks, rows)
+    keys.previous()
+    swap.wait_recv()
+    ag.one(0)
+    keys.pass_on()
+    ag.one(1)
+    keys.end()
+    width = 2 * GROUP * HEAD_DIM
+
+    def pair(j, _):
+        lanes = pl.ds(pl.multiple_of(j * 2 * HEAD_DIM, 2 * HEAD_DIM), 2 * HEAD_DIM)
+        head = pl.ds(pl.multiple_of(j * width, width), width)
+
+        def between(half):
+            u = 2 * j + half + 2
+
+            @pl.when((u == 3) | (u == 5))
+            def _():
+                ag.one((u + 1) // 2)
+
+            @pl.when((u == 2) | (u == 4) | (u == 6) | (u == 7))
+            def _():
+                ag.two(jnp.where(u == 7, 3, u // 2 - 1))
+
+        attend_pair(
+            chunks, rows, lax.rem(lax.axis_index("dev"), 2), q_ref.at[head, :], window.at[:, :, lanes],
+            o_ref.at[head, :], lse_ref.at[pl.ds(j, 1)], bias, between,
+        )
+        return 0
+
+    lax.fori_loop(0, KEY_HEADS // 2, pair, 0)
+
+    def last(u, _):
+        ag.arrived(lax.rem(u, 4), u // 4)
+        return 0
+    lax.fori_loop(0, 16, last, 0)
+    ag.sent()
+    keys.sent()
+    swap.wait_send()
+
+
+def attend_mesh(query_t, kv, lo, upstream, mine):
+    rows = query_t.shape[1]
+    chunks = 9
+    model = upstream.shape[1]
+    hbm, vmem = pl.BlockSpec(memory_space=pl.ANY), pl.BlockSpec(memory_space=pltpu.VMEM)
+    dma = pltpu.SemaphoreType.DMA
+    return pl.pallas_call(
+        functools.partial(attend_mesh_kernel, chunks, rows),
+        in_specs=[vmem] * 2 + [hbm, hbm, vmem],
+        out_specs=[vmem] * 4 + [hbm],
+        out_shape=[
+            jax.ShapeDtypeStruct(query_t.shape, BF16),
+            jax.ShapeDtypeStruct((KEY_HEADS // 2, 8, rows), F32),
+            jax.ShapeDtypeStruct((2, 10 * rows, kv.shape[2]), BF16),
+            jax.ShapeDtypeStruct((32, 8, rows), F32),
+            jax.ShapeDtypeStruct((32 * SLOTS, model), BF16),
+        ],
+        scratch_shapes=[pltpu.VMEM((chunks * rows, rows), F32), dma((32,)), dma((32,))]
+        + Window.scratch + Forth.scratch(rows, model // 2),
+        compiler_params=pltpu.CompilerParams(collective_id=16, has_side_effects=True, vmem_limit_bytes=56 * 2**20),
+        name="attend",
+    )(lo, query_t, kv, upstream, mine)
+
+
 def attend_back_mesh_kernel(
     chunks, rows, lo_ref, cos_ref, sin_ref, q_ref, kv_ref, g_ref, lse_ref, delta_ref, y_ref, slots_ref,
     dq_ref, dkv_ref, o_ref, bias, *scratch,
 ):
-    greet_all()
+    greet_near()
     rs = Back(y_ref, slots_ref, o_ref, scratch)
     rs.start()
     make_bias(bias, lo_ref, chunks, rows)
@@ -1316,9 +1484,10 @@
     return lax.all_gather(block, "dev", axis=0, tiled=True)
 
 
-def reduced(dense, cid, by_rows):
+def reduced(dense, more, cid):
     if meshed():
-        return reduce_all(dense, cid, by_rows)
+        return reduce_all(dense, more, cid)
+    dense = jnp.concatenate([dense, more], axis=1)
     return lax.psum_scatter(dense, "dev", scatter_dimension=0, tiled=True).astype(F32)
 
 
@@ -1345,7 +1514,6 @@
     capacity = split * ((9 * rows * TOP + 8 * EXPERTS * split - 1) // (8 * EXPERTS * split))
     weight_rows = query_weight.shape[0]
 
-    all_upstream = lax.all_gather(cotangent, "dev", axis=0, tiled=True)
     output_matrix = lax.all_gather(output_weight, "dev", axis=0, tiled=True)
 
     extra = jnp.concatenate([router_weight, first_gain[:, None], second_gain[:, None]], axis=1)
@@ -1379,9 +1547,15 @@
     query_t = rotate_t(qkv_t[:q_width], cos_t, sin_t).astype(BF16) * BF16(HEAD_DIM**-0.5)
     key = rotate_t(qkv_t[q_width : q_width + k_width], cos_t, sin_t).astype(BF16).T
     value = qkv_t[q_width + k_width :].astype(BF16).T
-    window, offset, plane_slots = window_of(jnp.stack([key, value]), slot_rows.reshape(-1, 8, rows))
+    kv = jnp.stack([key, value])
     lo = (jnp.arange(rows, dtype=jnp.int32) - positions)[None, :]
-    attended_t, lse = attend(query_t, window, offset, lo)
+    if meshed():
+        attended_t, lse, window, plane_slots, expert_up = attend_mesh(
+            query_t, kv, lo, cotangent, slot_rows.reshape(-1, 8, rows)
+        )
+    else:
+        window, offset = window_of(kv), jnp.int32(0)
+        attended_t, lse = attend(query_t, window, offset, lo)
     residual = inputs + dims(attended_t, output_matrix, 0, 0)
     scale_two = rms_scale(residual)
     normed_two = (residual * scale_two * gain_second).astype(BF16)
@@ -1393,8 +1567,8 @@
 
     if meshed():
         gate_rows = jnp.pad(gates.T.reshape(EXPERTS, rows // 128, 128), ((0, 0), (0, 8 - rows // 128), (0, 0)))
-        expert_in, expert_up, grad_rows, out_rows, gated_hidden, gate_in_grad, up_in_grad, gate_grad_rows = run_experts(
-            normed_two, gate_rows, plane_slots, all_upstream, gate_weight, up_weight, down_weight
+        expert_in, grad_rows, out_rows, gated_hidden, gate_in_grad, up_in_grad, gate_grad_rows = run_experts(
+            normed_two, gate_rows, plane_slots, expert_up, gate_weight, up_weight, down_weight
         )
         returned_grad, gate_grad, gate_gradient, up_gradient, down_gradient = run_grads(
             grad_rows, plane_slots, gate_grad_rows, expert_in, expert_up, gated_hidden, gate_in_grad, up_in_grad
@@ -1410,6 +1584,7 @@
             slot.reshape(devices // 2, 2, rows) + jnp.array([[0], [capacity]], F32),
             -1.0,
         ).astype(jnp.int32).reshape(devices // 2, 1, 2 * rows)
+        all_upstream = lax.all_gather(cotangent, "dev", axis=0, tiled=True)
         all_normed = lax.all_gather(normed_two, "dev", axis=0, tiled=True)
         expert_in, expert_up = dispatch(pair_slot, all_normed, all_upstream, 2 * capacity)
         slot_hit = slot[:, None, :] == jnp.arange(capacity, dtype=F32)[None, :, None]
@@ -1476,12 +1651,13 @@
         + scale_one * weighted_one
         - inputs * scale_one**3 * jnp.mean(weighted_one * inputs, axis=-1, keepdims=True)
     )
-    terms = jnp.concatenate(
-        [qkv_gradient, router_gradient, first_gain_grad[:, None], second_gain_grad[:, None],
-         jnp.zeros((model, (-(QKV + EXPERTS + 2)) % 256), F32)],
+    terms = qkv_gradient.astype(BF16)
+    more = jnp.concatenate(
+        [router_gradient, first_gain_grad[:, None], second_gain_grad[:, None],
+         jnp.zeros((model, (-(EXPERTS + 2)) % 256), F32)],
         axis=1,
     ).astype(BF16)
-    sums = reduced(terms, 4, False)
+    sums = reduced(terms, more, 4)
     return (
         layer_output,
         tokens_gradient,

time: 867 us -> 724 us (0.84)
  Pallas kernels: 716 us -> 615 us
  waiting for transfers between devices: 26.8 us -> 0.72 us
  local copies, waits for them, and re-layouts: 52.9 us -> 32.6 us
    pallas_call x1, Pallas kernels: 150 us -> 118 us  [attend_back_mesh(): pl.pallas_call(functools.partial(attend_back_mesh_kernel, chunks, rows),...]
    pallas_call x1, Pallas kernels: 132 us -> 101 us  [run_grads(): pl.pallas_call(grads_kernel, in_specs=[hbm, vmem, vmem, hbm, hbm, vmem, v...]
    all_gather x1 -> x0, waiting for transfers between devices: 25.4 us -> none  [on_device(): all_upstream = lax.all_gather(cotangent, 'dev', axis=0, tiled=True)]
    pallas_call x1, Pallas kernels: 137 us -> 114 us  [run_experts(): pl.pallas_call(experts_kernel, in_specs=[hbm, vmem, vmem, hbm, vmem, vmem...]
    pallas_call x2 -> x1, Pallas kernels: 142 us -> 125 us  [attend_mesh(): pl.pallas_call(functools.partial(attend_mesh_kernel, chunks, rows), in_sp...]
    concatenate x1, local copies, waits for them, and re-layouts: 14.2 us -> 0.08 us  [on_device(): jnp.concatenate([router_gradient, first_gain_grad[:, None], second_gain_g...]
    unnamed x48 -> x44, local copies, waits for them, and re-layouts: 19.6 us -> 14.9 us
  transfers between devices with their start and end apart: 3 -> 2, of which waited for: 1 -> 0; matrix products, arithmetic and copies ran while one was open for 9% -> 8% of each run, Pallas kernels for 52% -> 56%
where the time goes in v3:
time: 724 us; the launch traced here: 719 us
  Pallas kernels  615 us (85%)
  matrix products  36.4 us (5%)
  local copies, waits for them, and re-layouts  32.6 us (5%)
  other arithmetic  19 us (3%)
  between operations  14.7 us (2%)
    pallas_call x1, Pallas kernels, attend_mesh(): pl.pallas_call(functools.partial(attend_mesh_kernel, chunks, rows), in_sp...  125 us
    pallas_call x1, Pallas kernels, attend_back_mesh(): pl.pallas_call(functools.partial(attend_back_mesh_kernel, chunks, rows),...  118 us
    pallas_call x1, Pallas kernels, run_experts(): pl.pallas_call(experts_kernel, in_specs=[hbm, vmem, vmem, hbm, vmem, vmem...  114 us
    pallas_call x1, Pallas kernels, run_grads(): pl.pallas_call(grads_kernel, in_specs=[hbm, vmem, vmem, hbm, hbm, vmem, v...  101 us
    pallas_call x1, Pallas kernels, reduce_all(): pl.pallas_call(functools.partial(reduce_kernel, rows, cols, pieces), out_...  58.5 us
    pallas_call x1, Pallas kernels, gather_all(): pl.pallas_call(functools.partial(gather_kernel, rows, pieces), out_shape=...  54.7 us
    pallas_call x1, Pallas kernels, unwindow(): pl.pallas_call(functools.partial(unwindow_kernel, rows), out_shape=jax.Sh...  42.9 us
    dot_general x9, matrix products, dims(): lax.dot_general(a, b, (((ca,), (cb,)), ((), ())), preferred_element_type=...  36.4 us
  transfers between devices with their start and end apart: 2, of which 0 were waited for; matrix products, arithmetic and copies ran while one was open for 8% of the time, Pallas kernels for 56%

profile of v3, /device:TPU:0, one launch (start us, length us, event | category | flops | bytes accessed | tf_op | source)
XLA Modules:
  0.0 718.7 jit_solution(3520780323772932937)
XLA Ops:
  7.2 0.7 all-gather.2.cloned.1.call-update
  8.0 0.8 copy.69
  8.7 0.8 copy.70
  9.5 0.8 copy.71
  10.3 1.7 concatenate.10.x_ref
  12.0 54.7 %gather_all.1 = bf16[1536,2688]{1,0:T(8,128)(2,1)} custom-call(bf16[48,2688]{1,0:T(8,128)(2,1)} %concatenate.10.x_ref), custom_call_target="tpu_custom_call" | custom-call | tf_op jit(solution)/shard_map/gather_all/pallas_call | solution.py:111
  66.7 1.7 convert_reduce_fusion.1
  68.4 0.2 fusion.5
  68.7 5.7 fusion.2
  74.5 1.4 copy-done.7
  75.9 0.6 fusion.37
  76.5 0.2 fusion.33
  76.7 0.1 subtract_convert_fusion.2
  76.8 0.1 copy.72
  77.0 0.1 copy.82
  77.2 0.8 pad_maximum_fusion.3.kv_ref
  78.1 0.1 slice-done
  78.1 0.2 subtract_convert_fusion
  78.4 1.0 maximum_multiply_fusion
  79.4 2.8 convert_reduce_fusion
  82.2 0.6 convert_bitcast_fusion.1.mine_ref
  82.8 125.0 %attend.1 = (bf16[1536,256]{1,0:T(8,128)(2,1)}, f32[4,8,256]{2,1,0:T(8,128)}, bf16[2,2560,512]{2,1,0:T(8,128)(2,1)}, f32[32,8,256]{2,1,0:T(8,128)}, bf16[2560,1536]{1,0:T(8,128)(2,1)}) custom-call(s32[1,256]{1,0:T(1,128)} %bitcast.92, bf16[1536,256]{1,0:T(8,128)(2,1)} %bitcast.79, bf16[2,256,512]{2,1,0:T(8,128)(2,1)} %pad_maximum_fusion.3.kv_ref, ...), custom_call_target="tpu_custom_call" | custom-call | tf_op jit(solution)/shard_map/attend/pallas_call | solution.py:1404
  207.9 4.1 multiply_reduce_fusion.2
  211.9 0.2 multiply_convert_fusion.x_ref
  212.2 1.6 fusion.32
  213.9 0.7 pad.8.gates_ref
  214.6 114.4 %experts.1 = (bf16[2560,1536]{1,0:T(8,128)(2,1)}, bf16[2560,1536]{1,0:T(8,128)(2,1)}, bf16[2560,1536]{1,0:T(8,128)(2,1)}, bf16[2560,512]{1,0:T(8,128)(2,1)}, bf1...) custom-call(bf16[256,1536]{1,0:T(8,128)(2,1)} %copy-done.5, f32[32,8,128]{2,1,0:T(8,128)} %pad.8.gates_ref, ...), custom_call_target="tpu_custom_call" | custom-call | tf_op jit(solution)/shard_map/experts/pallas_call | solution.py:1090
  329.0 101.3 %grads.1 = (f32[256,1536]{1,0:T(8,128)}, f32[32,8,128]{2,1,0:T(8,128)}, f32[1536,512]{1,0:T(8,128)}, f32[1536,512]{1,0:T(8,128)}, f32[512,1536]{1,0:T(8,128)}) custom-call(bf16[2560,1536]{1,0:T(8,128)(2,1)} %get-tuple-element.36.dx_ref, f32[32,8,256]{2,1,0:T(8,128)} %get-tuple-element.34.slots_ref, f32[32,8,128]{2,1,0:T(8,128)} %get-tuple-element.37.gg_ref, ...), custom_call_target="tpu_custom_call" | custom-call | tf_op jit(solution)/shard_map/grads/pallas_call | solution.py:1325
  430.3 0.9 slice.72
  431.3 2.3 multiply_reduce_fusion
  433.6 0.5 multiply_subtract_fusion
  434.1 0.7 copy-done.6
  434.7 3.6 convolution_convert_fusion.1
  438.3 0.1 pad.13.clone
  438.4 1.4 convolution_convert_fusion.3
  439.8 0.9 copy.77
  440.7 5.5 convert_multiply_fusion.5
  446.2 1.6 reduce_sum.109
  447.8 0.6 pad.9.delta_ref
  448.4 118.2 %attend_back.1 = (bf16[1536,256]{1,0:T(8,128)(2,1)}, bf16[2,2560,512]{2,1,0:T(8,128)(2,1)}, f32[256,1536]{1,0:T(8,128)}) custom-call(s32[1,256]{1,0:T(1,128)} %bitcast.93, f32[32,256]{1,0:T(8,128)} %copy-done.12, f32[32,256]{1,0:T(8,128)} %copy-done.15, bf16[1536,256]{1,0:T(8,128)(2,1)} %bitcast.80, bf16[2,2560,512]{2,1,0:T(8,128)(2,1)} %get-tuple-element.33.kv_ref, ...), custom_call_target="tpu_custom_call" | custom-call | tf_op jit(solution)/shard_map/attend_back/pallas_call | solution.py:1454
  566.6 2.5 copy-done
  569.1 42.9 %unwindow.1 = f32[2,256,512]{2,1,0:T(8,128)S(1)} custom-call(bf16[2,2560,512]{2,1,0:T(8,128)(2,1)S(1)} %copy-done), custom_call_target="tpu_custom_call" | custom-call | tf_op jit(solution)/shard_map/unwindow/pallas_call | solution.py:483
  612.1 0.8 slice_bitcast_fusion
  612.9 2.1 copy.75
  615.0 0.7 fusion.18
  615.8 1.2 copy.76
  616.9 1.1 subtract_convert_fusion.1
  618.1 6.8 fusion.12
  624.9 0.3 broadcast_in_dim.92
  625.1 0.3 broadcast_in_dim.93
  625.4 5.5 convolution_convert_fusion.g_ref
  631.0 1.6 maximum_maximum_fusion.more_ref
  632.5 58.5 %reduce_all.1 = f32[48,2816]{1,0:T(8,128)} custom-call(bf16[1536,2560]{1,0:T(8,128)(2,1)} %convolution_convert_fusion.g_ref, bf16[1536,256]{1,0:T(8,128)(2,1)} %maximum_maximum_fusion.more_ref), custom_call_target="tpu_custom_call" | custom-call | tf_op jit(solution)/shard_map/reduce_all/pallas_call | solution.py:247
  691.0 1.7 slice.76
  692.7 0.7 slice.80
  693.5 0.7 copy.80
  694.2 1.5 slice_reduce_fusion
  695.7 1.6 fusion.36
  697.3 4.0 fusion.9
  701.3 1.6 convert_element_type.117
  702.9 4.0 copy.89
  706.9 1.7 copy.90
  708.6 1.4 copy-done.8
  710.0 1.7 copy.91
  (60 shorter events, 0.6 us)
Async XLA Ops:
  7.2 200.7 %all-gather.2.cloned.1.call-start = ((), (), s32[]{:S(2)}) async-start(), calls=%async_computation.1 | async-start | bytes 4866048 | tf_op jit(solution)/shard_map/all_gather | solution.py:1517
  7.9 693.4 %reduce-scatter.2.cloned.1.call-start = ((), (), s32[]{:S(2)}) async-start(), calls=%async_computation.2 | async-start | bytes 4866048 | tf_op jit(solution)/shard_map/reduce_scatter | solution.py:1630
  12.0 56.4 %copy-start.3 = (bf16[256,1536]{1,0:T(8,128)(2,1)S(1)}, bf16[256,1536]{1,0:T(8,128)(2,1)}, u32[]{:S(2)}) copy-start(bf16[256,1536]{1,0:T(8,128)(2,1)} %param.15) | copy-start | bytes 2359300
  74.4 1.5 copy-start.7
  74.5 1.4 copy-start.18
  75.9 1.2 copy-start.16
  75.9 1.3 copy-start.17
  76.7 1.4 copy-start.12
  76.7 1.4 copy-start.15
  76.7 1.4 slice-start
  212.2 2.4 copy-start.5
  431.3 2.3 copy-start.10
  433.6 1.1 copy-start.6
  434.7 6.0 copy-start.1
  566.6 2.5 copy-start
  612.1 4.9 copy-start.13
  612.9 5.2 copy-start.4
  615.7 2.3 copy-start.14
  625.4 5.6 copy-start.11
  632.5 64.8 %copy-start.2 = (f32[256,1536]{1,0:T(8,128)S(1)}, f32[256,1536]{1,0:T(8,128)}, u32[]{:S(2)}) copy-start(f32[256,1536]{1,0:T(8,128)} %copy-done.1) | copy-start | bytes 4718596
  702.9 4.0 copy-start.9
  706.9 3.0 copy-start.8
Sparse Core Ops, SparseCore 0:
  10.9 77.5 all-gather.1
  438.5 138.3 reduce-scatter.1

commit v4 on v3

--- a/solution.py
+++ b/solution.py
@@ -119,149 +119,6 @@
     )(block)
 
 
-def reduce_kernel(rows, cols, pieces, g_ref, more_ref, o_ref, acc, own, ra, rb, rz, own_sem, ssem, rsem, sa, ra_sem, sb, rb_sem, sz, rz_sem):
-    z, y, x, c = place()
-    greet(partners_of(z, y, x, c))
-    sibling = number(z, y, x, 1 - c)
-    around = (number(z, y, 1 - x, c), number(z, 1 - y, x, c))
-    blocks = [(dy, dx, k) for dy, dx in ((1, 1), (1, 0), (0, 1), (0, 0)) for k in (2, 1, 3, 0)]
-
-    def where(dy, dx, k):
-        return lax.rem(z + k, 4), (1 - y) if dy else y, (1 - x) if dx else x
-
-    def lane(dy, dx, k):
-        zz, yy, xx = where(dy, dx, k)
-        return (zz * 2 + yy) * 2 + xx
-
-    main = g_ref.shape[1]
-    sides = ((g_ref, pl.ds(0, main)), (more_ref, pl.ds(main, cols - main)))
-
-    def chip_rows(ref, dy, dx, k, core):
-        zz, yy, xx = where(dy, dx, k)
-        return ref.at[pl.ds(pl.multiple_of(number(zz, yy, xx, core) * rows, 16), rows), :]
-
-    def to_sibling(n):
-        return [
-            pltpu.make_async_remote_copy(
-                src_ref=chip_rows(ref, *blocks[n], 1 - c), dst_ref=acc.at[lane(*blocks[n]), :, at],
-                send_sem=ssem.at[n, i], recv_sem=rsem.at[n, i], device_id=(sibling,), device_id_type=MESH)
-            for i, (ref, at) in enumerate(sides)
-        ]
-
-    def load(n):
-        return [
-            pltpu.make_async_copy(chip_rows(ref, *blocks[n], c), own.at[n % 2, :, at], own_sem.at[n % 2, i])
-            for i, (ref, at) in enumerate(sides)
-        ]
-
-    def part(ref, p):
-        r0, nr, c0, nc = pieces[p]
-        return ref.at[pl.ds(r0, nr), pl.ds(c0, nc)]
-
-    def first(p, d2, k, dy, dx):
-        return pltpu.make_async_remote_copy(
-            src_ref=part(acc.at[lane(dy, dx, k)], p), dst_ref=ra.at[p, d2, k],
-            send_sem=sa.at[p, d2, k], recv_sem=ra_sem.at[p, d2, k], device_id=(around[p],), device_id_type=MESH)
-
-    def second(p, k):
-        dy, dx = (1, 0) if p == 0 else (0, 1)
-        return pltpu.make_async_remote_copy(
-            src_ref=part(acc.at[lane(dy, dx, k)], p), dst_ref=rb.at[p, k],
-            send_sem=sb.at[p, k], recv_sem=rb_sem.at[p, k], device_id=(around[1 - p],), device_id_type=MESH)
-
-    def third(p, k):
-        return pltpu.make_async_remote_copy(
-            src_ref=part(acc.at[lane(0, 0, k)], p), dst_ref=rz.at[p, k - 1],
-            send_sem=sz.at[p, k - 1], recv_sem=rz_sem.at[p, k - 1],
-            device_id=(number(lax.rem(z + k, 4), y, x, c),), device_id_type=MESH)
-
-    step = 16
-
-    def add(out, terms, nr):
-        def chunk(i, _):
-            at = pl.ds(pl.multiple_of(i * step, step), step)
-            total = terms[0][at, :].astype(jnp.float32)
-            for t in terms[1:]:
-                total = total + t[at, :].astype(jnp.float32)
-            out[at, :] = total.astype(out.dtype)
-            return 0
-        lax.fori_loop(0, nr // step, chunk, 0)
-
-    for n in range(16):
-        for cp in to_sibling(n):
-            cp.start()
-    for cp in load(0):
-        cp.start()
-    for n in range(16):
-        dy, dx, k = blocks[n]
-        if n + 1 < 16:
-            for cp in load(n + 1):
-                cp.start()
-        for cp in load(n):
-            cp.wait()
-        for cp in to_sibling(n):
-            cp.wait_recv()
-        block = acc.at[lane(dy, dx, k)]
-        add(block, [block, own.at[n % 2]], rows)
-        if dx:
-            first(0, dy, k, dy, dx).start()
-        if dy:
-            first(1, dx, k, dy, dx).start()
-    for k in (2, 1, 3, 0):
-        for p in range(2):
-            dy, dx = (1, 0) if p == 0 else (0, 1)
-            first(p, 1, k, 1, 1).wait_recv()
-            block = part(acc.at[lane(dy, dx, k)], p)
-            add(block, [block, ra.at[p, 1, k]], pieces[p][1])
-            second(p, k).start()
-    for k in (2, 1, 3, 0):
-        for p in range(2):
-            first(p, 0, k, 1 - p, p).wait_recv()
-            second(p, k).wait_recv()
-            block = part(acc.at[lane(0, 0, k)], p)
-            if k:
-                add(block, [block, ra.at[p, 0, k], rb.at[p, k]], pieces[p][1])
-                third(p, k).start()
-    for p in range(2):
-        for k in range(1, 4):
-            third(p, k).wait_recv()
-        block = part(acc.at[lane(0, 0, 0)], p)
-        add(part(o_ref, p), [block, ra.at[p, 0, 0], rb.at[p, 0]] + [rz.at[p, j] for j in range(3)], pieces[p][1])
-    for n in range(16):
-        for cp in to_sibling(n):
-            cp.wait_send()
-    for p in range(2):
-        for k in range(4):
-            first(p, 0, k, 1 - p, p).wait_send()
-            first(p, 1, k, 1, 1).wait_send()
-            second(p, k).wait_send()
-            if k:
-                third(p, k).wait_send()
-
-
-def reduce_all(dense, more, cid):
-    rows, cols = dense.shape[0] // 32, dense.shape[1] + more.shape[1]
-    half = cols // 2
-    pieces = ((0, rows, 0, half), (0, rows, half, half))
-    dma = pltpu.SemaphoreType.DMA
-    return pl.pallas_call(
-        functools.partial(reduce_kernel, rows, cols, pieces),
-        out_shape=jax.ShapeDtypeStruct((rows, cols), jnp.float32),
-        in_specs=[pl.BlockSpec(memory_space=pl.ANY)] * 2,
-        out_specs=pl.BlockSpec(memory_space=pltpu.VMEM),
-        scratch_shapes=[
-            pltpu.VMEM((16, rows, cols), dense.dtype),
-            pltpu.VMEM((2, rows, cols), dense.dtype),
-            pltpu.VMEM((2, 2, 4, rows, half), dense.dtype),
-            pltpu.VMEM((2, 4, rows, half), dense.dtype),
-            pltpu.VMEM((2, 3, rows, half), dense.dtype),
-            dma((2, 2)), dma((16, 2)), dma((16, 2)), dma((2, 2, 4)), dma((2, 2, 4)), dma((2, 4)), dma((2, 4)), dma((2, 3)), dma((2, 3)),
-        ],
-        compiler_params=pltpu.CompilerParams(collective_id=cid, has_side_effects=True, vmem_limit_bytes=56 * 2**20),
-        name="reduce_all",
-    )(dense, more)
-
-
 from jax.sharding import PartitionSpec as P
 
 QUERY_HEADS = 24
@@ -380,121 +237,114 @@
     return jnp.concatenate(parts + [kv, jnp.zeros_like(kv)], axis=1)
 
 
-def unwindow_kernel(rows, g_ref, o_ref, mine, got, near_got, far, lsem, ss, rs):
-    z, y, x, c = place()
-    p = y * 2 + x
-    sibling = number(z, y, x, 1 - c)
-    up = number(lax.rem(z + 1, 4), y, x, c)
-    down = number(lax.rem(z + 3, 4), y, x, c)
-
-    def chip(q):
-        return (z * 4 + q) * 2 + c
-
-    ahead = [chip(lax.rem(p + d, 4)) for d in (1, 2, 3)]
-    behind = [chip(lax.rem(p + 4 - d, 4)) for d in (1, 2, 3)]
-    greet([sibling, up, down] + ahead)
-
-    def slot(s, core):
-        return g_ref.at[:, pl.ds(pl.multiple_of((2 * s + core) * rows, 16), rows), :]
-
-    def to_sibling(s):
+class Unwindow:
+    @staticmethod
+    def scratch(rows, width):
+        return [
+            pltpu.VMEM((5, 2, rows, width), BF16),
+            pltpu.VMEM((3, 2, rows, width), BF16),
+            pltpu.VMEM((2, rows, width), BF16),
+            pltpu.SemaphoreType.DMA((9,)), pltpu.SemaphoreType.DMA((9,)),
+        ]
+
+    n_scratch = 5
+    order = (3, 1, 2, 0, 4)
+
+    def __init__(self, rows, grads, o_ref, scratch):
+        self.rows, self.grads, self.o_ref = rows, grads, o_ref
+        self.got, self.near_got, self.far, self.ss, self.rs = scratch
+        self.z, self.y, self.x, self.c = place()
+        self.p = self.y * 2 + self.x
+        self.sibling = number(self.z, self.y, self.x, 1 - self.c)
+        self.to_down = pltpu.make_async_remote_copy(
+            src_ref=self.got.at[0], dst_ref=self.far, send_sem=self.ss.at[8], recv_sem=self.rs.at[8],
+            device_id=(number(lax.rem(self.z + 3, 4), self.y, self.x, self.c),), device_id_type=MESH)
+
+    def to_sibling(self, s):
+        at = pl.ds(pl.multiple_of((2 * s + 1 - self.c) * self.rows, 16), self.rows)
         return pltpu.make_async_remote_copy(
-            src_ref=slot(s, 1 - c), dst_ref=got.at[s], send_sem=ss.at[s], recv_sem=rs.at[s],
-            device_id=(sibling,), device_id_type=MESH)
-
-    def load(s):
-        return pltpu.make_async_copy(slot(s, c), mine.at[s], lsem.at[s])
-
-    def to_owner(d):
+            src_ref=self.grads.at[:, at, :], dst_ref=self.got.at[s], send_sem=self.ss.at[s], recv_sem=self.rs.at[s],
+            device_id=(self.sibling,), device_id_type=MESH)
+
+    def to_owner(self, d):
+        owner = (self.z * 4 + lax.rem(self.p + 4 - d, 4)) * 2 + self.c
         return pltpu.make_async_remote_copy(
-            src_ref=got.at[4 - d], dst_ref=near_got.at[d - 1], send_sem=ss.at[4 + d], recv_sem=rs.at[4 + d],
-            device_id=(behind[d - 1],), device_id_type=MESH)
-
-    to_down = pltpu.make_async_remote_copy(
-        src_ref=got.at[0], dst_ref=far, send_sem=ss.at[8], recv_sem=rs.at[8],
-        device_id=(down,), device_id_type=MESH)
-    order = (3, 1, 2, 0, 4)
-    for s in order:
-        to_sibling(s).start()
-        load(s).start()
-
-    def rowwise(body):
+            src_ref=self.got.at[4 - d], dst_ref=self.near_got.at[d - 1], send_sem=self.ss.at[4 + d], recv_sem=self.rs.at[4 + d],
+            device_id=(owner,), device_id_type=MESH)
+
+    def rowwise(self, body):
         for h in range(2):
             def step(i, _, h=h):
-                body(h, pl.ds(pl.multiple_of(i * 32, 32), 32))
+                body(h, pl.multiple_of(i * 32, 32))
                 return 0
-            lax.fori_loop(0, rows // 32, step, 0)
-
-    for s in order:
-        load(s).wait()
-        to_sibling(s).wait_recv()
-
-        def both(h, at, s=s):
-            total = got[s, h, at, :].astype(F32) + mine[s, h, at, :].astype(F32)
-            if s == 4:
-                o_ref[h, at, :] = total
-            else:
-                got[s, h, at, :] = total.astype(BF16)
-        rowwise(both)
-        if 0 < s < 4:
-            to_owner(4 - s).start()
-    for d in (1, 3, 2):
-        to_owner(d).wait_recv()
-
-        @pl.when(p + d < 4)
-        def _(d=d):
-            def body(h, at):
-                o_ref[h, at, :] += near_got[d - 1, h, at, :].astype(F32)
-            rowwise(body)
-
-        @pl.when(p + d >= 4)
-        def _(d=d):
-            def body(h, at):
-                total = got[0, h, at, :].astype(F32) + near_got[d - 1, h, at, :].astype(F32)
-                got[0, h, at, :] = total.astype(BF16)
-            rowwise(body)
-
-    @pl.when(z > 0)
-    def _():
-        to_down.start()
-
-    @pl.when(z < 3)
-    def _():
-        to_down.wait_recv()
-
-        def body(h, at):
-            o_ref[h, at, :] += far[h, at, :].astype(F32)
-        rowwise(body)
-
-    @pl.when(z > 0)
-    def _():
-        to_down.wait_send()
-
-    for s in range(5):
-        to_sibling(s).wait_send()
-    for d in (1, 2, 3):
-        to_owner(d).wait_send()
+            lax.fori_loop(0, self.rows // 32, step, 0)
+
+    def start(self):
+        for s in self.order:
+            self.to_sibling(s).start()
+
+    def sums(self):
+        for s in self.order:
+            self.to_sibling(s).wait_recv()
+            first = (2 * s + self.c) * self.rows
+
+            def both(h, r, s=s, first=first):
+                at = pl.ds(r, 32)
+                mine = self.grads[h, pl.ds(pl.multiple_of(first + r, 32), 32), :]
+                total = self.got[s, h, at, :].astype(F32) + mine.astype(F32)
+                if s == 4:
+                    self.o_ref[h, at, :] = total
+                else:
+                    self.got[s, h, at, :] = total.astype(BF16)
+            self.rowwise(both)
+            if 0 < s < 4:
+                self.to_owner(4 - s).start()
+
+    def near(self):
+        for d in (1, 3, 2):
+            self.to_owner(d).wait_recv()
+
+            @pl.when(self.p + d < 4)
+            def _(d=d):
+                def body(h, r):
+                    at = pl.ds(r, 32)
+                    self.o_ref[h, at, :] += self.near_got[d - 1, h, at, :].astype(F32)
+                self.rowwise(body)
+
+            @pl.when(self.p + d >= 4)
+            def _(d=d):
+                def body(h, r):
+                    at = pl.ds(r, 32)
+                    total = self.got[0, h, at, :].astype(F32) + self.near_got[d - 1, h, at, :].astype(F32)
+                    self.got[0, h, at, :] = total.astype(BF16)
+                self.rowwise(body)
+
+        @pl.when(self.z > 0)
+        def _():
+            self.to_down.start()
+
+    def end(self):
+        @pl.when(self.z < 3)
+        def _():
+            self.to_down.wait_recv()
+
+            def body(h, r):
+                at = pl.ds(r, 32)
+                self.o_ref[h, at, :] += self.far[h, at, :].astype(F32)
+            self.rowwise(body)
+
+        @pl.when(self.z > 0)
+        def _():
+            self.to_down.wait_send()
+
+        for s in range(5):
+            self.to_sibling(s).wait_send()
+        for d in (1, 2, 3):
+            self.to_owner(d).wait_send()
 
 
 def unwindow(grads):
-    rows, width = grads.shape[1] // 10, grads.shape[2]
-    if meshed():
-        dma = pltpu.SemaphoreType.DMA
-        return pl.pallas_call(
-            functools.partial(unwindow_kernel, rows),
-            out_shape=jax.ShapeDtypeStruct((2, rows, width), F32),
-            in_specs=[pl.BlockSpec(memory_space=pl.ANY)],
-            out_specs=pl.BlockSpec(memory_space=pltpu.VMEM),
-            scratch_shapes=[
-                pltpu.VMEM((5, 2, rows, width), BF16),
-                pltpu.VMEM((5, 2, rows, width), BF16),
-                pltpu.VMEM((3, 2, rows, width), BF16),
-                pltpu.VMEM((2, rows, width), BF16),
-                dma((5,)), dma((9,)), dma((9,)),
-            ],
-            compiler_params=pltpu.CompilerParams(collective_id=12, has_side_effects=True, vmem_limit_bytes=40 * 2**20),
-            name="unwindow",
-        )(grads)
+    rows = grads.shape[1] // 10
     devices = lax.axis_size("dev")
     back = (MAXDOC + rows - 2) // rows
     total = grads[:, back * rows : (back + 1) * rows].astype(F32)
@@ -568,14 +418,16 @@
 
 
 def attend_back_pair(
-    chunks, rows, off, cos_ref, sin_ref, q_ref, kv_ref, g_ref, lse_ref, delta_ref, dq_ref, dkv_ref, bias, between
+    chunks, rows, off, cos_ref, sin_ref, q_ref, kv_ref, g_ref, lse_ref, out_ref, dq_ref, dkv_ref, bias, between
 ):
     unused = pl.ds(pl.multiple_of((1 - off) * chunks * rows, rows), rows)
     dkv_ref[:, unused, :] = jnp.zeros((2, rows, 2 * HEAD_DIM), BF16)
     for half in range(2):
         lanes = slice(half * HEAD_DIM, (half + 1) * HEAD_DIM)
         queries, grads = side_by_side(q_ref, half), side_by_side(g_ref, half)
-        lse, delta = stats_of(lse_ref, half), stats_of(delta_ref, half)
+        lse = stats_of(lse_ref, half)
+        mixed = side_by_side(out_ref, half).astype(F32)
+        delta = jnp.sum(mixed * grads.astype(F32), axis=0, keepdims=True)
 
         def chunk(ch, query_grad, lanes=lanes, queries=queries, grads=grads, lse=lse, delta=delta):
             at = pl.ds(pl.multiple_of((ch + off) * rows, rows), rows)
@@ -601,14 +453,14 @@
 
 
 def attend_back_kernel(
-    chunks, rows, off_ref, lo_ref, cos_ref, sin_ref, q_ref, kv_ref, g_ref, lse_ref, delta_ref, dq_ref, dkv_ref, bias
+    chunks, rows, off_ref, lo_ref, cos_ref, sin_ref, q_ref, kv_ref, g_ref, lse_ref, out_ref, dq_ref, dkv_ref, bias
 ):
     @pl.when(pl.program_id(0) == 0)
     def _():
         make_bias(bias, lo_ref, chunks, rows)
 
     attend_back_pair(
-        chunks, rows, off_ref[0], cos_ref, sin_ref, q_ref, kv_ref, g_ref, lse_ref, delta_ref, dq_ref, dkv_ref, bias,
+        chunks, rows, off_ref[0], cos_ref, sin_ref, q_ref, kv_ref, g_ref, lse_ref, out_ref, dq_ref, dkv_ref, bias,
         lambda half: None,
     )
 
@@ -645,14 +497,14 @@
     )(offset.reshape(1), lo, query_t, window)
 
 
-def attend_back(query_t, window, offset, lo, grad_t, lse, delta, cos_t, sin_t):
+def attend_back(query_t, window, offset, lo, grad_t, lse, attended_t, cos_t, sin_t):
     rows, span = query_t.shape[1], window.shape[1]
     chunks = span // rows - 1
     s = attention_specs(rows, span)
     return pl.pallas_call(
         functools.partial(attend_back_kernel, chunks, rows),
         grid=(KEY_HEADS // 2,),
-        in_specs=[s["smem"], s["row"], s["table"], s["table"], s["query"], s["kv"], s["query"], s["stat"], s["stat"]],
+        in_specs=[s["smem"], s["row"], s["table"], s["table"], s["query"], s["kv"], s["query"], s["stat"], s["query"]],
         out_specs=[s["query"], s["kv"]],
         out_shape=[
             jax.ShapeDtypeStruct(query_t.shape, BF16),
@@ -662,7 +514,7 @@
         compiler_params=pltpu.CompilerParams(vmem_limit_bytes=40 * 2**20),
         cost_estimate=pl.CostEstimate(flops=18 * 10**9, bytes_accessed=16 * 10**6, transcendentals=15 * 10**6),
         name="attend_back",
-    )(offset.reshape(1), lo, cos_t, sin_t, query_t, window, grad_t, lse, delta)
+    )(offset.reshape(1), lo, cos_t, sin_t, query_t, window, grad_t, lse, attended_t)
 
 
 def hits(slot_ref, slots):
@@ -782,6 +634,7 @@
         [number(z, y, x, 1 - c)]
         + [number(z, 1 - y, x, cc) for cc in (c, 1 - c)]
         + [number(z, y, 1 - x, cc) for cc in (c, 1 - c)]
+        + [number(z, 1 - y, 1 - x, c)]
         + [number(lax.rem(z + d, 4), y, x, c) for d in (1, 2, 3)]
     )
 
@@ -1192,6 +1045,7 @@
         return total
 
     def step(self, u):
+        u = jnp.int32(u)
         i = u // 2
         k = far_first(i)
         early = lax.rem(u, 2) == 0
@@ -1420,11 +1274,12 @@
 
 
 def attend_back_mesh_kernel(
-    chunks, rows, lo_ref, cos_ref, sin_ref, q_ref, kv_ref, g_ref, lse_ref, delta_ref, y_ref, slots_ref,
-    dq_ref, dkv_ref, o_ref, bias, *scratch,
+    chunks, rows, lo_ref, cos_ref, sin_ref, q_ref, kv_ref, g_ref, lse_ref, out_ref, y_ref, slots_ref, residual_ref,
+    grad_out, layer_ref, bias, dkv, sums_ref, gt_ref, o_ref, *scratch,
 ):
     greet_near()
-    rs = Back(y_ref, slots_ref, o_ref, scratch)
+    rs = Back(y_ref, slots_ref, o_ref, scratch[: Back.n_scratch])
+    keys = Unwindow(rows, dkv, sums_ref, scratch[Back.n_scratch :])
     rs.start()
     make_bias(bias, lo_ref, chunks, rows)
     width = 2 * GROUP * HEAD_DIM
@@ -1434,36 +1289,304 @@
         head = pl.ds(pl.multiple_of(j * width, width), width)
 
         def between(half):
-            rs.step(2 * j + half)
+            if half == 0:
+                rs.step(j)
 
         attend_back_pair(
             chunks, rows, lax.rem(lax.axis_index("dev"), 2), cos_ref, sin_ref, q_ref.at[head, :], kv_ref.at[:, :, lanes], g_ref.at[head, :],
-            lse_ref.at[pl.ds(j, 1)], delta_ref.at[pl.ds(j, 1)], dq_ref.at[head, :], dkv_ref.at[:, :, lanes], bias, between,
+            lse_ref.at[pl.ds(j, 1)], out_ref.at[head, :], gt_ref.at[head, :], dkv.at[:, :, lanes], bias, between,
         )
         return 0
 
     lax.fori_loop(0, KEY_HEADS // 2, pair, 0)
+    keys.start()
+
+    def turned(first, last):
+        for n in range(first, last, 256):
+            grad_out[:, n : n + 256] = gt_ref[n : n + 256, :].T
+
+    def rest(u, _):
+        rs.step(u)
+
+        @pl.when(u == 4)
+        def _():
+            keys.sums()
+
+        @pl.when(u == 6)
+        def _():
+            keys.near()
+            turned(0, QUERY_HEADS * HEAD_DIM)
+        return 0
+
+    lax.fori_loop(4, 8, rest, 0)
+    keys.end()
+    base = QUERY_HEADS * HEAD_DIM
+    key_t = sums_ref[0].T
+    cosine, sine = cos_ref[...], sin_ref[...]
+    for n in range(KEY_HEADS):
+        first, middle = n * HEAD_DIM, n * HEAD_DIM + HEAD_DIM // 2
+        u, w = key_t[first:middle], key_t[middle : first + HEAD_DIM]
+        gt_ref[base + first : base + middle, :] = (u * cosine + w * sine).astype(BF16)
+        gt_ref[base + middle : base + first + HEAD_DIM, :] = (w * cosine - u * sine).astype(BF16)
+    turned(base, base + KEY_HEADS * HEAD_DIM)
+    grad_out[:, base + KEY_HEADS * HEAD_DIM :] = sums_ref[1].astype(BF16)
     rs.finish()
-
-
-def attend_back_mesh(query_t, window, lo, grad_t, lse, delta, cos_t, sin_t, y, slots):
-    rows, span = query_t.shape[1], window.shape[1]
+    layer_ref[...] = (residual_ref[...] + o_ref[...]).astype(BF16)
+
+
+def attend_back_mesh(query_t, window, lo, grad_t, lse, attended_t, cos_t, sin_t, y, slots, residual):
+    rows, span, keys = query_t.shape[1], window.shape[1], window.shape[2]
     chunks = span // rows - 1
     model = y.shape[1]
     hbm, vmem = pl.BlockSpec(memory_space=pl.ANY), pl.BlockSpec(memory_space=pltpu.VMEM)
     return pl.pallas_call(
         functools.partial(attend_back_mesh_kernel, chunks, rows),
-        in_specs=[vmem] * 8 + [hbm, vmem],
-        out_specs=[vmem] * 3,
+        in_specs=[vmem] * 8 + [hbm, vmem, vmem],
+        out_specs=[vmem] * 2,
         out_shape=[
-            jax.ShapeDtypeStruct(query_t.shape, BF16),
-            jax.ShapeDtypeStruct(window.shape, BF16),
-            jax.ShapeDtypeStruct((rows, model), F32),
+            jax.ShapeDtypeStruct((rows, QKV), BF16),
+            jax.ShapeDtypeStruct((rows, model), BF16),
         ],
-        scratch_shapes=[pltpu.VMEM((chunks * rows, rows), F32)] + Back.scratch(rows, model // 2),
+        scratch_shapes=[
+            pltpu.VMEM((chunks * rows, rows), F32), pltpu.VMEM(window.shape, BF16), pltpu.VMEM((2, rows, keys), F32),
+            pltpu.VMEM((QKV, rows), BF16), pltpu.VMEM((rows, model), F32),
+        ]
+        + Back.scratch(rows, model // 2) + Unwindow.scratch(rows, keys),
         compiler_params=pltpu.CompilerParams(collective_id=15, has_side_effects=True, vmem_limit_bytes=56 * 2**20),
         name="attend_back",
-    )(lo, cos_t, sin_t, query_t, window, grad_t, lse, delta, y, slots)
+    )(lo, cos_t, sin_t, query_t, window, grad_t, lse, attended_t, y, slots, residual)
+
+
+def finish_kernel(
+    rows, n_ref, g_ref, w_ref, more_ref, gain_ref, scale_ref, x_ref, rg_ref,
+    oq_ref, ok_ref, ov_ref, om_ref, tg_ref, fg_ref, dense, acc, ra, rb, rz, out, ng, mine, theirs,
+    ssem, rsem, sa, ra_sem, sb, rb_sem, sz, rz_sem, gs, gr,
+):
+    z, y, x, c = place()
+    greet_all()
+    sibling = number(z, y, x, 1 - c)
+    cols = acc.shape[2]
+    main = g_ref.shape[1]
+    half = cols // 2
+    pieces = [pl.ds(0, half), pl.ds(half, half)]
+    around = (number(z, y, 1 - x, c), number(z, 1 - y, x, c))
+    swap = Swap(lambda t: mine.at[t], theirs, gs, gr)
+
+    def lane(dy, dx, k):
+        yy = 1 - y if dy else y
+        xx = 1 - x if dx else x
+        return (lax.rem(z + k, 4) * 2 + yy) * 2 + xx
+
+    def to_sibling(dy, dx, k):
+        chip = lane(dy, dx, k)
+        n = (k, dy, dx)
+        sides = (
+            (dense.at[chip, pl.ds(pl.multiple_of((1 - c) * rows, 16), rows), :], pl.ds(0, main)),
+            (more_ref.at[pl.ds(pl.multiple_of((2 * chip + 1 - c) * rows, 16), rows), :], pl.ds(main, cols - main)),
+        )
+        return [
+            pltpu.make_async_remote_copy(
+                src_ref=source, dst_ref=acc.at[chip, :, at], send_sem=ssem.at[(*n, i)], recv_sem=rsem.at[(*n, i)],
+                device_id=(sibling,), device_id_type=MESH)
+            for i, (source, at) in enumerate(sides)
+        ]
+
+    def first(p, d2, k, dy, dx):
+        return pltpu.make_async_remote_copy(
+            src_ref=acc.at[lane(dy, dx, k), :, pieces[p]], dst_ref=ra.at[p, d2, k],
+            send_sem=sa.at[p, d2, k], recv_sem=ra_sem.at[p, d2, k], device_id=(around[p],), device_id_type=MESH)
+
+    def second(p, k):
+        dy, dx = (1, 0) if p == 0 else (0, 1)
+        return pltpu.make_async_remote_copy(
+            src_ref=acc.at[lane(dy, dx, k), :, pieces[p]], dst_ref=rb.at[p, k],
+            send_sem=sb.at[p, k], recv_sem=rb_sem.at[p, k], device_id=(around[1 - p],), device_id_type=MESH)
+
+    def third(p, k):
+        return pltpu.make_async_remote_copy(
+            src_ref=acc.at[lane(0, 0, k), :, pieces[p]], dst_ref=rz.at[p, k],
+            send_sem=sz.at[p, k], recv_sem=rz_sem.at[p, k],
+            device_id=(number(lax.rem(z + k, 4), y, x, c),), device_id_type=MESH)
+
+    quarter = ((1, 1), (1, 0), (0, 1), (0, 0))
+
+    def product(i, _):
+        k = far_first(i)
+        zz = lax.rem(z + k, 4)
+        at = pl.ds(pl.multiple_of(zz * 8 * rows, 128), 8 * rows)
+        part = dims(n_ref[:, at], g_ref[...], 0, 0).astype(BF16)
+        for chip in range(4):
+            dense[zz * 4 + chip] = part[chip * 2 * rows : (chip + 1) * 2 * rows]
+        for dy, dx in quarter:
+            for cp in to_sibling(dy, dx, k):
+                cp.start()
+        return 0
+
+    def own_sums(k):
+        for dy, dx in quarter:
+            chip = lane(dy, dx, k)
+            for cp in to_sibling(dy, dx, k):
+                cp.wait_recv()
+            acc[chip, :, :main] = (
+                acc[chip, :, :main].astype(F32) + dense[chip, pl.ds(pl.multiple_of(c * rows, 16), rows), :].astype(F32)
+            ).astype(BF16)
+            acc[chip, :, main:] = (
+                acc[chip, :, main:].astype(F32)
+                + more_ref[pl.ds(pl.multiple_of((2 * chip + c) * rows, 16), rows), :].astype(F32)
+            ).astype(BF16)
+            if dx:
+                first(0, dy, k, dy, dx).start()
+            if dy:
+                first(1, dx, k, dy, dx).start()
+
+    def middle(k):
+        for p in range(2):
+            dy, dx = (1, 0) if p == 0 else (0, 1)
+            first(p, 1, k, 1, 1).wait_recv()
+            block = acc.at[lane(dy, dx, k), :, pieces[p]]
+            block[...] = (block[...].astype(F32) + ra[p, 1, k].astype(F32)).astype(BF16)
+            second(p, k).start()
+
+    def late(k):
+        for p in range(2):
+            first(p, 0, k, 1 - p, p).wait_recv()
+            second(p, k).wait_recv()
+            block = acc.at[lane(0, 0, k), :, pieces[p]]
+            total = block[...].astype(F32) + ra[p, 0, k].astype(F32) + rb[p, k].astype(F32)
+
+            @pl.when(k > 0)
+            def _(p=p, block=block, total=total):
+                block[...] = total.astype(BF16)
+                third(p, k).start()
+
+            @pl.when(k == 0)
+            def _(p=p, total=total):
+                out[:, pieces[p]] = total
+
+    def rest_of_tokens():
+        ng[...] = dims(g_ref[...], w_ref[:, :main], 1, 1)
+
+        def tail(i, total):
+            at = pl.ds(pl.multiple_of(i * 32, 32), 32)
+            grad, scale, values = ng[at, :], scale_ref[at, :], x_ref[at, :].astype(F32)
+            weighted = grad * gain_ref[...]
+            scaled = values * scale
+            mean = jnp.mean(weighted * values, axis=1, keepdims=True)
+            tg_ref[at, :] = rg_ref[at, :] + scale * weighted - scaled * (scale * scale * mean)
+            return total + jnp.sum(grad * scaled, axis=0, keepdims=True)
+        total = lax.fori_loop(0, x_ref.shape[0] // 32, tail, jnp.zeros(gain_ref.shape, F32))
+        mine[...] = jnp.zeros_like(mine)
+        for t in range(32):
+            mine[t, 0:1, 0:rows] = total[:, t * rows : (t + 1) * rows]
+        swap.start()
+
+    lax.fori_loop(0, 4, product, 0)
+
+    def steps(i, _):
+        @pl.when(i < 4)
+        def _():
+            own_sums(far_first(i))
+
+        @pl.when(i == 3)
+        def _():
+            rest_of_tokens()
+
+        @pl.when((i >= 1) & (i < 5))
+        def _():
+            middle(far_first(i - 1))
+
+        @pl.when(i >= 2)
+        def _():
+            late(far_first(i - 2))
+        return 0
+    lax.fori_loop(0, 6, steps, 0)
+    swap.wait_recv()
+    fg_ref[...] = jnp.sum(theirs[...], axis=0)
+    for p in range(2):
+        for k in range(1, 4):
+            third(p, k).wait_recv()
+        out[:, pieces[p]] += rz[p, 1].astype(F32) + rz[p, 2].astype(F32) + rz[p, 3].astype(F32)
+    at = 0
+    for ref in (oq_ref, ok_ref, ov_ref, om_ref):
+        ref[...] = out[:, at : at + ref.shape[1]]
+        at += ref.shape[1]
+
+    def sent(k, _):
+        for dy, dx in quarter:
+            for cp in to_sibling(dy, dx, k):
+                cp.wait_send()
+        for p in range(2):
+            first(p, 0, k, 1 - p, p).wait_send()
+            first(p, 1, k, 1, 1).wait_send()
+            second(p, k).wait_send()
+
+            @pl.when(k > 0)
+            def _(p=p):
+                third(p, k).wait_send()
+        return 0
+    lax.fori_loop(0, 4, sent, 0)
+    swap.wait_send()
+
+
+def finish(normed, grad, matrices, more, gain, scale, tokens, residual_grad):
+    count, model = normed.shape
+    rows = model // 32
+    main, cols = grad.shape[1], grad.shape[1] + more.shape[1]
+    half = cols // 2
+    dma = pltpu.SemaphoreType.DMA
+    vmem = pl.BlockSpec(memory_space=pltpu.VMEM)
+    widths = [QUERY_HEADS * HEAD_DIM, KEY_HEADS * HEAD_DIM, KEY_HEADS * HEAD_DIM, more.shape[1]]
+    return pl.pallas_call(
+        functools.partial(finish_kernel, rows),
+        in_specs=[vmem] * 8,
+        out_specs=[vmem] * 6,
+        out_shape=[jax.ShapeDtypeStruct((rows, w), F32) for w in widths] + [
+            jax.ShapeDtypeStruct((count, model), F32),
+            jax.ShapeDtypeStruct((8, 128), F32),
+        ],
+        scratch_shapes=[
+            pltpu.VMEM((16, 2 * rows, main), BF16),
+            pltpu.VMEM((16, rows, cols), BF16),
+            pltpu.VMEM((2, 2, 4, rows, half), BF16),
+            pltpu.VMEM((2, 4, rows, half), BF16),
+            pltpu.VMEM((2, 4, rows, half), BF16),
+            pltpu.VMEM((rows, cols), F32),
+            pltpu.VMEM((count, model), F32),
+            pltpu.VMEM((32, 8, 128), F32),
+            pltpu.VMEM((32, 8, 128), F32),
+            dma((4, 2, 2, 2)), dma((4, 2, 2, 2)), dma((2, 2, 4)), dma((2, 2, 4)), dma((2, 4)), dma((2, 4)), dma((2, 4)), dma((2, 4)),
+            dma((32,)), dma((32,)),
+        ],
+        compiler_params=pltpu.CompilerParams(collective_id=17, has_side_effects=True, vmem_limit_bytes=56 * 2**20),
+        name="finish",
+    )(normed, grad, matrices, more, gain, scale, tokens, residual_grad)
+
+
+def hand_over_kernel(count, *refs):
+    sources, outs, held = refs[:count], refs[count : 2 * count], refs[2 * count : 3 * count]
+    sems = refs[3 * count]
+    into = [pltpu.make_async_copy(sources[i], held[i], sems.at[0, i]) for i in range(count)]
+    out = [pltpu.make_async_copy(held[i], outs[i], sems.at[1, i]) for i in range(count)]
+    for cp in into:
+        cp.start()
+    for a, b in zip(into, out, strict=True):
+        a.wait()
+        b.start()
+    for cp in out:
+        cp.wait()
+
+
+def hand_over(*arrays):
+    hbm = pl.BlockSpec(memory_space=pl.ANY)
+    return pl.pallas_call(
+        functools.partial(hand_over_kernel, len(arrays)),
+        in_specs=[hbm] * len(arrays),
+        out_specs=[hbm] * len(arrays),
+        out_shape=[jax.ShapeDtypeStruct(a.shape, a.dtype) for a in arrays],
+        scratch_shapes=[pltpu.VMEM(a.shape, a.dtype) for a in arrays] + [pltpu.SemaphoreType.DMA((2, len(arrays)))],
+        compiler_params=pltpu.CompilerParams(vmem_limit_bytes=60 * 2**20),
+        name="hand_over",
+    )(*arrays)
 
 
 def rms_scale(values):
@@ -1482,13 +1605,6 @@
     if meshed():
         return gather_all(block, cid, by_rows)
     return lax.all_gather(block, "dev", axis=0, tiled=True)
-
-
-def reduced(dense, more, cid):
-    if meshed():
-        return reduce_all(dense, more, cid)
-    dense = jnp.concatenate([dense, more], axis=1)
-    return lax.psum_scatter(dense, "dev", scatter_dimension=0, tiled=True).astype(F32)
 
 
 def on_device(
@@ -1630,44 +1746,55 @@
     output_gradient = lax.psum_scatter(output_gradient, "dev", scatter_dimension=0, tiled=True).astype(F32)
     grad_t = dims(output_matrix, branch_grad, 1, 1).astype(BF16)
 
-    delta = jnp.sum((attended_t.astype(F32) * grad_t.astype(F32)).reshape(QUERY_HEADS, HEAD_DIM, rows), axis=1)
-    delta = jnp.pad(delta.reshape(KEY_HEADS // 2, 2 * GROUP, rows), ((0, 0), (0, 8 - 2 * GROUP), (0, 0)))
     if meshed():
-        query_grad_t, window_grad, mixture = attend_back_mesh(
-            query_t, window, lo, grad_t, lse, delta, cos_t, sin_t, out_rows, plane_slots
+        qkv_grad, layer_output = attend_back_mesh(
+            query_t, window, lo, grad_t, lse, attended_t, cos_t, sin_t, out_rows, plane_slots, residual
         )
     else:
-        query_grad_t, window_grad = attend_back(query_t, window, offset, lo, grad_t, lse, delta, cos_t, sin_t)
-    layer_output = (residual + mixture).astype(BF16)
-    key_grad, value_grad = unwindow(window_grad)
-    key_grad_t = rotate_t(key_grad.T, cos_t, -sin_t).astype(BF16)
-    qkv_grad_t = jnp.concatenate([query_grad_t, key_grad_t, value_grad.T.astype(BF16)], axis=0)
-    qkv_gradient = dims(normed_one, qkv_grad_t, 0, 1)
-    normed_one_grad = dims(qkv_grad_t, qkv_matrix, 0, 1)
-    weighted_one = normed_one_grad * gain_first
-    first_gain_grad = jnp.sum(normed_one_grad * inputs * scale_one, axis=0)
-    tokens_gradient = (
-        residual_grad
-        + scale_one * weighted_one
-        - inputs * scale_one**3 * jnp.mean(weighted_one * inputs, axis=-1, keepdims=True)
-    )
-    terms = qkv_gradient.astype(BF16)
+        query_grad_t, window_grad = attend_back(query_t, window, offset, lo, grad_t, lse, attended_t, cos_t, sin_t)
+        key_grad, value_grad = unwindow(window_grad)
+        key_grad_t = rotate_t(key_grad.T, cos_t, -sin_t).astype(BF16)
+        qkv_grad_t = jnp.concatenate([query_grad_t, key_grad_t, value_grad.T.astype(BF16)], axis=0)
+        layer_output = (residual + mixture).astype(BF16)
     more = jnp.concatenate(
-        [router_gradient, first_gain_grad[:, None], second_gain_grad[:, None],
-         jnp.zeros((model, (-(EXPERTS + 2)) % 256), F32)],
-        axis=1,
+        [router_gradient, second_gain_grad[:, None], jnp.zeros((model, (-(EXPERTS + 1)) % 256), F32)], axis=1
     ).astype(BF16)
-    sums = reduced(terms, more, 4)
+    if meshed():
+        query_sums, key_sums, value_sums, more_sums, tokens_gradient, first_sums = finish(
+            normed_one, qkv_grad, matrices, more, gain_first[None, :], scale_one, tokens, residual_grad
+        )
+        first_sums = first_sums[0, :weight_rows]
+        (
+            gate_gradient, up_gradient, down_gradient, layer_output, tokens_gradient, query_sums, key_sums, value_sums
+        ) = hand_over(
+            gate_gradient, up_gradient, down_gradient, layer_output, tokens_gradient, query_sums, key_sums, value_sums
+        )
+    else:
+        qkv_gradient = dims(normed_one, qkv_grad_t, 0, 1).astype(BF16)
+        normed_one_grad = dims(qkv_grad_t, qkv_matrix, 0, 1)
+        weighted_one = normed_one_grad * gain_first
+        tokens_gradient = (
+            residual_grad
+            + scale_one * weighted_one
+            - inputs * scale_one**3 * jnp.mean(weighted_one * inputs, axis=-1, keepdims=True)
+        )
+        sums = lax.psum_scatter(
+            jnp.concatenate([qkv_gradient, more], axis=1), "dev", scatter_dimension=0, tiled=True
+        ).astype(F32)
+        query_sums, key_sums, value_sums, more_sums = jnp.split(sums, [q_width, q_width + k_width, QKV], axis=1)
+        first_sums = lax.psum_scatter(
+            jnp.sum(normed_one_grad * inputs * scale_one, axis=0), "dev", scatter_dimension=0, tiled=True
+        )
     return (
         layer_output,
         tokens_gradient,
-        sums[:, QKV + EXPERTS],
-        sums[:, :q_width],
-        sums[:, q_width : q_width + k_width],
-        sums[:, q_width + k_width : QKV],
+        first_sums,
+        query_sums,
+        key_sums,
+        value_sums,
         output_gradient,
-        sums[:, QKV + EXPERTS + 1],
-        sums[:, QKV : QKV + EXPERTS],
+        more_sums[:, EXPERTS],
+        more_sums[:, :EXPERTS],
         gate_gradient,
         up_gradient,
         down_gradient,

time: 724 us -> 662 us (0.914)
  Pallas kernels: 615 us -> 593 us
  local copies, waits for them, and re-layouts: 32.6 us -> 13.5 us
  matrix products: 36.4 us -> 22.4 us
    pallas_call x2, Pallas kernels: 101 us -> 65.9 us  [the longest x1 57.3 us: finish(): pl.pallas_call(functools.partial(finish_kernel, rows), in_specs=[vmem] *...]
    dot_general x9 -> x7, matrix products: 36.4 us -> 22.4 us  [dims(): lax.dot_general(a, b, (((ca,), (cb,)), ((), ())), preferred_element_type=...]
    pallas_call x1, Pallas kernels: 118 us -> 132 us  [attend_back_mesh(): pl.pallas_call(functools.partial(attend_back_mesh_kernel, chunks, rows),...]
    unnamed x44 -> x33, local copies, waits for them, and re-layouts: 14.9 us -> 3.73 us
  transfers between devices with their start and end apart: 2 -> 2, of which waited for: 0 -> 0; matrix products, arithmetic and copies ran while one was open for 8% -> 5% of each run, Pallas kernels for 56% -> 57%
where the time goes in v4:
time: 662 us; the launch traced here: 657 us
  Pallas kernels  593 us (90%)
  matrix products  22.4 us (3%)
  between operations  14.7 us (2%)
  local copies, waits for them, and re-layouts  13.5 us (2%)
  other arithmetic  12.6 us (2%)
    pallas_call x1, Pallas kernels, attend_back_mesh(): pl.pallas_call(functools.partial(attend_back_mesh_kernel, chunks, rows),...  132 us
    pallas_call x1, Pallas kernels, attend_mesh(): pl.pallas_call(functools.partial(attend_mesh_kernel, chunks, rows), in_sp...  125 us
    pallas_call x1, Pallas kernels, run_experts(): pl.pallas_call(experts_kernel, in_specs=[hbm, vmem, vmem, hbm, vmem, vmem...  114 us
    pallas_call x1, Pallas kernels, run_grads(): pl.pallas_call(grads_kernel, in_specs=[hbm, vmem, vmem, hbm, hbm, vmem, v...  102 us
    pallas_call x1, Pallas kernels, finish(): pl.pallas_call(functools.partial(finish_kernel, rows), in_specs=[vmem] *...  57.3 us
    pallas_call x1, Pallas kernels, gather_all(): pl.pallas_call(functools.partial(gather_kernel, rows, pieces), out_shape=...  54.7 us
    dot_general x7, matrix products, dims(): lax.dot_general(a, b, (((ca,), (cb,)), ((), ())), preferred_element_type=...  22.4 us
  transfers between devices with their start and end apart: 2, of which 0 were waited for; matrix products, arithmetic and copies ran while one was open for 5% of the time, Pallas kernels for 57%

profile of v4, /device:TPU:0, one launch (start us, length us, event | category | flops | bytes accessed | tf_op | source)
XLA Modules:
  0.0 657.1 jit_solution(9185193452395297774)
XLA Ops:
  7.2 0.0 all-gather.2.cloned.1.call-start
  7.2 0.7 all-gather.2.cloned.1.call-update
  7.9 0.0 reduce-scatter.2.cloned.1.call-start
  8.0 0.8 copy.62
  8.7 0.8 copy.63
  9.5 0.8 copy.64
  10.3 1.7 concatenate.7.x_ref
  12.0 54.7 %gather_all.1.w_ref = bf16[1536,2688]{1,0:T(8,128)(2,1)} custom-call(bf16[48,2688]{1,0:T(8,128)(2,1)} %concatenate.7.x_ref), custom_call_target="tpu_custom_call" | custom-call | tf_op jit(solution)/shard_map/gather_all/pallas_call | solution.py:111
  66.7 1.7 convert_reduce_fusion.1
  68.4 0.0 copy-done.3
  68.4 0.2 fusion.3
  68.7 0.3 fusion.5.n_ref
  68.9 0.0 copy-start.8
  69.0 5.9 fusion
  74.9 0.0 copy-start.6
  75.0 0.0 copy-start.14
  75.0 1.4 copy-done.6
  76.4 0.6 fusion.23
  77.0 0.2 multiply_cosine_fusion
  77.2 0.0 copy-start.9
  77.2 0.0 copy-start.10
  77.2 0.0 slice-start
  77.2 0.1 subtract_convert_fusion.1
  77.3 0.1 copy.65
  77.5 0.1 copy.73
  77.7 0.8 pad_maximum_fusion.kv_ref
  78.6 0.1 slice-done
  78.6 0.2 subtract_convert_fusion
  78.9 1.0 maximum_multiply_fusion
  79.9 3.1 convert_reduce_fusion
  83.0 0.6 convert_bitcast_fusion.1.mine_ref
  83.6 125.0 %attend.1 = (bf16[1536,256]{1,0:T(8,128)(2,1)}, f32[4,8,256]{2,1,0:T(8,128)}, bf16[2,2560,512]{2,1,0:T(8,128)(2,1)}, f32[32,8,256]{2,1,0:T(8,128)}, bf16[2560,1536]{1,0:T(8,128)(2,1)}) custom-call(s32[1,256]{1,0:T(1,128)} %bitcast.81, bf16[1536,256]{1,0:T(8,128)(2,1)} %bitcast.72, bf16[2,256,512]{2,1,0:T(8,128)(2,1)} %pad_maximum_fusion.kv_ref, ...), custom_call_target="tpu_custom_call" | custom-call | tf_op jit(solution)/shard_map/attend/pallas_call | solution.py:1258
  208.6 0.0 all-gather.2.cloned.1.call-done
  208.7 4.1 multiply_reduce_fusion.2
  212.7 0.0 copy-start
  212.8 0.2 multiply_convert_fusion.x_ref
  213.0 0.0 copy-start.4
  213.0 1.7 fusion.22
  214.7 0.7 pad.4.gates_ref
  215.4 114.2 %experts.1 = (bf16[2560,1536]{1,0:T(8,128)(2,1)}, bf16[2560,1536]{1,0:T(8,128)(2,1)}, bf16[2560,1536]{1,0:T(8,128)(2,1)}, bf16[2560,512]{1,0:T(8,128)(2,1)}, bf1...) custom-call(bf16[256,1536]{1,0:T(8,128)(2,1)} %copy-done.4, f32[32,8,128]{2,1,0:T(8,128)} %pad.4.gates_ref, ...), custom_call_target="tpu_custom_call" | custom-call | tf_op jit(solution)/shard_map/experts/pallas_call | solution.py:943
  329.6 101.5 %grads.1 = (f32[256,1536]{1,0:T(8,128)}, f32[32,8,128]{2,1,0:T(8,128)}, f32[1536,512]{1,0:T(8,128)}, f32[1536,512]{1,0:T(8,128)}, f32[512,1536]{1,0:T(8,128)}) custom-call(bf16[2560,1536]{1,0:T(8,128)(2,1)} %get-tuple-element.48.dx_ref, f32[32,8,256]{2,1,0:T(8,128)} %get-tuple-element.46.slots_ref, f32[32,8,128]{2,1,0:T(8,128)} %get-tuple-element.49.gg_ref, ...), custom_call_target="tpu_custom_call" | custom-call | tf_op jit(solution)/shard_map/grads/pallas_call | solution.py:1179
  431.1 0.9 slice.57
  432.1 0.0 copy-start.7
  432.1 2.3 multiply_reduce_fusion
  434.4 0.5 multiply_subtract_fusion.rg_ref
  434.9 0.7 copy-done.1
  435.6 3.5 convolution_convert_fusion
  439.1 0.0 reduce-scatter.2.cloned.1.call-update
  439.1 0.6 reshape.182.gain_ref
  439.7 0.8 copy.70.scale_ref
  440.5 0.1 pad.7.clone
  440.6 0.2 convolution_convert_fusion.2
  440.8 0.2 copy.68
  441.0 0.3 broadcast_in_dim.82
  441.3 4.7 fusion.2.g_ref
  446.1 131.8 %attend_back.1 = (bf16[256,2560]{1,0:T(8,128)(2,1)}, bf16[256,1536]{1,0:T(8,128)(2,1)}) custom-call(s32[1,256]{1,0:T(1,128)} %bitcast.82, f32[32,256]{1,0:T(8,128)} %copy-done.9, f32[32,256]{1,0:T(8,128)} %copy-done.10, bf16[1536,256]{1,0:T(8,128)(2,1)} %bitcast.73, bf16[2,2560,512]{2,1,0:T(8,128)(2,1)} %get-tuple-element.57.kv_ref, ...), custom_call_target="tpu_custom_call" | custom-call | tf_op jit(solution)/shard_map/attend_back/pallas_call | solution.py:1342
  577.9 1.2 maximum_maximum_fusion.more_ref
  579.2 57.3 %finish.1 = (f32[48,1536]{1,0:T(8,128)}, f32[48,512]{1,0:T(8,128)}, f32[48,512]{1,0:T(8,128)}, f32[48,256]{1,0:T(8,128)}, f32[256,1536]{1,0:T(8,128)}, /*index=5*/f32[8,128]{1,0:T(8,128)}) custom-call(bf16[256,1536]{1,0:T(8,128)(2,1)} %copy-done.8, bf16[256,2560]{1,0:T(8,128)(2,1)} %get-tuple-element.63.g_ref, bf16[1536,2688]{1,0:T(8,128)(2,1)} %gather_all.1.w_ref, ...), custom_call_target="tpu_custom_call" | custom-call | tf_op jit(solution)/shard_map/finish/pallas_call | solution.py:1539
  636.5 0.7 slice.60
  637.2 0.7 copy.71
  637.9 8.6 %hand_over.1 = (f32[1536,512]{1,0:T(8,128)}, f32[1536,512]{1,0:T(8,128)}, f32[512,1536]{1,0:T(8,128)}, bf16[256,1536]{1,0:T(8,128)(2,1)}, f32[256,1536]{1,0:T(8,...) custom-call(f32[1536,512]{1,0:T(8,128)} %get-tuple-element.54.refs_0_, ...), custom_call_target="tpu_custom_call" | custom-call | tf_op jit(solution)/shard_map/hand_over/pallas_call | solution.py:1581
  646.5 0.7 slice_reduce_fusion
  647.2 1.2 slice_bitcast_fusion
  648.4 1.6 convert_element_type.96
  (37 shorter events, 0.4 us)
Async XLA Ops:
  7.2 201.5 %all-gather.2.cloned.1.call-start = ((), (), s32[]{:S(2)}) async-start(), calls=%async_computation.1 | async-start | bytes 4866048 | tf_op jit(solution)/shard_map/all_gather | solution.py:1633
  7.9 640.5 %reduce-scatter.2.cloned.1.call-start = ((), (), s32[]{:S(2)}) async-start(), calls=%async_computation.2 | async-start | bytes 4866048 | tf_op jit(solution)/shard_map/reduce_scatter | solution.py:1746
  12.0 56.4 %copy-start.3 = (bf16[256,1536]{1,0:T(8,128)(2,1)S(1)}, bf16[256,1536]{1,0:T(8,128)(2,1)}, u32[]{:S(2)}) copy-start(bf16[256,1536]{1,0:T(8,128)(2,1)} %x_ref.1) | copy-start | bytes 2359300
  68.9 5.9 copy-start.8
  74.9 1.5 copy-start.6
  75.0 1.4 copy-start.14
  76.4 1.2 copy-start.12
  76.4 1.3 copy-start.13
  77.2 1.4 copy-start.9
  77.2 1.4 copy-start.10
  77.2 1.4 slice-start
  212.7 221.7 %copy-start = (f32[256,1536]{1,0:T(8,128)}, f32[256,1536]{1,0:T(8,128)S(1)}, u32[]{:S(2)}) copy-start(f32[256,1536]{1,0:T(8,128)S(1)} %get-tuple-element.141.residual_ref) | copy-start | bytes 4718596
  213.0 2.4 copy-start.4
  432.1 2.3 copy-start.7
  434.4 1.1 copy-start.1
  435.6 5.8 copy-start.2
  439.1 1.5 copy-start.5
  637.9 8.6 %copy-start.11 = (f32[48,256]{1,0:T(8,128)S(1)}, f32[48,256]{1,0:T(8,128)}, u32[]{:S(2)}) copy-start(f32[48,256]{1,0:T(8,128)} %get-tuple-element.74) | copy-start | bytes 147460
Sparse Core Ops, SparseCore 0:
  10.9 77.5 all-gather.1
  439.2 142.7 reduce-scatter.1

commit v5 on v4

--- a/solution.py
+++ b/solution.py
@@ -34,89 +34,113 @@
     ]
 
 
-def gather_kernel(rows, pieces, x_ref, o_ref, local_sem, ss, rs):
-    z, y, x, c = place()
-    greet(partners_of(z, y, x, c))
-    sibling = number(z, y, x, 1 - c)
-    me = number(z, y, x, c)
-    around = (number(z, 1 - y, x, c), number(z, y, 1 - x, c))
-
-    def part(ref, block, p):
-        r0, nr, c0, nc = pieces[p]
-        return ref.at[pl.ds(pl.multiple_of(block * rows + r0, 16), nr), pl.ds(c0, nc)]
-
-    def copy(block, p, slot, target, own=False):
-        source = part(x_ref, 0, p) if own else part(o_ref, block, p)
+class Whole:
+    scratch = [pltpu.SemaphoreType.DMA] + [
+        pltpu.SemaphoreType.DMA(shape)
+        for shape in ((2, 2, 4), (2, 4), (2, 3, 4), (2, 3, 4), (2, 4, 4), (2, 4, 4))
+    ]
+
+    def __init__(self, x_ref, o_ref, scratch):
+        self.x_ref, self.o_ref = x_ref, o_ref
+        self.local_sem, self.zs, self.zr, self.fs, self.fr, self.cs, self.cr = scratch
+        self.z, self.y, self.x, self.c = z, y, x, c = place()
+        self.rows, cols = x_ref.shape
+        half = (cols // 256) * 128
+        self.pieces = (pl.ds(0, half), pl.ds(half, cols - half))
+        self.sibling = number(z, y, x, 1 - c)
+        self.me = number(z, y, x, c)
+        self.around = (number(z, 1 - y, x, c), number(z, y, 1 - x, c))
+        self.far = ((1, 0), (0, 1))
+        self.local = pltpu.make_async_copy(x_ref, self.there(self.me), self.local_sem)
+
+    def turn(self, i):
+        middle = i if i < 2 else 5 - i
+        return jnp.where(self.z == 0, (4 - i) % 4, jnp.where(self.z == 3, i, middle))
+
+    def there(self, block, p=None):
+        at = pl.ds(pl.multiple_of(block * self.rows, 16), self.rows)
+        return self.o_ref.at[at, :] if p is None else self.o_ref.at[at, self.pieces[p]]
+
+    def copy(self, source, block, p, send_sem, recv_sem, target):
         return pltpu.make_async_remote_copy(
-            src_ref=source, dst_ref=part(o_ref, block, p),
-            send_sem=ss.at[p * 31 + slot], recv_sem=rs.at[p * 31 + slot],
+            src_ref=source, dst_ref=self.there(block, p), send_sem=send_sem, recv_sem=recv_sem,
             device_id=(target,), device_id_type=MESH)
 
-    pending = []
-
-    def send(*args, **kw):
-        cp = copy(*args, **kw)
-        cp.start()
-        pending.append(cp)
-
-    def at(k, fy, fx):
-        return number(lax.rem(z + 4 - k, 4), (1 - y) if fy else y, (1 - x) if fx else x, c)
-
-    local = pltpu.make_async_copy(x_ref, o_ref.at[pl.ds(pl.multiple_of(me * rows, 16), rows), :], local_sem)
-    local.start()
-    order = (0, 1, 3, 2)
-    far = ((1, 0), (0, 1))
-    for k in (1, 3, 2):
+    def block(self, k, fy=0, fx=0):
+        return number(lax.rem(self.z + 4 - k, 4), (1 - self.y) if fy else self.y, (1 - self.x) if fx else self.x, self.c)
+
+    def along(self, i, use):
+        k = self.turn(i)
+        zz = lax.rem(self.z + 4 - k, 4)
+        for up, step in ((1, 1), (0, 3)):
+            go = (zz <= self.z) & (self.z < 3) if up else (zz >= self.z) & (self.z > 0)
+
+            @pl.when(go)
+            def _(up=up, step=step):
+                block = self.block(k)
+                target = number(lax.rem(self.z + step, 4), self.y, self.x, self.c)
+                for p in range(2):
+                    source = self.x_ref.at[:, self.pieces[p]] if i == 0 else self.there(block, p)
+                    use(self.copy(
+                        source, block, p, self.zs.at[p, up, k], self.zr.at[p, lax.rem(k + step, 4)], target))
+
+    def hop(self, p, n, k):
+        block = self.block(k, *self.far[p]) if n == 2 else self.block(k)
+        target = self.around[p] if n == 0 else self.around[1 - p]
+        return self.copy(self.there(block, p), block, p, self.fs.at[p, n, k], self.fr.at[p, n, k], target)
+
+    def across(self, p, n, k):
+        fy, fx = ((0, 0), self.far[p], (1 - self.far[p][0], 1 - self.far[p][1]), (1, 1))[n]
+        block = self.block(k, fy, fx)
+        return self.copy(self.there(block, p), block, p, self.cs.at[p, n, k], self.cr.at[p, n, k], self.sibling)
+
+    def start(self):
+        self.local.start()
+        self.along(0, lambda cp: cp.start())
+
+    def one(self, i):
+        k = self.turn(i)
+        if i == 0:
+            self.local.wait()
+        else:
+            block = self.block(k)
+            for p in range(2):
+                self.copy(self.there(block, p), block, p, self.zs.at[p, 0, 0], self.zr.at[p, k], self.sibling).wait_recv()
+            self.along(i, lambda cp: cp.start())
         for p in range(2):
-            send(me, p, k - 1, number(lax.rem(z + k, 4), y, x, c), own=True)
-    for k in order:
+            self.hop(p, 0, k).start()
+            self.hop(p, 1, k).start()
+            self.across(p, 0, k).start()
+
+    def two(self, i):
+        k = self.turn(i)
         for p in range(2):
-            block = at(k, 0, 0)
-            if k:
-                copy(block, p, k - 1, sibling).wait_recv()
-            own = k == 0
-            send(block, p, 3 + k, around[p], own=own)
-            send(block, p, 7 + k, around[1 - p], own=own)
-            send(block, p, 15 + k, sibling, own=own)
-    for k in order:
-        for p in range(2):
-            fy, fx = far[p]
-            block = at(k, fy, fx)
-            copy(block, p, 3 + k, sibling).wait_recv()
-            send(block, p, 11 + k, around[1 - p])
-            send(block, p, 19 + k, sibling)
-    for j, slot in ((0, 7), (1, 11)):
-        for k in order:
+            self.hop(p, 0, k).wait_recv()
+            self.hop(p, 2, k).start()
+            self.across(p, 1, k).start()
+
+    def three(self, i):
+        k = self.turn(i)
+        for n in (1, 2):
             for p in range(2):
-                fy, fx = (1, 1) if j else (1 - far[p][0], 1 - far[p][1])
-                block = at(k, fy, fx)
-                copy(block, p, slot + k, sibling).wait_recv()
-                send(block, p, 23 + 4 * j + k, sibling)
-    for k in range(4):
-        for p in range(2):
-            for s in (15, 19, 23, 27):
-                copy(me, p, s + k, sibling).wait_recv()
-    for cp in pending:
-        cp.wait_send()
-    local.wait()
-
-
-def gather_all(block, cid, by_rows):
-    rows, cols = block.shape
-    if by_rows:
-        pieces = ((0, rows // 2, 0, cols), (rows // 2, rows // 2, 0, cols))
-    else:
-        half = (cols // 256) * 128
-        pieces = ((0, rows, 0, half), (0, rows, half, cols - half))
-    return pl.pallas_call(
-        functools.partial(gather_kernel, rows, pieces),
-        out_shape=jax.ShapeDtypeStruct((32 * rows, cols), block.dtype),
-        in_specs=[pl.BlockSpec(memory_space=pl.ANY)],
-        out_specs=pl.BlockSpec(memory_space=pl.ANY),
-        scratch_shapes=[pltpu.SemaphoreType.DMA, pltpu.SemaphoreType.DMA((62,)), pltpu.SemaphoreType.DMA((62,))],
-        compiler_params=pltpu.CompilerParams(collective_id=cid, has_side_effects=True),
-        name="gather_all",
-    )(block)
+                self.hop(p, n, k).wait_recv()
+                self.across(p, n + 1, k).start()
+
+    def end(self):
+        for k in range(4):
+            for p in range(2):
+                for n in range(4):
+                    self.across(p, n, k).wait_recv()
+
+    def sent(self):
+        for i in range(4):
+            self.along(i, lambda cp: cp.wait_send())
+        for k in range(4):
+            for p in range(2):
+                for n in range(3):
+                    self.hop(p, n, k).wait_send()
+                for n in range(4):
+                    self.across(p, n, k).wait_send()
 
 
 from jax.sharding import PartitionSpec as P
@@ -129,6 +153,8 @@
 EXPERTS = 32
 MAXDOC = 2000
 EPSILON = 1e-06
+UNPICKED = 1e9
+CAPACITY = 72
 MASKED = -1e30
 QKV = (QUERY_HEADS + 2 * KEY_HEADS) * HEAD_DIM
 F32 = jnp.float32
@@ -740,7 +766,13 @@
             self.own(p).start()
         self.along_own(lambda cp: cp.start())
 
-    def one(self, i):
+    def come(self, i):
+        k = self.turn(i)
+        for p in range(2):
+            self.to_z(p, True, lax.rem(k + 3, 4)).wait_recv()
+        self.along(i, lambda cp: cp.start())
+
+    def one(self, i, come=True):
         k = self.turn(i)
 
         @pl.when(i == 0)
@@ -748,12 +780,11 @@
             for p in range(2):
                 self.own(p).wait()
 
-        @pl.when(i > 0)
-        def _():
-            for p in range(2):
-                self.to_z(p, True, lax.rem(k + 3, 4)).wait_recv()
-
-        self.along(i, lambda cp: cp.start())
+        if come:
+            @pl.when(i > 0)
+            def _():
+                self.come(i)
+
         for p in range(2):
             self.hop(p, k).start()
         for p in range(2):
@@ -816,10 +847,14 @@
         lax.fori_loop(0, 4, each, 0)
 
 
+BEFORE_UNIT = {0: ("o1", "t0", "o2", "t1"), 4: ("o3", "t2"), 8: ("t3",)}
+
+
 def experts_kernel(
-    x_ref, gates_ref, slots_ref, ui_ref, wg_ref, wu_ref, wd_ref,
-    xi_out, dx_out, y_out, hg_ref, dg_ref, du_ref, gg_ref,
-    gates, xi, ubuf, dx_buf, y_buf, gs, gr, usem, xsem, osem, *scratch,
+    x_ref, gates_ref, slots_ref, ui_ref, wg_in, wu_in, wd_in,
+    xi_out, dx_out, y_out, hg_out, dg_out, du_out, gg_ref,
+    gates, xi, ubuf, dx_buf, y_buf, hg_ref, dg_ref, du_ref, wg_ref, wu_ref, wd_ref, wgt, wut, wdt,
+    gs, gr, usem, xsem, osem, wsem, *scratch,
 ):
     z, y, x, c = place()
     rows = x_ref.shape[0]
@@ -839,7 +874,16 @@
 
     load_up(0).start()
     swap.start()
+    loads = [
+        pltpu.make_async_copy(source, into, wsem.at[i])
+        for i, (source, into) in enumerate(((wg_in, wg_ref), (wu_in, wu_ref), (wd_in, wd_ref)))
+    ]
+    for cp in loads:
+        cp.start()
     ag.one(0)
+    for cp, source, into in zip(loads, (wg_ref, wu_ref, wd_ref), (wgt, wut, wdt), strict=True):
+        cp.wait()
+        into[...] = source[...].T
     swap.wait_recv()
 
     def store(n, buf, out, u):
@@ -849,7 +893,10 @@
         return [store(0, dx_buf, dx_out, u), store(1, y_buf, y_out, u)]
 
     def keep(u):
-        return pltpu.make_async_copy(xi.at[at_chip(u), :], xi_out.at[at_chip(u), :], xsem.at[u])
+        return [
+            pltpu.make_async_copy(held.at[at_chip(u), :], out.at[at_chip(u), :], xsem.at[i, u])
+            for i, (held, out) in enumerate(((xi, xi_out), (hg_ref, hg_out), (dg_ref, dg_out), (du_ref, du_out)))
+        ]
 
     def unit(u):
         slot = lax.rem(u, 2)
@@ -877,7 +924,7 @@
             gate_row = jnp.concatenate([gates[block, 0:1, :], gates[block, 1:2, :]], axis=1)
             gate.append(jnp.sum(jnp.where(hit, gate_row, 0.0), axis=1, keepdims=True))
         gate_of_slot = jnp.concatenate(gate, axis=0)
-        hidden_up = dims(ubuf[slot], wd_ref[...], 1, 1)
+        hidden_up = dims(ubuf[slot], wdt[...], 1, 0)
         rows_in = xi[at, :]
         gate_in = dims(rows_in, wg_ref[...], 1, 0)
         up_in = dims(rows_in, wu_ref[...], 1, 0)
@@ -891,7 +938,7 @@
         hg_ref[at, :] = gated
         dg_ref[at, :] = gate_back
         du_ref[at, :] = up_back
-        dx_buf[slot] = (dims(gate_back, wg_ref[...], 1, 1) + dims(up_back, wu_ref[...], 1, 1)).astype(BF16)
+        dx_buf[slot] = (dims(gate_back, wgt[...], 1, 0) + dims(up_back, wut[...], 1, 0)).astype(BF16)
         y_buf[slot] = dims(gated, wd_ref[...], 1, 0).astype(BF16)
         gate_grad = jnp.sum(hidden * hidden_up, axis=1, keepdims=True)
         for core in range(2):
@@ -901,31 +948,34 @@
             gg_ref[block, 1:2, :] = row[:, 128:]
         for s in stores(u):
             s.start()
-        keep(u).start()
-
-    def each(v, _):
-        i, group = v // 4, lax.rem(v, 4)
-
-        @pl.when((group == 0) & (i < 3))
-        def _():
-            ag.one(i + 1)
-
-        @pl.when((group == 0) & (i < 4))
-        def _():
-            ag.two(i)
-
-        @pl.when(v >= 4)
-        def _():
-            unit(v - 4)
+        for s in keep(u):
+            s.start()
+
+    step = {}
+    for i in range(4):
+        step[f"o{i}"] = functools.partial(ag.one, jnp.int32(i))
+        step[f"c{i}"] = functools.partial(ag.come, jnp.int32(i))
+        step[f"s{i}"] = functools.partial(ag.one, jnp.int32(i), False)
+        step[f"t{i}"] = functools.partial(ag.two, jnp.int32(i))
+
+    def each(u, _):
+        for when, names in BEFORE_UNIT.items():
+            @pl.when(u == when)
+            def _(names=names):
+                for name in names:
+                    step[name]()
+
+        unit(u)
         return 0
 
-    lax.fori_loop(0, 20, each, 0)
+    lax.fori_loop(0, 16, each, 0)
     for u in (14, 15):
         for s in stores(u):
             s.wait()
 
     def last(u, _):
-        keep(u).wait()
+        for s in keep(u):
+            s.wait()
         return 0
     lax.fori_loop(0, 16, last, 0)
     ag.sent()
@@ -942,8 +992,8 @@
     short = jax.ShapeDtypeStruct((n, ff), BF16)
     return pl.pallas_call(
         experts_kernel,
-        in_specs=[hbm, vmem, vmem, hbm, vmem, vmem, vmem],
-        out_specs=[hbm] * 3 + [vmem] * 4,
+        in_specs=[hbm, vmem, vmem, hbm, hbm, hbm, hbm],
+        out_specs=[hbm] * 6 + [vmem],
         out_shape=[long] * 3 + [short] * 3 + [jax.ShapeDtypeStruct((32, 8, 128), F32)],
         scratch_shapes=[
             pltpu.VMEM((32, 8, 128), F32),
@@ -951,7 +1001,10 @@
             pltpu.VMEM((2, 2 * SLOTS, model), BF16),
             pltpu.VMEM((2, 2 * SLOTS, model), BF16),
             pltpu.VMEM((2, 2 * SLOTS, model), BF16),
-            dma((32,)), dma((32,)), dma((2,)), dma((16,)), dma((2, 2)),
+            pltpu.VMEM((n, ff), BF16), pltpu.VMEM((n, ff), BF16), pltpu.VMEM((n, ff), BF16),
+            pltpu.VMEM((model, ff), BF16), pltpu.VMEM((model, ff), BF16), pltpu.VMEM((ff, model), BF16),
+            pltpu.VMEM((ff, model), BF16), pltpu.VMEM((ff, model), BF16), pltpu.VMEM((model, ff), BF16),
+            dma((32,)), dma((32,)), dma((2,)), dma((4, 16)), dma((2, 2)), dma((3,)),
         ] + Forth.scratch(rows, model // 2),
         compiler_params=pltpu.CompilerParams(collective_id=13, has_side_effects=True, vmem_limit_bytes=56 * 2**20),
         name="experts",
@@ -1045,10 +1098,9 @@
         return total
 
     def step(self, u):
-        u = jnp.int32(u)
         i = u // 2
-        k = far_first(i)
-        early = lax.rem(u, 2) == 0
+        k = far_first(jnp.int32(i))
+        early = u % 2 == 0
 
         @pl.when(early)
         def _():
@@ -1060,7 +1112,7 @@
             def _():
                 self.issue(1, i + 1)
 
-        @pl.when(jnp.logical_not(early))
+        @pl.when(u % 2 == 1)
         def _():
             for p in range(2):
                 total = self.dense(p, 0, k)
@@ -1103,8 +1155,9 @@
 
 
 def grads_kernel(
-    dx_ref, slots_ref, gg_ref, xi_ref, ui_ref, hg_ref, dg_ref, du_ref,
-    o_ref, back_ref, wg_out, wu_out, wd_out, xcol, ucol, gout, uout, dout, gs, gr, isem, osem, *scratch,
+    dx_ref, slots_ref, gg_ref, xi_ref, ui_ref, hg_in, dg_in, du_in,
+    o_ref, back_ref, wg_out, wu_out, wd_out, xcol, ucol, gout, uout, dout, hg_ref, dg_ref, du_ref,
+    gs, gr, isem, osem, wsem, *scratch,
 ):
     greet_all()
     swap = Swap(lambda t: gg_ref.at[t], back_ref, gs, gr)
@@ -1132,6 +1185,14 @@
 
     for cp in loads(0):
         cp.start()
+    whole = [
+        pltpu.make_async_copy(source, into, wsem.at[i])
+        for i, (source, into) in enumerate(((hg_in, hg_ref), (dg_in, dg_ref), (du_in, du_ref)))
+    ]
+    for cp in whole:
+        cp.start()
+    for cp in whole:
+        cp.wait()
 
     def one(u, _):
         @pl.when(u < 6)
@@ -1178,7 +1239,7 @@
     dma = pltpu.SemaphoreType.DMA
     return pl.pallas_call(
         grads_kernel,
-        in_specs=[hbm, vmem, vmem, hbm, hbm, vmem, vmem, vmem],
+        in_specs=[hbm, vmem, vmem, hbm, hbm, hbm, hbm, hbm],
         out_specs=[vmem, vmem, hbm, hbm, hbm],
         out_shape=[
             jax.ShapeDtypeStruct((rows, model), F32),
@@ -1190,31 +1251,129 @@
         scratch_shapes=[
             pltpu.VMEM((2, n, 256), BF16), pltpu.VMEM((2, n, 256), BF16),
             pltpu.VMEM((2, 256, ff), F32), pltpu.VMEM((2, 256, ff), F32), pltpu.VMEM((2, ff, 256), F32),
-            dma((32,)), dma((32,)), dma((2, 2)), dma((3, 2)),
+            pltpu.VMEM((n, ff), BF16), pltpu.VMEM((n, ff), BF16), pltpu.VMEM((n, ff), BF16),
+            dma((32,)), dma((32,)), dma((2, 2)), dma((3, 2)), dma((3,)),
         ] + Back.scratch(rows, model // 2),
         compiler_params=pltpu.CompilerParams(collective_id=14, has_side_effects=True, vmem_limit_bytes=56 * 2**20),
         name="grads",
     )(dx, slots, gg, xi, ui, hg, dg, du)
 
 
-def attend_mesh_kernel(
-    chunks, rows, lo_ref, q_ref, kv_ref, u_ref, mine_ref, o_ref, lse_ref, window, slots_ref, ui_ref,
-    bias, gs, gr, lsem, ws, wr, *scratch,
+BEFORE_HEADS = (
+    "w0", "rank", "w1", "v0", "w2", "v1", "w3", "v2", "v3", "bias", "gains", "norm", "u0", "u1",
+    "u2", "u3", "wend", "kv", "ag", "o0", "q", "prev", "o1", "pass", "t0", "kend",
+)
+AFTER_HEAD = ("o2", "t1", "o3", "t2", "", "t3", "", "")
+
+
+def front_kernel(
+    chunks, rows, lo_ref, cos_ref, sin_ref, x_ref, wq_ref, wk_ref, wv_ref, router_ref, u_ref, turn_ref, turn_t_ref,
+    gain_one_ref, gain_two_ref, q_out, o_ref, lse_ref, window_out, slots_ref, ui_ref, w_out, n_ref, gains_ref, scale_ref,
+    q_ref, window, w_ref, part_ref, bias, mine, kv, key_t, insem, outsem, gs, gr, lsem, ws, wr, *scratch,
 ):
+    loads, at = [], 0
+    for i, ref in enumerate((wq_ref, wk_ref, wv_ref)):
+        loads.append(pltpu.make_async_copy(ref, part_ref.at[:, pl.ds(at, ref.shape[1])], insem.at[i]))
+        at += ref.shape[1]
+    for cp in loads:
+        cp.start()
+    part_ref[:, at:] = jnp.zeros((part_ref.shape[0], part_ref.shape[1] - at), BF16)
+    part_ref[:, at : at + EXPERTS] = router_ref[...]
     greet_all()
-    swap = Swap(lambda t: mine_ref.at[t // 8], slots_ref, gs, gr)
-    keys = Window(rows, kv_ref, window, (lsem, ws, wr))
-    ag = Forth(u_ref, slots_ref, ui_ref, scratch)
-    keys.start()
-    swap.start()
-    ag.start()
-    make_bias(bias, lo_ref, chunks, rows)
-    keys.previous()
-    swap.wait_recv()
-    ag.one(0)
-    keys.pass_on()
-    ag.one(1)
-    keys.end()
+    weights = Whole(part_ref, w_ref, scratch[:7])
+    swap = Swap(lambda t: mine.at[t // 8], slots_ref, gs, gr)
+    keys = Window(rows, kv, window, (lsem, ws, wr))
+    ag = Forth(u_ref, slots_ref, ui_ref, scratch[7:])
+    cosine, sine = cos_ref[...], sin_ref[...]
+    q_width, k_width = QUERY_HEADS * HEAD_DIM, KEY_HEADS * HEAD_DIM
+
+    def rank():
+        for e in range(EXPERTS):
+            own = turn_t_ref[e : e + 1, :]
+            place_of = jnp.sum(jnp.where(turn_ref[:, e : e + 1] < own, 1.0, 0.0), axis=0, keepdims=True)
+            slot = jnp.where((own < UNPICKED) & (place_of < CAPACITY), place_of, -1.0)
+            mine[e // 8, e % 8 : e % 8 + 1, :] = slot
+        mine[:, 8:16, :] = jnp.zeros((4, 8, rows), F32)
+        for plane in range(4):
+            mine[plane, 8:9, 0 : part_ref.shape[0]] = gain_one_ref[...].astype(F32)
+            mine[plane, 9:10, 0 : part_ref.shape[0]] = gain_two_ref[...].astype(F32)
+        swap.start()
+
+    def gains():
+        swap.wait_recv()
+        part = part_ref.shape[0]
+        for t in range(32):
+            gains_ref[0:8, t * part : (t + 1) * part] = slots_ref[t, 8:16, 0:part]
+
+    def norm():
+        def some(i, _):
+            at = pl.ds(pl.multiple_of(i * 32, 32), 32)
+            values = x_ref[at, :].astype(F32)
+            scale = lax.rsqrt(jnp.mean(values * values, axis=1, keepdims=True) + EPSILON)
+            scale_ref[at, :] = scale
+            n_ref[at, :] = (values * scale * gains_ref[0:1, :]).astype(BF16)
+            return 0
+        lax.fori_loop(0, rows // 32, some, 0)
+
+    def roped(values, into, first):
+        turned = values.T
+        for n in range(256 // HEAD_DIM):
+            u = turned[n * HEAD_DIM : n * HEAD_DIM + HEAD_DIM // 2]
+            w = turned[n * HEAD_DIM + HEAD_DIM // 2 : (n + 1) * HEAD_DIM]
+            at = first + n * HEAD_DIM
+            into[pl.ds(pl.multiple_of(at, 32), 32), :] = (u * cosine - w * sine).astype(BF16)
+            into[pl.ds(pl.multiple_of(at + 32, 32), 32), :] = (w * cosine + u * sine).astype(BF16)
+
+    def keys_and_values():
+        for n in range(k_width // 256):
+            roped(dims(n_ref[...], w_ref[:, q_width + n * 256 : q_width + (n + 1) * 256], 1, 0), key_t, n * 256)
+            kv[0, :, n * 256 : (n + 1) * 256] = key_t[n * 256 : (n + 1) * 256, :].T
+        kv[1] = dims(n_ref[...], w_ref[:, q_width + k_width : QKV], 1, 0).astype(BF16)
+        keys.start()
+
+    def queries():
+        def some(i, _):
+            at = pl.ds(pl.multiple_of(i * 256, 256), 256)
+            roped(dims(n_ref[...], w_ref[:, at], 1, 0), q_ref, i * 256)
+            q_ref[at, :] = (q_ref[at, :].astype(F32) * HEAD_DIM**-0.5).astype(BF16)
+            return 0
+        lax.fori_loop(0, q_width // 256, some, 0)
+
+    def whole():
+        weights.end()
+        outs[0].start()
+
+    def queried():
+        queries()
+        outs[1].start()
+
+    def windowed():
+        keys.end()
+        outs[2].start()
+
+    outs = [
+        pltpu.make_async_copy(held, out, outsem.at[i])
+        for i, (held, out) in enumerate(((w_ref, w_out), (q_ref, q_out), (window, window_out)))
+    ]
+    step = {
+        "rank": rank, "gains": gains, "norm": norm, "kv": keys_and_values, "q": queried,
+        "ag": ag.start, "bias": lambda: make_bias(bias, lo_ref, chunks, rows), "wend": whole,
+        "prev": keys.previous, "pass": keys.pass_on, "kend": windowed,
+    }
+    for i in range(4):
+        step[f"w{i}"] = functools.partial(weights.one, i)
+        step[f"v{i}"] = functools.partial(weights.two, i)
+        step[f"u{i}"] = functools.partial(weights.three, i)
+        step[f"c{i}"] = functools.partial(ag.come, jnp.int32(i))
+        step[f"s{i}"] = functools.partial(ag.one, jnp.int32(i), False)
+        step[f"o{i}"] = functools.partial(ag.one, jnp.int32(i))
+        step[f"t{i}"] = functools.partial(ag.two, jnp.int32(i))
+
+    for cp in loads:
+        cp.wait()
+    weights.start()
+    for name in BEFORE_HEADS:
+        step[name]()
     width = 2 * GROUP * HEAD_DIM
 
     def pair(j, _):
@@ -1222,15 +1381,11 @@
         head = pl.ds(pl.multiple_of(j * width, width), width)
 
         def between(half):
-            u = 2 * j + half + 2
-
-            @pl.when((u == 3) | (u == 5))
-            def _():
-                ag.one((u + 1) // 2)
-
-            @pl.when((u == 2) | (u == 4) | (u == 6) | (u == 7))
-            def _():
-                ag.two(jnp.where(u == 7, 3, u // 2 - 1))
+            for u in range(half, 8, 2):
+                if AFTER_HEAD[u]:
+                    @pl.when(2 * j + half == u)
+                    def _(u=u):
+                        step[AFTER_HEAD[u]]()
 
         attend_pair(
             chunks, rows, lax.rem(lax.axis_index("dev"), 2), q_ref.at[head, :], window.at[:, :, lanes],
@@ -1247,41 +1402,76 @@
     ag.sent()
     keys.sent()
     swap.wait_send()
-
-
-def attend_mesh(query_t, kv, lo, upstream, mine):
-    rows = query_t.shape[1]
+    weights.sent()
+    for cp in outs:
+        cp.wait()
+
+
+def front(lo, cos_t, sin_t, tokens, projections, router, upstream, turn, gain_one, gain_two):
+    rows, model = tokens.shape
     chunks = 9
-    model = upstream.shape[1]
+    keys = KEY_HEADS * HEAD_DIM
+    part = jax.ShapeDtypeStruct((router.shape[0], -(-(QKV + EXPERTS) // 128) * 128), BF16)
     hbm, vmem = pl.BlockSpec(memory_space=pl.ANY), pl.BlockSpec(memory_space=pltpu.VMEM)
     dma = pltpu.SemaphoreType.DMA
     return pl.pallas_call(
-        functools.partial(attend_mesh_kernel, chunks, rows),
-        in_specs=[vmem] * 2 + [hbm, hbm, vmem],
-        out_specs=[vmem] * 4 + [hbm],
+        functools.partial(front_kernel, chunks, rows),
+        in_specs=[vmem] * 4 + [hbm] * 3 + [vmem, hbm] + [vmem] * 4,
+        out_specs=[hbm, vmem, vmem, hbm, vmem, hbm, hbm, vmem, vmem, vmem],
         out_shape=[
-            jax.ShapeDtypeStruct(query_t.shape, BF16),
+            jax.ShapeDtypeStruct((QUERY_HEADS * HEAD_DIM, rows), BF16),
+            jax.ShapeDtypeStruct((QUERY_HEADS * HEAD_DIM, rows), BF16),
             jax.ShapeDtypeStruct((KEY_HEADS // 2, 8, rows), F32),
-            jax.ShapeDtypeStruct((2, 10 * rows, kv.shape[2]), BF16),
-            jax.ShapeDtypeStruct((32, 8, rows), F32),
+            jax.ShapeDtypeStruct((2, 10 * rows, keys), BF16),
+            jax.ShapeDtypeStruct((32, 16, rows), F32),
             jax.ShapeDtypeStruct((32 * SLOTS, model), BF16),
+            jax.ShapeDtypeStruct((32 * part.shape[0], part.shape[1]), BF16),
+            jax.ShapeDtypeStruct((rows, model), BF16),
+            jax.ShapeDtypeStruct((8, model), F32),
+            jax.ShapeDtypeStruct((rows, 1), F32),
         ],
-        scratch_shapes=[pltpu.VMEM((chunks * rows, rows), F32), dma((32,)), dma((32,))]
-        + Window.scratch + Forth.scratch(rows, model // 2),
-        compiler_params=pltpu.CompilerParams(collective_id=16, has_side_effects=True, vmem_limit_bytes=56 * 2**20),
-        name="attend",
-    )(lo, query_t, kv, upstream, mine)
+        scratch_shapes=[
+            pltpu.VMEM((QUERY_HEADS * HEAD_DIM, rows), BF16), pltpu.VMEM((2, 10 * rows, keys), BF16),
+            pltpu.VMEM((32 * part.shape[0], part.shape[1]), BF16), pltpu.VMEM(part.shape, BF16),
+            pltpu.VMEM((chunks * rows, rows), F32), pltpu.VMEM((4, 16, rows), F32), pltpu.VMEM((2, rows, keys), BF16),
+            pltpu.VMEM((keys, rows), BF16), dma((3,)), dma((3,)), dma((32,)), dma((32,)),
+        ]
+        + Window.scratch + Whole.scratch + Forth.scratch(rows, model // 2),
+        compiler_params=pltpu.CompilerParams(collective_id=16, has_side_effects=True, vmem_limit_bytes=58 * 2**20),
+        name="front",
+    )(lo, cos_t, sin_t, tokens, *projections, router, upstream, turn, turn.T, gain_one, gain_two)
+
+
+IN_PAIRS = {0: (0,), 2: (1,), 4: (2,), 6: (3,)}
+AFTER_PAIRS = (4, "sums", 5, 6, "near", "turn", 7)
 
 
 def attend_back_mesh_kernel(
-    chunks, rows, lo_ref, cos_ref, sin_ref, q_ref, kv_ref, g_ref, lse_ref, out_ref, y_ref, slots_ref, residual_ref,
-    grad_out, layer_ref, bias, dkv, sums_ref, gt_ref, o_ref, *scratch,
+    chunks, rows, lo_ref, cos_ref, sin_ref, q_ref, kv_in, branch_ref, wo_in, lse_ref, out_ref, y_ref, slots_ref, residual_in,
+    grad_out, layer_ref, wo, g_ref, wsem, kv_ref, residual_ref, insem, bias, dkv, sums_ref, gt_ref, o_ref, *scratch,
 ):
     greet_near()
     rs = Back(y_ref, slots_ref, o_ref, scratch[: Back.n_scratch])
     keys = Unwindow(rows, dkv, sums_ref, scratch[Back.n_scratch :])
     rs.start()
+    kv_load = pltpu.make_async_copy(kv_in, kv_ref, insem.at[0])
+    residual_load = pltpu.make_async_copy(residual_in, residual_ref, insem.at[1])
+    kv_load.start()
+    residual_load.start()
+    step = wo.shape[1]
+
+    def wo_load(i):
+        return pltpu.make_async_copy(wo_in.at[pl.ds(i * step, step), :], wo.at[i % 2], wsem.at[i % 2])
+
+    wo_load(0).start()
     make_bias(bias, lo_ref, chunks, rows)
+    for i in range(wo_in.shape[0] // step):
+        if (i + 1) * step < wo_in.shape[0]:
+            wo_load(i + 1).start()
+        wo_load(i).wait()
+        g_ref[i * step : (i + 1) * step, :] = dims(wo[i % 2], branch_ref[...], 1, 1).astype(BF16)
+    kv_load.wait()
+    residual_load.wait()
     width = 2 * GROUP * HEAD_DIM
 
     def pair(j, _):
@@ -1289,8 +1479,12 @@
         head = pl.ds(pl.multiple_of(j * width, width), width)
 
         def between(half):
-            if half == 0:
-                rs.step(j)
+            for n, names in IN_PAIRS.items():
+                if n % 2 == half:
+                    @pl.when(2 * j + half == n)
+                    def _(names=names):
+                        for name in names:
+                            rs.step(name)
 
         attend_back_pair(
             chunks, rows, lax.rem(lax.axis_index("dev"), 2), cos_ref, sin_ref, q_ref.at[head, :], kv_ref.at[:, :, lanes], g_ref.at[head, :],
@@ -1299,26 +1493,21 @@
         return 0
 
     lax.fori_loop(0, KEY_HEADS // 2, pair, 0)
-    keys.start()
 
     def turned(first, last):
         for n in range(first, last, 256):
             grad_out[:, n : n + 256] = gt_ref[n : n + 256, :].T
 
-    def rest(u, _):
-        rs.step(u)
-
-        @pl.when(u == 4)
-        def _():
+    keys.start()
+    for name in AFTER_PAIRS:
+        if isinstance(name, int):
+            rs.step(name)
+        elif name == "sums":
             keys.sums()
-
-        @pl.when(u == 6)
-        def _():
+        elif name == "turn":
+            turned(0, QUERY_HEADS * HEAD_DIM)
+        else:
             keys.near()
-            turned(0, QUERY_HEADS * HEAD_DIM)
-        return 0
-
-    lax.fori_loop(4, 8, rest, 0)
     keys.end()
     base = QUERY_HEADS * HEAD_DIM
     key_t = sums_ref[0].T
@@ -1334,33 +1523,35 @@
     layer_ref[...] = (residual_ref[...] + o_ref[...]).astype(BF16)
 
 
-def attend_back_mesh(query_t, window, lo, grad_t, lse, attended_t, cos_t, sin_t, y, slots, residual):
+def attend_back_mesh(query_t, window, lo, branch_grad, output_matrix, lse, attended_t, cos_t, sin_t, y, slots, residual):
     rows, span, keys = query_t.shape[1], window.shape[1], window.shape[2]
     chunks = span // rows - 1
     model = y.shape[1]
     hbm, vmem = pl.BlockSpec(memory_space=pl.ANY), pl.BlockSpec(memory_space=pltpu.VMEM)
     return pl.pallas_call(
         functools.partial(attend_back_mesh_kernel, chunks, rows),
-        in_specs=[vmem] * 8 + [hbm, vmem, vmem],
+        in_specs=[vmem] * 4 + [hbm, vmem, hbm] + [vmem] * 2 + [hbm, vmem, hbm],
         out_specs=[vmem] * 2,
         out_shape=[
             jax.ShapeDtypeStruct((rows, QKV), BF16),
             jax.ShapeDtypeStruct((rows, model), BF16),
         ],
         scratch_shapes=[
+            pltpu.VMEM((2, 384, model), BF16), pltpu.VMEM(query_t.shape, BF16), pltpu.SemaphoreType.DMA((2,)),
+            pltpu.VMEM(window.shape, BF16), pltpu.VMEM((rows, model), F32), pltpu.SemaphoreType.DMA((2,)),
             pltpu.VMEM((chunks * rows, rows), F32), pltpu.VMEM(window.shape, BF16), pltpu.VMEM((2, rows, keys), F32),
             pltpu.VMEM((QKV, rows), BF16), pltpu.VMEM((rows, model), F32),
         ]
         + Back.scratch(rows, model // 2) + Unwindow.scratch(rows, keys),
-        compiler_params=pltpu.CompilerParams(collective_id=15, has_side_effects=True, vmem_limit_bytes=56 * 2**20),
+        compiler_params=pltpu.CompilerParams(collective_id=15, has_side_effects=True, vmem_limit_bytes=60 * 2**20),
         name="attend_back",
-    )(lo, cos_t, sin_t, query_t, window, grad_t, lse, attended_t, y, slots, residual)
+    )(lo, cos_t, sin_t, query_t, window, branch_grad, output_matrix, lse, attended_t, y, slots, residual)
 
 
 def finish_kernel(
-    rows, n_ref, g_ref, w_ref, more_ref, gain_ref, scale_ref, x_ref, rg_ref,
-    oq_ref, ok_ref, ov_ref, om_ref, tg_ref, fg_ref, dense, acc, ra, rb, rz, out, ng, mine, theirs,
-    ssem, rsem, sa, ra_sem, sb, rb_sem, sz, rz_sem, gs, gr,
+    rows, n_ref, g_ref, w_in, more_ref, gain_ref, scale_ref, x_in, rg_in,
+    oq_ref, ok_ref, ov_ref, om_ref, tg_ref, fg_ref, w_ref, x_ref, rg_ref, insem,
+    dense, acc, ra, rb, rz, out, ng, mine, theirs, ssem, rsem, sa, ra_sem, sb, rb_sem, sz, rz_sem, gs, gr,
 ):
     z, y, x, c = place()
     greet_all()
@@ -1480,7 +1671,15 @@
             mine[t, 0:1, 0:rows] = total[:, t * rows : (t + 1) * rows]
         swap.start()
 
+    loads = [
+        pltpu.make_async_copy(source, into, insem.at[i])
+        for i, (source, into) in enumerate(((w_in, w_ref), (x_in, x_ref), (rg_in, rg_ref)))
+    ]
+    for cp in loads:
+        cp.start()
     lax.fori_loop(0, 4, product, 0)
+    for cp in loads:
+        cp.wait()
 
     def steps(i, _):
         @pl.when(i < 4)
@@ -1534,17 +1733,18 @@
     main, cols = grad.shape[1], grad.shape[1] + more.shape[1]
     half = cols // 2
     dma = pltpu.SemaphoreType.DMA
-    vmem = pl.BlockSpec(memory_space=pltpu.VMEM)
+    hbm, vmem = pl.BlockSpec(memory_space=pl.ANY), pl.BlockSpec(memory_space=pltpu.VMEM)
     widths = [QUERY_HEADS * HEAD_DIM, KEY_HEADS * HEAD_DIM, KEY_HEADS * HEAD_DIM, more.shape[1]]
     return pl.pallas_call(
         functools.partial(finish_kernel, rows),
-        in_specs=[vmem] * 8,
+        in_specs=[vmem, vmem, hbm, vmem, vmem, vmem, hbm, hbm],
         out_specs=[vmem] * 6,
         out_shape=[jax.ShapeDtypeStruct((rows, w), F32) for w in widths] + [
             jax.ShapeDtypeStruct((count, model), F32),
             jax.ShapeDtypeStruct((8, 128), F32),
         ],
         scratch_shapes=[
+            pltpu.VMEM(matrices.shape, BF16), pltpu.VMEM((count, model), BF16), pltpu.VMEM((count, model), F32), dma((3,)),
             pltpu.VMEM((16, 2 * rows, main), BF16),
             pltpu.VMEM((16, rows, cols), BF16),
             pltpu.VMEM((2, 2, 4, rows, half), BF16),
@@ -1557,16 +1757,28 @@
             dma((4, 2, 2, 2)), dma((4, 2, 2, 2)), dma((2, 2, 4)), dma((2, 2, 4)), dma((2, 4)), dma((2, 4)), dma((2, 4)), dma((2, 4)),
             dma((32,)), dma((32,)),
         ],
-        compiler_params=pltpu.CompilerParams(collective_id=17, has_side_effects=True, vmem_limit_bytes=56 * 2**20),
+        compiler_params=pltpu.CompilerParams(collective_id=17, has_side_effects=True, vmem_limit_bytes=42 * 2**20),
         name="finish",
     )(normed, grad, matrices, more, gain, scale, tokens, residual_grad)
+
+
+def chunks_of(shape):
+    rows = shape[0]
+    count = 1
+    while rows % (32 * count) == 0 and rows // count * shape[1] > 2**18:
+        count *= 2
+    return [(i * (rows // count), rows // count) for i in range(count)]
 
 
 def hand_over_kernel(count, *refs):
     sources, outs, held = refs[:count], refs[count : 2 * count], refs[2 * count : 3 * count]
     sems = refs[3 * count]
-    into = [pltpu.make_async_copy(sources[i], held[i], sems.at[0, i]) for i in range(count)]
-    out = [pltpu.make_async_copy(held[i], outs[i], sems.at[1, i]) for i in range(count)]
+    into, out = [], []
+    for source, there, here in zip(sources, outs, held, strict=True):
+        for first, rows in chunks_of(source.shape):
+            at, n = pl.ds(first, rows), len(into)
+            into.append(pltpu.make_async_copy(source.at[at, :], here.at[at, :], sems.at[0, n]))
+            out.append(pltpu.make_async_copy(here.at[at, :], there.at[at, :], sems.at[1, n]))
     for cp in into:
         cp.start()
     for a, b in zip(into, out, strict=True):
@@ -1578,12 +1790,13 @@
 
 def hand_over(*arrays):
     hbm = pl.BlockSpec(memory_space=pl.ANY)
+    total = sum(len(chunks_of(a.shape)) for a in arrays)
     return pl.pallas_call(
         functools.partial(hand_over_kernel, len(arrays)),
         in_specs=[hbm] * len(arrays),
         out_specs=[hbm] * len(arrays),
         out_shape=[jax.ShapeDtypeStruct(a.shape, a.dtype) for a in arrays],
-        scratch_shapes=[pltpu.VMEM(a.shape, a.dtype) for a in arrays] + [pltpu.SemaphoreType.DMA((2, len(arrays)))],
+        scratch_shapes=[pltpu.VMEM(a.shape, a.dtype) for a in arrays] + [pltpu.SemaphoreType.DMA((2, total))],
         compiler_params=pltpu.CompilerParams(vmem_limit_bytes=60 * 2**20),
         name="hand_over",
     )(*arrays)
@@ -1599,12 +1812,6 @@
     u, w = shaped[:, 0], shaped[:, 1]
     turned = jnp.stack([u * cosine - w * sine, w * cosine + u * sine], axis=1)
     return turned.reshape(values.shape)
-
-
-def gathered(block, cid, by_rows):
-    if meshed():
-        return gather_all(block, cid, by_rows)
-    return lax.all_gather(block, "dev", axis=0, tiled=True)
 
 
 def on_device(
@@ -1632,46 +1839,43 @@
 
     output_matrix = lax.all_gather(output_weight, "dev", axis=0, tiled=True)
 
-    extra = jnp.concatenate([router_weight, first_gain[:, None], second_gain[:, None]], axis=1)
-    pad = (-extra.shape[1]) % 128
-    packed = jnp.concatenate(
-        [query_weight, key_projection_matrix, value_projection_matrix, extra, jnp.zeros((weight_rows, pad), BF16)],
-        axis=1,
-    )
-    matrices = gathered(packed, 1, False)
-    qkv_matrix = matrices[:, :QKV]
-    router_matrix = matrices[:, QKV : QKV + EXPERTS]
-    gain_first = matrices[:, QKV + EXPERTS].astype(F32)
-    gain_second = matrices[:, QKV + EXPERTS + 1].astype(F32)
-
-    one_hot = expert_picks[:, :, None] == jnp.arange(EXPERTS, dtype=jnp.int32)
-    picked_any = jnp.any(one_hot, axis=1)
-    turn = jnp.sum(jnp.where(one_hot, priority[:, :, None], 0), axis=1)
-    turn = jnp.where(picked_any, turn, jnp.int32(2**30)).T
-    rank = jnp.sum((turn[:, None, :] < turn[:, :, None]).astype(jnp.int32), axis=2)
-    slot_rows = jnp.where(picked_any.T & (rank < capacity), rank, -1).astype(F32)
-
+    extra = [query_weight, key_projection_matrix, value_projection_matrix, router_weight]
+    pad = (-(QKV + EXPERTS)) % 128
+    packed = jnp.concatenate(extra + [jnp.zeros((weight_rows, pad), BF16)], axis=1)
+    q_width, k_width = QUERY_HEADS * HEAD_DIM, KEY_HEADS * HEAD_DIM
     inputs = tokens.astype(F32)
-    scale_one = rms_scale(inputs)
-    normed_one = (inputs * scale_one * gain_first).astype(BF16)
     half_dim = HEAD_DIM // 2
     frequency = jnp.power(10000.0, -(jnp.arange(half_dim, dtype=F32) * 2.0) / HEAD_DIM)
     angle = positions.astype(F32)[None, :] * frequency[:, None]
     cos_t, sin_t = jnp.cos(angle), jnp.sin(angle)
-    qkv_t = dims(qkv_matrix, normed_one, 0, 1)
-    q_width, k_width = QUERY_HEADS * HEAD_DIM, KEY_HEADS * HEAD_DIM
-    query_t = rotate_t(qkv_t[:q_width], cos_t, sin_t).astype(BF16) * BF16(HEAD_DIM**-0.5)
-    key = rotate_t(qkv_t[q_width : q_width + k_width], cos_t, sin_t).astype(BF16).T
-    value = qkv_t[q_width + k_width :].astype(BF16).T
-    kv = jnp.stack([key, value])
     lo = (jnp.arange(rows, dtype=jnp.int32) - positions)[None, :]
+    one_hot = expert_picks[:, :, None] == jnp.arange(EXPERTS, dtype=jnp.int32)
+    picked_any = jnp.any(one_hot, axis=1)
+    turn = jnp.sum(jnp.where(one_hot, priority[:, :, None], 0), axis=1).astype(F32)
+    turn = jnp.where(picked_any, turn, UNPICKED)
+
     if meshed():
-        attended_t, lse, window, plane_slots, expert_up = attend_mesh(
-            query_t, kv, lo, cotangent, slot_rows.reshape(-1, 8, rows)
+        query_t, attended_t, lse, window, plane_slots, expert_up, matrices, normed_one, gains, scale_one = front(
+            lo, cos_t, sin_t, tokens, extra[:3], router_weight, cotangent, turn, first_gain[None, :], second_gain[None, :]
         )
+        gain_first, gain_second = gains[0], gains[1]
     else:
-        window, offset = window_of(kv), jnp.int32(0)
+        matrices, gain_first, gain_second = (
+            lax.all_gather(v, "dev", axis=0, tiled=True) for v in (packed, first_gain, second_gain)
+        )
+        gain_first, gain_second = gain_first.astype(F32), gain_second.astype(F32)
+        rank = jnp.sum((turn.T[:, None, :] < turn.T[:, :, None]).astype(jnp.int32), axis=2)
+        slot_rows = jnp.where(picked_any.T & (rank < capacity), rank, -1).astype(F32)
+        scale_one = rms_scale(inputs)
+        normed_one = (inputs * scale_one * gain_first).astype(BF16)
+        qkv_t = dims(matrices[:, :QKV], normed_one, 0, 1)
+        query_t = rotate_t(qkv_t[:q_width], cos_t, sin_t).astype(BF16) * BF16(HEAD_DIM**-0.5)
+        key = rotate_t(qkv_t[q_width : q_width + k_width], cos_t, sin_t).astype(BF16).T
+        value = qkv_t[q_width + k_width :].astype(BF16).T
+        window, offset = window_of(jnp.stack([key, value])), jnp.int32(0)
         attended_t, lse = attend(query_t, window, offset, lo)
+    qkv_matrix = matrices[:, :QKV]
+    router_matrix = matrices[:, QKV : QKV + EXPERTS]
     residual = inputs + dims(attended_t, output_matrix, 0, 0)
     scale_two = rms_scale(residual)
     normed_two = (residual * scale_two * gain_second).astype(BF16)
@@ -1744,13 +1948,13 @@
     branch_grad = residual_grad.astype(BF16)
     output_gradient = dims(attended_t, branch_grad, 1, 0).astype(BF16)
     output_gradient = lax.psum_scatter(output_gradient, "dev", scatter_dimension=0, tiled=True).astype(F32)
-    grad_t = dims(output_matrix, branch_grad, 1, 1).astype(BF16)
 
     if meshed():
         qkv_grad, layer_output = attend_back_mesh(
-            query_t, window, lo, grad_t, lse, attended_t, cos_t, sin_t, out_rows, plane_slots, residual
+            query_t, window, lo, branch_grad, output_matrix, lse, attended_t, cos_t, sin_t, out_rows, plane_slots, residual
         )
     else:
+        grad_t = dims(output_matrix, branch_grad, 1, 1).astype(BF16)
         query_grad_t, window_grad = attend_back(query_t, window, offset, lo, grad_t, lse, attended_t, cos_t, sin_t)
         key_grad, value_grad = unwindow(window_grad)
         key_grad_t = rotate_t(key_grad.T, cos_t, -sin_t).astype(BF16)

time: 662 us -> 633 us (0.956)
  Pallas kernels: 593 us -> 580 us
  matrix products: 22.4 us -> 11.8 us
    pallas_call x5 -> x4, Pallas kernels: 453 us -> 439 us  [the longest x1 184 us: front(): pl.pallas_call(functools.partial(front_kernel, chunks, rows), in_specs=[v...]
    dot_general x7 -> x5, matrix products: 22.4 us -> 11.8 us  [dims(): lax.dot_general(a, b, (((ca,), (cb,)), ((), ())), preferred_element_type=...]
  transfers between devices with their start and end apart: 2 -> 2, of which waited for: 0 -> 0; matrix products, arithmetic and copies ran while one was open for 5% -> 2% of each run, Pallas kernels for 57% -> 60%
where the time goes in v5:
time: 633 us; the launch traced here: 629 us
  Pallas kernels  580 us (92%)
  between operations  14.6 us (2%)
  local copies, waits for them, and re-layouts  12.9 us (2%)
  matrix products  11.8 us (2%)
  other arithmetic  9.05 us (1%)
    pallas_call x1, Pallas kernels, front(): pl.pallas_call(functools.partial(front_kernel, chunks, rows), in_specs=[v...  184 us
    pallas_call x1, Pallas kernels, attend_back_mesh(): pl.pallas_call(functools.partial(attend_back_mesh_kernel, chunks, rows),...  132 us
    pallas_call x1, Pallas kernels, run_experts(): pl.pallas_call(experts_kernel, in_specs=[hbm, vmem, vmem, hbm, hbm, hbm,...  103 us
    pallas_call x1, Pallas kernels, run_grads(): pl.pallas_call(grads_kernel, in_specs=[hbm, vmem, vmem, hbm, hbm, hbm, hb...  99.8 us
    pallas_call x1, Pallas kernels, finish(): pl.pallas_call(functools.partial(finish_kernel, rows), in_specs=[vmem, vm...  51.6 us
  transfers between devices with their start and end apart: 2, of which 0 were waited for; matrix products, arithmetic and copies ran while one was open for 2% of the time, Pallas kernels for 60%

profile of v5, /device:TPU:0, one launch (start us, length us, event | category | flops | bytes accessed | tf_op | source)
XLA Modules:
  0.0 629.1 jit_solution(5066303028887898626)
XLA Ops:
  7.2 0.0 copy-start
  7.2 0.0 all-gather.2.cloned.1.call-start
  7.2 0.7 all-gather.2.cloned.1.call-update
  7.9 0.0 reduce-scatter.2.cloned.1.call-start
  8.0 0.7 fusion.2
  8.7 0.8 select_reduce_fusion
  9.5 0.0 copy-start.14
  9.5 0.8 copy.46.turn_ref
  10.2 1.4 copy.45.router_ref
  11.6 1.3 fusion.13
  13.0 0.8 multiply_sine_fusion
  13.8 0.0 copy-done.14
  13.8 184.5 %front.1 = (bf16[1536,256]{1,0:T(8,128)(2,1)}, bf16[1536,256]{1,0:T(8,128)(2,1)}, f32[4,8,256]{2,1,0:T(8,128)}, bf16[2,2560,512]{2,1,0:T(8,128)(2,1)}, f32[32,16...) custom-call(s32[1,256]{1,0:T(1,128)} %bitcast.44, ...), custom_call_target="tpu_custom_call" | custom-call | tf_op jit(solution)/shard_map/front/pallas_call | solution.py:1417
  198.3 0.9 fusion.12
  199.2 0.0 all-gather.2.cloned.1.call-done.wo_in
  199.2 0.0 copy-done
  199.2 4.1 multiply_reduce_fusion.2
  203.3 0.0 copy-start.8
  203.3 0.2 multiply_convert_fusion.x_ref
  203.5 0.0 copy-start.10
  203.5 1.7 fusion.14
  205.3 0.7 pad.4.gates_ref
  205.9 0.0 copy-done.10
  205.9 102.9 %experts.1 = (bf16[2560,1536]{1,0:T(8,128)(2,1)}, bf16[2560,1536]{1,0:T(8,128)(2,1)}, bf16[2560,1536]{1,0:T(8,128)(2,1)}, bf16[2560,512]{1,0:T(8,128)(2,1)}, bf1...) custom-call(bf16[256,1536]{1,0:T(8,128)(2,1)} %copy-done.10, ...), custom_call_target="tpu_custom_call" | custom-call | tf_op jit(solution)/shard_map/experts/pallas_call | solution.py:993
  308.8 99.8 %grads.1 = (f32[256,1536]{1,0:T(8,128)}, f32[32,8,128]{2,1,0:T(8,128)}, f32[1536,512]{1,0:T(8,128)}, f32[1536,512]{1,0:T(8,128)}, f32[512,1536]{1,0:T(8,128)}) custom-call(bf16[2560,1536]{1,0:T(8,128)(2,1)} %get-tuple-element.55.dx_ref, f32[32,16,256]{2,1,0:T(8,128)} %get-tuple-element.53.slots_ref, f32[32,8,128]{2,1,0:T(8,128)} %get-tuple-element.56.gg_ref, ...), custom_call_target="tpu_custom_call" | custom-call | tf_op jit(solution)/shard_map/grads/pallas_call | solution.py:1240
  408.7 0.9 slice.23
  409.6 0.0 copy-done.8
  409.6 0.0 copy-start.13
  409.7 2.3 multiply_reduce_fusion
  412.0 0.0 copy-done.13
  412.0 0.0 copy-start.9
  412.0 2.0 fusion.11
  414.0 0.0 copy-start.12
  414.0 0.9 copy-done.12
  414.9 0.0 copy-done.9
  414.9 3.5 convolution_convert_fusion
  418.4 0.0 copy-start.11
  418.4 0.0 reduce-scatter.2.cloned.1.call-update
  418.4 0.1 pad.7.clone
  418.5 1.0 copy-done.11
  419.5 0.2 convolution_convert_fusion.1
  419.8 0.9 copy.47
  420.7 0.3 broadcast_in_dim.54
  421.0 0.0 copy-start.3
  421.0 132.1 %attend_back.1 = (bf16[256,2560]{1,0:T(8,128)(2,1)}, bf16[256,1536]{1,0:T(8,128)(2,1)}) custom-call(s32[1,256]{1,0:T(1,128)} %bitcast.45, f32[32,256]{1,0:T(8,128)} %get-tuple-element.143.cos_ref, f32[32,256]{1,0:T(8,128)} %get-tuple-element.142.sin_ref, bf16[1536,256]{1,0:T(8,128)(2,1)} %get-tuple-element.64.q_ref, ...), custom_call_target="tpu_custom_call" | custom-call | tf_op jit(solution)/shard_map/attend_back/pallas_call | solution.py:1531
  553.1 0.0 copy-start.2
  553.1 0.0 copy-start.5
  553.1 1.5 maximum_maximum_fusion.more_ref
  554.6 0.0 copy-done.3
  554.6 0.0 copy-done.2
  554.6 0.0 copy-done.5
  554.7 51.6 %finish.1 = (f32[48,1536]{1,0:T(8,128)S(1)}, f32[48,512]{1,0:T(8,128)S(1)}, f32[48,512]{1,0:T(8,128)S(1)}, f32[48,256]{1,0:T(8,128)S(1)}, f32[256,1536]{1,0:T(8,128)S(1)}, /*index=5*/f32[8,128]{1,0:T(8,128)S(1)}) custom-call(bf16[256,1536]{1,0:T(8,128)(2,1)S(1)} %copy-done.3, bf16[256,2560]{1,0:T(8,128)(2,1)S(1)} %copy-done.2, ...), custom_call_target="tpu_custom_call" | custom-call | tf_op jit(solution)/shard_map/finish/pallas_call | solution.py:1738
  606.2 0.0 copy-start.1
  606.2 1.2 copy-done.1
  607.4 0.0 copy-start.4
  607.4 0.7 copy-done.4
  608.1 0.0 copy-start.6
  608.1 0.6 copy-done.6
  608.8 0.6 copy-done.7
  609.4 0.7 copy.49
  610.1 9.1 %hand_over.1 = (f32[1536,512]{1,0:T(8,128)}, f32[1536,512]{1,0:T(8,128)}, f32[512,1536]{1,0:T(8,128)}, bf16[256,1536]{1,0:T(8,128)(2,1)}, f32[256,1536]{1,0:T(8,...) custom-call(f32[1536,512]{1,0:T(8,128)} %get-tuple-element.61.refs_0_, ...), custom_call_target="tpu_custom_call" | custom-call | tf_op jit(solution)/shard_map/hand_over/pallas_call | solution.py:1794
  619.2 0.7 slice_reduce_fusion
  619.9 0.5 slice_bitcast_fusion
  620.4 1.6 convert_element_type.40
  (13 shorter events, 0.2 us)
Async XLA Ops:
  7.2 192.0 %copy-start = (bf16[256,1536]{1,0:T(8,128)(2,1)S(1)}, bf16[256,1536]{1,0:T(8,128)(2,1)}, u32[]{:S(2)}) copy-start(bf16[256,1536]{1,0:T(8,128)(2,1)} %x_in.1) | copy-start | bytes 2359300
  7.2 192.0 %all-gather.2.cloned.1.call-start = ((), (), s32[]{:S(2)}) async-start(), calls=%async_computation.1 | async-start | bytes 4866048 | tf_op jit(solution)/shard_map/all_gather | solution.py:1840
  7.9 612.5 %reduce-scatter.2.cloned.1.call-start = ((), (), s32[]{:S(2)}) async-start(), calls=%async_computation.2 | async-start | bytes 4866048 | tf_op jit(solution)/shard_map/reduce_scatter | solution.py:1950
  9.5 4.3 copy-start.14
  203.3 206.4 %copy-start.8 = (f32[256,1536]{1,0:T(8,128)}, f32[256,1536]{1,0:T(8,128)S(1)}, u32[]{:S(2)}) copy-start(f32[256,1536]{1,0:T(8,128)S(1)} %get-tuple-element.149.residual_in) | copy-start | bytes 4718596
  203.5 2.4 copy-start.10
  409.6 2.4 copy-start.13
  412.0 2.9 copy-start.9
  414.0 0.9 copy-start.12
  418.4 1.1 copy-start.11
  421.0 133.7 %copy-start.3 = (bf16[256,1536]{1,0:T(8,128)(2,1)S(1)}, bf16[256,1536]{1,0:T(8,128)(2,1)}, u32[]{:S(2)}) copy-start(bf16[256,1536]{1,0:T(8,128)(2,1)} %get-tuple-element.71.n_ref) | copy-start | bytes 2359300
  553.1 1.5 copy-start.2
  553.1 1.5 copy-start.5
  606.2 1.2 copy-start.1
  607.4 0.7 copy-start.4
  608.1 0.6 copy-start.6
  608.8 0.6 copy-start.7
Sparse Core Ops, SparseCore 0:
  10.9 82.1 all-gather.1
  418.5 143.3 reduce-scatter.1

commit v6 on v5

--- a/solution.py
+++ b/solution.py
@@ -1066,14 +1066,32 @@
             src_ref=self.sout.at[p, k], dst_ref=self.rb.at[p, k], send_sem=self.bs.at[p, k], recv_sem=self.br.at[p, k],
             device_id=(target,), device_id_type=MESH)
 
+    def order(self, i):
+        return jnp.where(self.z < 2, 3 - i, lax.rem(i + 1, 4))
+
+    def relay(self, k):
+        zz = lax.rem(self.z + k, 4)
+        adds = ((self.z == 1) & (zz >= 2)) | ((self.z == 2) & (zz <= 1))
+        return adds, 2 + jnp.where(zz >= 2, zz - 2, 1 - zz)
+
     def third(self, p, k):
-        target = number(lax.rem(self.z + k, 4), self.y, self.x, self.c)
+        z = self.z
+        zz = lax.rem(z + k, 4)
+        to = jnp.where(z == 0, 1, jnp.where(z == 3, 2, zz))
+        passed = ((z == 0) & (zz >= 2)) | ((z == 3) & (zz <= 1))
+        last = ((z == 2) & (zz <= 1)) | ((z == 3) & (zz == 2)) | ((z == 1) & (zz == 3))
+        slot = jnp.where(passed, 2 + jnp.where(zz >= 2, zz - 2, 1 - zz), jnp.where(last, 1, 0))
         return pltpu.make_async_remote_copy(
-            src_ref=self.zout.at[p, k], dst_ref=self.rz.at[p, k], send_sem=self.zs.at[p, k], recv_sem=self.zr.at[p, k],
-            device_id=(target,), device_id_type=MESH)
+            src_ref=self.zout.at[p, k], dst_ref=self.rz.at[p, slot], send_sem=self.zs.at[p, k], recv_sem=self.zr.at[p, slot],
+            device_id=(number(to, self.y, self.x, self.c),), device_id_type=MESH)
+
+    def along(self, p, slot):
+        return pltpu.make_async_remote_copy(
+            src_ref=self.zout.at[p, 0], dst_ref=self.rz.at[p, slot], send_sem=self.zs.at[p, 0], recv_sem=self.zr.at[p, slot],
+            device_id=(number(self.z, self.y, self.x, 1 - self.c),), device_id_type=MESH)
 
     def issue(self, h, i):
-        k = far_first(i)
+        k = self.order(i)
         for p in range(2):
             for t in (1, 2, 0):
                 self.to(p, t, h, k).start()
@@ -1099,7 +1117,7 @@
 
     def step(self, u):
         i = u // 2
-        k = far_first(jnp.int32(i))
+        k = self.order(jnp.int32(i))
         early = u % 2 == 0
 
         @pl.when(early)
@@ -1119,7 +1137,15 @@
                 self.second(p, k).wait_recv()
                 total = total + self.rb[p, k].astype(F32)
 
-                @pl.when(k > 0)
+                adds, slot = self.relay(k)
+
+                @pl.when((k > 0) & adds)
+                def _(p=p, total=total):
+                    self.along(p, slot).wait_recv()
+                    self.zout[p, k] = (total + self.rz[p, slot].astype(F32)).astype(BF16)
+                    self.third(p, k).start()
+
+                @pl.when((k > 0) & jnp.logical_not(adds))
                 def _(p=p, total=total):
                     self.zout[p, k] = total.astype(BF16)
                     self.third(p, k).start()
@@ -1134,11 +1160,9 @@
 
     def finish(self):
         for p in range(2):
-            for k in range(1, 4):
-                self.third(p, k).wait_recv()
-            self.o_ref[:, self.cols[p]] += (
-                self.rz[p, 1].astype(F32) + self.rz[p, 2].astype(F32) + self.rz[p, 3].astype(F32)
-            )
+            for slot in range(2):
+                self.along(p, slot).wait_recv()
+            self.o_ref[:, self.cols[p]] += self.rz[p, 0].astype(F32) + self.rz[p, 1].astype(F32)
 
         def one(k, _):
             for p in range(2):

time: 633 us -> 621 us (0.981)
  Pallas kernels: 580 us -> 567 us
    pallas_call x1, Pallas kernels: 99.8 us -> 88.9 us  [run_grads(): pl.pallas_call(grads_kernel, in_specs=[hbm, vmem, vmem, hbm, hbm, hbm, hb...]
  transfers between devices with their start and end apart: 2 -> 2, of which waited for: 0 -> 0; matrix products, arithmetic and copies ran while one was open for 2% -> 2% of each run, Pallas kernels for 60% -> 61%
where the time goes in v6:
time: 621 us; the launch traced here: 616 us
  Pallas kernels  567 us (91%)
  between operations  14.6 us (2%)
  local copies, waits for them, and re-layouts  12.9 us (2%)
  matrix products  11.8 us (2%)
  other arithmetic  9.05 us (1%)
    pallas_call x1, Pallas kernels, front(): pl.pallas_call(functools.partial(front_kernel, chunks, rows), in_specs=[v...  184 us
    pallas_call x1, Pallas kernels, attend_back_mesh(): pl.pallas_call(functools.partial(attend_back_mesh_kernel, chunks, rows),...  129 us
    pallas_call x1, Pallas kernels, run_experts(): pl.pallas_call(experts_kernel, in_specs=[hbm, vmem, vmem, hbm, hbm, hbm,...  103 us
    pallas_call x1, Pallas kernels, run_grads(): pl.pallas_call(grads_kernel, in_specs=[hbm, vmem, vmem, hbm, hbm, hbm, hb...  88.9 us
    pallas_call x1, Pallas kernels, finish(): pl.pallas_call(functools.partial(finish_kernel, rows), in_specs=[vmem, vm...  52.6 us
  transfers between devices with their start and end apart: 2, of which 0 were waited for; matrix products, arithmetic and copies ran while one was open for 2% of the time, Pallas kernels for 61%

profile of v6, /device:TPU:0, one launch (start us, length us, event | category | flops | bytes accessed | tf_op | source)
XLA Modules:
  0.0 616.5 jit_solution(16382789957479388712)
XLA Ops:
  7.2 0.0 copy-start
  7.2 0.0 all-gather.2.cloned.1.call-start
  7.2 0.7 all-gather.2.cloned.1.call-update
  7.9 0.0 reduce-scatter.2.cloned.1.call-start
  8.0 0.7 fusion.2
  8.7 0.8 select_reduce_fusion
  9.5 0.0 copy-start.14
  9.5 0.8 copy.46.turn_ref
  10.2 1.4 copy.45.router_ref
  11.6 1.3 fusion.13
  13.0 0.8 multiply_sine_fusion
  13.8 0.0 copy-done.14
  13.8 184.5 %front.1 = (bf16[1536,256]{1,0:T(8,128)(2,1)}, bf16[1536,256]{1,0:T(8,128)(2,1)}, f32[4,8,256]{2,1,0:T(8,128)}, bf16[2,2560,512]{2,1,0:T(8,128)(2,1)}, f32[32,16...) custom-call(s32[1,256]{1,0:T(1,128)} %bitcast.44, ...), custom_call_target="tpu_custom_call" | custom-call | tf_op jit(solution)/shard_map/front/pallas_call | solution.py:1441
  198.2 0.9 fusion.12
  199.1 0.0 all-gather.2.cloned.1.call-done.wo_in
  199.2 0.0 copy-done
  199.2 4.1 multiply_reduce_fusion.2
  203.3 0.0 copy-start.8
  203.3 0.2 multiply_convert_fusion.x_ref
  203.5 0.0 copy-start.10
  203.5 1.7 fusion.14
  205.2 0.7 pad.4.gates_ref
  205.9 0.0 copy-done.10
  205.9 102.8 %experts.1 = (bf16[2560,1536]{1,0:T(8,128)(2,1)}, bf16[2560,1536]{1,0:T(8,128)(2,1)}, bf16[2560,1536]{1,0:T(8,128)(2,1)}, bf16[2560,512]{1,0:T(8,128)(2,1)}, bf1...) custom-call(bf16[256,1536]{1,0:T(8,128)(2,1)} %copy-done.10, ...), custom_call_target="tpu_custom_call" | custom-call | tf_op jit(solution)/shard_map/experts/pallas_call | solution.py:993
  308.7 88.9 %grads.1 = (f32[256,1536]{1,0:T(8,128)}, f32[32,8,128]{2,1,0:T(8,128)}, f32[1536,512]{1,0:T(8,128)}, f32[1536,512]{1,0:T(8,128)}, f32[512,1536]{1,0:T(8,128)}) custom-call(bf16[2560,1536]{1,0:T(8,128)(2,1)} %get-tuple-element.55.dx_ref, f32[32,16,256]{2,1,0:T(8,128)} %get-tuple-element.53.slots_ref, f32[32,8,128]{2,1,0:T(8,128)} %get-tuple-element.56.gg_ref, ...), custom_call_target="tpu_custom_call" | custom-call | tf_op jit(solution)/shard_map/grads/pallas_call | solution.py:1264
  397.6 0.9 slice.23
  398.6 0.0 copy-done.8
  398.6 0.0 copy-start.13
  398.6 2.3 multiply_reduce_fusion
  401.0 0.0 copy-done.13
  401.0 0.0 copy-start.9
  401.0 2.0 fusion.11
  403.0 0.0 copy-start.12
  403.0 0.9 copy-done.12
  403.9 0.0 copy-done.9
  403.9 3.5 convolution_convert_fusion
  407.4 0.0 copy-start.11
  407.4 0.0 reduce-scatter.2.cloned.1.call-update
  407.4 0.1 pad.7.clone
  407.5 1.0 copy-done.11
  408.5 0.2 convolution_convert_fusion.1
  408.7 0.9 copy.47
  409.7 0.3 broadcast_in_dim.54
  409.9 0.0 copy-start.3
  410.0 129.4 %attend_back.1 = (bf16[256,2560]{1,0:T(8,128)(2,1)}, bf16[256,1536]{1,0:T(8,128)(2,1)}) custom-call(s32[1,256]{1,0:T(1,128)} %bitcast.45, f32[32,256]{1,0:T(8,128)} %get-tuple-element.143.cos_ref, f32[32,256]{1,0:T(8,128)} %get-tuple-element.142.sin_ref, bf16[1536,256]{1,0:T(8,128)(2,1)} %get-tuple-element.64.q_ref, ...), custom_call_target="tpu_custom_call" | custom-call | tf_op jit(solution)/shard_map/attend_back/pallas_call | solution.py:1555
  539.4 0.0 copy-start.2
  539.4 0.0 copy-start.5
  539.4 1.5 maximum_maximum_fusion.more_ref
  540.9 0.0 copy-done.3
  540.9 0.0 copy-done.2
  540.9 0.0 copy-done.5
  540.9 52.6 %finish.1 = (f32[48,1536]{1,0:T(8,128)S(1)}, f32[48,512]{1,0:T(8,128)S(1)}, f32[48,512]{1,0:T(8,128)S(1)}, f32[48,256]{1,0:T(8,128)S(1)}, f32[256,1536]{1,0:T(8,128)S(1)}, /*index=5*/f32[8,128]{1,0:T(8,128)S(1)}) custom-call(bf16[256,1536]{1,0:T(8,128)(2,1)S(1)} %copy-done.3, bf16[256,2560]{1,0:T(8,128)(2,1)S(1)} %copy-done.2, ...), custom_call_target="tpu_custom_call" | custom-call | tf_op jit(solution)/shard_map/finish/pallas_call | solution.py:1762
  593.6 0.0 copy-start.1
  593.6 1.2 copy-done.1
  594.8 0.0 copy-start.4
  594.8 0.7 copy-done.4
  595.5 0.0 copy-start.6
  595.5 0.6 copy-done.6
  596.1 0.6 copy-done.7
  596.8 0.7 copy.49
  597.4 9.1 %hand_over.1 = (f32[1536,512]{1,0:T(8,128)}, f32[1536,512]{1,0:T(8,128)}, f32[512,1536]{1,0:T(8,128)}, bf16[256,1536]{1,0:T(8,128)(2,1)}, f32[256,1536]{1,0:T(8,...) custom-call(f32[1536,512]{1,0:T(8,128)} %get-tuple-element.61.refs_0_, ...), custom_call_target="tpu_custom_call" | custom-call | tf_op jit(solution)/shard_map/hand_over/pallas_call | solution.py:1818
  606.5 0.7 slice_reduce_fusion
  607.2 0.5 slice_bitcast_fusion
  607.7 1.6 convert_element_type.40
  (13 shorter events, 0.2 us)
Async XLA Ops:
  7.2 192.0 %copy-start = (bf16[256,1536]{1,0:T(8,128)(2,1)S(1)}, bf16[256,1536]{1,0:T(8,128)(2,1)}, u32[]{:S(2)}) copy-start(bf16[256,1536]{1,0:T(8,128)(2,1)} %x_in.1) | copy-start | bytes 2359300
  7.2 192.0 %all-gather.2.cloned.1.call-start = ((), (), s32[]{:S(2)}) async-start(), calls=%async_computation.1 | async-start | bytes 4866048 | tf_op jit(solution)/shard_map/all_gather | solution.py:1864
  7.9 599.8 %reduce-scatter.2.cloned.1.call-start = ((), (), s32[]{:S(2)}) async-start(), calls=%async_computation.2 | async-start | bytes 4866048 | tf_op jit(solution)/shard_map/reduce_scatter | solution.py:1974
  9.5 4.3 copy-start.14
  203.3 195.4 %copy-start.8 = (f32[256,1536]{1,0:T(8,128)}, f32[256,1536]{1,0:T(8,128)S(1)}, u32[]{:S(2)}) copy-start(f32[256,1536]{1,0:T(8,128)S(1)} %get-tuple-element.149.residual_in) | copy-start | bytes 4718596
  203.5 2.4 copy-start.10
  398.6 2.4 copy-start.13
  401.0 2.9 copy-start.9
  403.0 0.9 copy-start.12
  407.4 1.1 copy-start.11
  409.9 131.0 %copy-start.3 = (bf16[256,1536]{1,0:T(8,128)(2,1)S(1)}, bf16[256,1536]{1,0:T(8,128)(2,1)}, u32[]{:S(2)}) copy-start(bf16[256,1536]{1,0:T(8,128)(2,1)} %get-tuple-element.71.n_ref) | copy-start | bytes 2359300
  539.4 1.5 copy-start.2
  539.4 1.5 copy-start.5
  593.6 1.2 copy-start.1
  594.8 0.7 copy-start.4
  595.5 0.6 copy-start.6
  596.1 0.6 copy-start.7
Sparse Core Ops, SparseCore 0:
  10.9 82.1 all-gather.1
  407.5 133.2 reduce-scatter.1

commit v7 on v6

--- a/solution.py
+++ b/solution.py
@@ -1617,16 +1617,28 @@
             src_ref=acc.at[lane(dy, dx, k), :, pieces[p]], dst_ref=rb.at[p, k],
             send_sem=sb.at[p, k], recv_sem=rb_sem.at[p, k], device_id=(around[1 - p],), device_id_type=MESH)
 
+    def order(i):
+        return jnp.where(z < 2, 3 - i, lax.rem(i + 1, 4))
+
     def third(p, k):
+        zz = lax.rem(z + k, 4)
+        to = jnp.where(z == 0, 1, jnp.where(z == 3, 2, zz))
+        passed = ((z == 0) & (zz >= 2)) | ((z == 3) & (zz <= 1))
+        last = ((z == 2) & (zz <= 1)) | ((z == 3) & (zz == 2)) | ((z == 1) & (zz == 3))
+        slot = jnp.where(passed, 2 + jnp.where(zz >= 2, zz - 2, 1 - zz), jnp.where(last, 1, 0))
         return pltpu.make_async_remote_copy(
-            src_ref=acc.at[lane(0, 0, k), :, pieces[p]], dst_ref=rz.at[p, k],
-            send_sem=sz.at[p, k], recv_sem=rz_sem.at[p, k],
-            device_id=(number(lax.rem(z + k, 4), y, x, c),), device_id_type=MESH)
+            src_ref=acc.at[lane(0, 0, k), :, pieces[p]], dst_ref=rz.at[p, slot],
+            send_sem=sz.at[p, k], recv_sem=rz_sem.at[p, slot], device_id=(number(to, y, x, c),), device_id_type=MESH)
+
+    def along(p, slot):
+        return pltpu.make_async_remote_copy(
+            src_ref=acc.at[lane(0, 0, 0), :, pieces[p]], dst_ref=rz.at[p, slot],
+            send_sem=sz.at[p, 0], recv_sem=rz_sem.at[p, slot], device_id=(sibling,), device_id_type=MESH)
 
     quarter = ((1, 1), (1, 0), (0, 1), (0, 0))
 
     def product(i, _):
-        k = far_first(i)
+        k = order(i)
         zz = lax.rem(z + k, 4)
         at = pl.ds(pl.multiple_of(zz * 8 * rows, 128), 8 * rows)
         part = dims(n_ref[:, at], g_ref[...], 0, 0).astype(BF16)
@@ -1669,7 +1681,17 @@
             block = acc.at[lane(0, 0, k), :, pieces[p]]
             total = block[...].astype(F32) + ra[p, 0, k].astype(F32) + rb[p, k].astype(F32)
 
-            @pl.when(k > 0)
+            zz = lax.rem(z + k, 4)
+            adds = ((z == 1) & (zz >= 2)) | ((z == 2) & (zz <= 1))
+            slot = 2 + jnp.where(zz >= 2, zz - 2, 1 - zz)
+
+            @pl.when((k > 0) & adds)
+            def _(p=p, block=block, total=total):
+                along(p, slot).wait_recv()
+                block[...] = (total + rz[p, slot].astype(F32)).astype(BF16)
+                third(p, k).start()
+
+            @pl.when((k > 0) & jnp.logical_not(adds))
             def _(p=p, block=block, total=total):
                 block[...] = total.astype(BF16)
                 third(p, k).start()
@@ -1708,27 +1730,27 @@
     def steps(i, _):
         @pl.when(i < 4)
         def _():
-            own_sums(far_first(i))
+            own_sums(order(i))
 
         @pl.when(i == 3)
         def _():
             rest_of_tokens()
 
-        @pl.when((i >= 1) & (i < 5))
-        def _():
-            middle(far_first(i - 1))
-
-        @pl.when(i >= 2)
-        def _():
-            late(far_first(i - 2))
+        @pl.when(i < 4)
+        def _():
+            middle(order(i))
+
+        @pl.when(i >= 1)
+        def _():
+            late(order(i - 1))
         return 0
-    lax.fori_loop(0, 6, steps, 0)
+    lax.fori_loop(0, 5, steps, 0)
     swap.wait_recv()
     fg_ref[...] = jnp.sum(theirs[...], axis=0)
     for p in range(2):
-        for k in range(1, 4):
-            third(p, k).wait_recv()
-        out[:, pieces[p]] += rz[p, 1].astype(F32) + rz[p, 2].astype(F32) + rz[p, 3].astype(F32)
+        for slot in range(2):
+            along(p, slot).wait_recv()
+        out[:, pieces[p]] += rz[p, 0].astype(F32) + rz[p, 1].astype(F32)
     at = 0
     for ref in (oq_ref, ok_ref, ov_ref, om_ref):
         ref[...] = out[:, at : at + ref.shape[1]]

time: 621 us -> 615 us (level)
  no operation moved by 1% of the time
where the time goes in v7:
time: 615 us; the launch traced here: 611 us
  Pallas kernels  562 us (91%)
  between operations  14.6 us (2%)
  local copies, waits for them, and re-layouts  12.9 us (2%)
  matrix products  11.8 us (2%)
  other arithmetic  9.05 us (1%)
    pallas_call x1, Pallas kernels, front(): pl.pallas_call(functools.partial(front_kernel, chunks, rows), in_specs=[v...  184 us
    pallas_call x1, Pallas kernels, attend_back_mesh(): pl.pallas_call(functools.partial(attend_back_mesh_kernel, chunks, rows),...  129 us
    pallas_call x1, Pallas kernels, run_experts(): pl.pallas_call(experts_kernel, in_specs=[hbm, vmem, vmem, hbm, hbm, hbm,...  103 us
    pallas_call x1, Pallas kernels, run_grads(): pl.pallas_call(grads_kernel, in_specs=[hbm, vmem, vmem, hbm, hbm, hbm, hb...  88.9 us
    pallas_call x1, Pallas kernels, finish(): pl.pallas_call(functools.partial(finish_kernel, rows), in_specs=[vmem, vm...  47.3 us
  transfers between devices with their start and end apart: 2, of which 0 were waited for; matrix products, arithmetic and copies ran while one was open for 2% of the time, Pallas kernels for 61%

profile of v7, /device:TPU:0, one launch (start us, length us, event | category | flops | bytes accessed | tf_op | source)
XLA Modules:
  0.0 611.2 jit_solution(17700095829643733416)
XLA Ops:
  7.2 0.0 copy-start
  7.2 0.0 all-gather.2.cloned.1.call-start
  7.2 0.7 all-gather.2.cloned.1.call-update
  7.9 0.0 reduce-scatter.2.cloned.1.call-start
  8.0 0.7 fusion.2
  8.7 0.8 select_reduce_fusion
  9.5 0.0 copy-start.14
  9.5 0.8 copy.46.turn_ref
  10.2 1.4 copy.45.router_ref
  11.6 1.3 fusion.13
  13.0 0.8 multiply_sine_fusion
  13.8 0.0 copy-done.14
  13.8 184.5 %front.1 = (bf16[1536,256]{1,0:T(8,128)(2,1)}, bf16[1536,256]{1,0:T(8,128)(2,1)}, f32[4,8,256]{2,1,0:T(8,128)}, bf16[2,2560,512]{2,1,0:T(8,128)(2,1)}, f32[32,16...) custom-call(s32[1,256]{1,0:T(1,128)} %bitcast.44, ...), custom_call_target="tpu_custom_call" | custom-call | tf_op jit(solution)/shard_map/front/pallas_call | solution.py:1441
  198.2 0.9 fusion.12
  199.1 0.0 all-gather.2.cloned.1.call-done.wo_in
  199.2 0.0 copy-done
  199.2 4.1 multiply_reduce_fusion.2
  203.3 0.0 copy-start.8
  203.3 0.2 multiply_convert_fusion.x_ref
  203.5 0.0 copy-start.10
  203.5 1.7 fusion.14
  205.2 0.7 pad.4.gates_ref
  205.9 0.0 copy-done.10
  205.9 102.8 %experts.1 = (bf16[2560,1536]{1,0:T(8,128)(2,1)}, bf16[2560,1536]{1,0:T(8,128)(2,1)}, bf16[2560,1536]{1,0:T(8,128)(2,1)}, bf16[2560,512]{1,0:T(8,128)(2,1)}, bf1...) custom-call(bf16[256,1536]{1,0:T(8,128)(2,1)} %copy-done.10, ...), custom_call_target="tpu_custom_call" | custom-call | tf_op jit(solution)/shard_map/experts/pallas_call | solution.py:993
  308.7 88.9 %grads.1 = (f32[256,1536]{1,0:T(8,128)}, f32[32,8,128]{2,1,0:T(8,128)}, f32[1536,512]{1,0:T(8,128)}, f32[1536,512]{1,0:T(8,128)}, f32[512,1536]{1,0:T(8,128)}) custom-call(bf16[2560,1536]{1,0:T(8,128)(2,1)} %get-tuple-element.55.dx_ref, f32[32,16,256]{2,1,0:T(8,128)} %get-tuple-element.53.slots_ref, f32[32,8,128]{2,1,0:T(8,128)} %get-tuple-element.56.gg_ref, ...), custom_call_target="tpu_custom_call" | custom-call | tf_op jit(solution)/shard_map/grads/pallas_call | solution.py:1264
  397.6 0.9 slice.23
  398.6 0.0 copy-done.8
  398.6 0.0 copy-start.13
  398.6 2.3 multiply_reduce_fusion
  401.0 0.0 copy-done.13
  401.0 0.0 copy-start.9
  401.0 2.0 fusion.11
  403.0 0.0 copy-start.12
  403.0 0.9 copy-done.12
  403.9 0.0 copy-done.9
  403.9 3.5 convolution_convert_fusion
  407.4 0.0 reduce-scatter.2.cloned.1.call-update
  407.4 0.1 pad.7.clone
  407.5 1.0 copy-done.11
  408.5 0.2 convolution_convert_fusion.1
  408.7 0.9 copy.47
  409.7 0.3 broadcast_in_dim.54
  409.9 0.0 copy-start.3
  410.0 129.4 %attend_back.1 = (bf16[256,2560]{1,0:T(8,128)(2,1)}, bf16[256,1536]{1,0:T(8,128)(2,1)}) custom-call(s32[1,256]{1,0:T(1,128)} %bitcast.45, f32[32,256]{1,0:T(8,128)} %get-tuple-element.143.cos_ref, f32[32,256]{1,0:T(8,128)} %get-tuple-element.142.sin_ref, bf16[1536,256]{1,0:T(8,128)(2,1)} %get-tuple-element.64.q_ref, ...), custom_call_target="tpu_custom_call" | custom-call | tf_op jit(solution)/shard_map/attend_back/pallas_call | solution.py:1555
  539.4 0.0 copy-start.2
  539.4 0.0 copy-start.5
  539.4 1.5 maximum_maximum_fusion.more_ref
  540.9 0.0 copy-done.3
  540.9 0.0 copy-done.2
  540.9 0.0 copy-done.5
  540.9 47.3 %finish.1 = (f32[48,1536]{1,0:T(8,128)S(1)}, f32[48,512]{1,0:T(8,128)S(1)}, f32[48,512]{1,0:T(8,128)S(1)}, f32[48,256]{1,0:T(8,128)S(1)}, f32[256,1536]{1,0:T(8,128)S(1)}, /*index=5*/f32[8,128]{1,0:T(8,128)S(1)}) custom-call(bf16[256,1536]{1,0:T(8,128)(2,1)S(1)} %copy-done.3, bf16[256,2560]{1,0:T(8,128)(2,1)S(1)} %copy-done.2, ...), custom_call_target="tpu_custom_call" | custom-call | tf_op jit(solution)/shard_map/finish/pallas_call | solution.py:1784
  588.2 0.0 copy-start.1
  588.2 1.2 copy-done.1
  589.4 0.0 copy-start.4
  589.4 0.7 copy-done.4
  590.1 0.0 copy-start.6
  590.1 0.6 copy-done.6
  590.8 0.0 copy-start.7
  590.8 0.6 copy-done.7
  591.4 0.7 copy.49
  592.1 9.1 %hand_over.1 = (f32[1536,512]{1,0:T(8,128)}, f32[1536,512]{1,0:T(8,128)}, f32[512,1536]{1,0:T(8,128)}, bf16[256,1536]{1,0:T(8,128)(2,1)}, f32[256,1536]{1,0:T(8,...) custom-call(f32[1536,512]{1,0:T(8,128)} %get-tuple-element.61.refs_0_, ...), custom_call_target="tpu_custom_call" | custom-call | tf_op jit(solution)/shard_map/hand_over/pallas_call | solution.py:1840
  601.2 0.7 slice_reduce_fusion
  601.9 0.5 slice_bitcast_fusion
  602.4 1.6 convert_element_type.40
  (13 shorter events, 0.2 us)
Async XLA Ops:
  7.2 192.0 %copy-start = (bf16[256,1536]{1,0:T(8,128)(2,1)S(1)}, bf16[256,1536]{1,0:T(8,128)(2,1)}, u32[]{:S(2)}) copy-start(bf16[256,1536]{1,0:T(8,128)(2,1)} %x_in.1) | copy-start | bytes 2359300
  7.2 192.0 %all-gather.2.cloned.1.call-start = ((), (), s32[]{:S(2)}) async-start(), calls=%async_computation.1 | async-start | bytes 4866048 | tf_op jit(solution)/shard_map/all_gather | solution.py:1886
  7.9 594.5 %reduce-scatter.2.cloned.1.call-start = ((), (), s32[]{:S(2)}) async-start(), calls=%async_computation.2 | async-start | bytes 4866048 | tf_op jit(solution)/shard_map/reduce_scatter | solution.py:1996
  9.5 4.3 copy-start.14
  203.3 195.4 %copy-start.8 = (f32[256,1536]{1,0:T(8,128)}, f32[256,1536]{1,0:T(8,128)S(1)}, u32[]{:S(2)}) copy-start(f32[256,1536]{1,0:T(8,128)S(1)} %get-tuple-element.149.residual_in) | copy-start | bytes 4718596
  203.5 2.4 copy-start.10
  398.6 2.4 copy-start.13
  401.0 2.9 copy-start.9
  403.0 0.9 copy-start.12
  407.4 1.1 copy-start.11
  409.9 131.0 %copy-start.3 = (bf16[256,1536]{1,0:T(8,128)(2,1)S(1)}, bf16[256,1536]{1,0:T(8,128)(2,1)}, u32[]{:S(2)}) copy-start(bf16[256,1536]{1,0:T(8,128)(2,1)} %get-tuple-element.71.n_ref) | copy-start | bytes 2359300
  539.4 1.5 copy-start.2
  539.4 1.5 copy-start.5
  588.2 1.2 copy-start.1
  589.4 0.7 copy-start.4
  590.1 0.6 copy-start.6
  590.8 0.6 copy-start.7
Sparse Core Ops, SparseCore 0:
  10.9 82.1 all-gather.1
  407.5 133.2 reduce-scatter.1

commit v8 on v7

--- a/solution.py
+++ b/solution.py
@@ -873,7 +873,6 @@
         return pltpu.make_async_copy(ui_ref.at[at_chip(u), :], ubuf.at[lax.rem(u, 2)], usem.at[lax.rem(u, 2)])
 
     load_up(0).start()
-    swap.start()
     loads = [
         pltpu.make_async_copy(source, into, wsem.at[i])
         for i, (source, into) in enumerate(((wg_in, wg_ref), (wu_in, wu_ref), (wd_in, wd_ref)))
@@ -881,10 +880,10 @@
     for cp in loads:
         cp.start()
     ag.one(0)
+    swap.start()
     for cp, source, into in zip(loads, (wg_ref, wu_ref, wd_ref), (wgt, wut, wdt), strict=True):
         cp.wait()
         into[...] = source[...].T
-    swap.wait_recv()
 
     def store(n, buf, out, u):
         return pltpu.make_async_copy(buf.at[lax.rem(u, 2)], out.at[at_chip(u), :], osem.at[n, lax.rem(u, 2)])
@@ -964,6 +963,10 @@
             def _(names=names):
                 for name in names:
                     step[name]()
+
+        @pl.when(u == 0)
+        def _():
+            swap.wait_recv()
 
         unit(u)
         return 0

time: 615 us -> 612 us (level)
  no operation moved by 1% of the time
where the time goes in v8:
time: 612 us; the launch traced here: 608 us
  Pallas kernels  558 us (91%)
  between operations  14.6 us (2%)
  local copies, waits for them, and re-layouts  12.9 us (2%)
  matrix products  11.8 us (2%)
  other arithmetic  9.05 us (1%)
    pallas_call x1, Pallas kernels, front(): pl.pallas_call(functools.partial(front_kernel, chunks, rows), in_specs=[v...  184 us
    pallas_call x1, Pallas kernels, attend_back_mesh(): pl.pallas_call(functools.partial(attend_back_mesh_kernel, chunks, rows),...  130 us
    pallas_call x1, Pallas kernels, run_experts(): pl.pallas_call(experts_kernel, in_specs=[hbm, vmem, vmem, hbm, hbm, hbm,...  98.6 us
    pallas_call x1, Pallas kernels, run_grads(): pl.pallas_call(grads_kernel, in_specs=[hbm, vmem, vmem, hbm, hbm, hbm, hb...  89.3 us
    pallas_call x1, Pallas kernels, finish(): pl.pallas_call(functools.partial(finish_kernel, rows), in_specs=[vmem, vm...  47.2 us
  transfers between devices with their start and end apart: 2, of which 0 were waited for; matrix products, arithmetic and copies ran while one was open for 2% of the time, Pallas kernels for 61%

profile of v8, /device:TPU:0, one launch (start us, length us, event | category | flops | bytes accessed | tf_op | source)
XLA Modules:
  0.0 607.5 jit_solution(3706991487783397273)
XLA Ops:
  7.2 0.0 copy-start
  7.2 0.0 all-gather.2.cloned.1.call-start
  7.2 0.7 all-gather.2.cloned.1.call-update
  7.9 0.0 reduce-scatter.2.cloned.1.call-start
  8.0 0.7 fusion.2
  8.7 0.8 select_reduce_fusion
  9.5 0.0 copy-start.14
  9.5 0.8 copy.46.turn_ref
  10.2 1.4 copy.45.router_ref
  11.6 1.3 fusion.13
  13.0 0.8 multiply_sine_fusion
  13.8 0.0 copy-done.14
  13.8 184.5 %front.1 = (bf16[1536,256]{1,0:T(8,128)(2,1)}, bf16[1536,256]{1,0:T(8,128)(2,1)}, f32[4,8,256]{2,1,0:T(8,128)}, bf16[2,2560,512]{2,1,0:T(8,128)(2,1)}, f32[32,16...) custom-call(s32[1,256]{1,0:T(1,128)} %bitcast.44, ...), custom_call_target="tpu_custom_call" | custom-call | tf_op jit(solution)/shard_map/front/pallas_call | solution.py:1444
  198.2 0.9 fusion.12
  199.1 0.0 all-gather.2.cloned.1.call-done.wo_in
  199.2 0.0 copy-done
  199.2 4.1 multiply_reduce_fusion.2
  203.3 0.0 copy-start.8
  203.3 0.2 multiply_convert_fusion.x_ref
  203.5 0.0 copy-start.10
  203.5 1.7 fusion.14
  205.2 0.7 pad.4.gates_ref
  205.9 0.0 copy-done.10
  205.9 98.6 %experts.1 = (bf16[2560,1536]{1,0:T(8,128)(2,1)}, bf16[2560,1536]{1,0:T(8,128)(2,1)}, bf16[2560,1536]{1,0:T(8,128)(2,1)}, bf16[2560,512]{1,0:T(8,128)(2,1)}, bf1...) custom-call(bf16[256,1536]{1,0:T(8,128)(2,1)} %copy-done.10, ...), custom_call_target="tpu_custom_call" | custom-call | tf_op jit(solution)/shard_map/experts/pallas_call | solution.py:996
  304.6 89.3 %grads.1 = (f32[256,1536]{1,0:T(8,128)}, f32[32,8,128]{2,1,0:T(8,128)}, f32[1536,512]{1,0:T(8,128)}, f32[1536,512]{1,0:T(8,128)}, f32[512,1536]{1,0:T(8,128)}) custom-call(bf16[2560,1536]{1,0:T(8,128)(2,1)} %get-tuple-element.55.dx_ref, f32[32,16,256]{2,1,0:T(8,128)} %get-tuple-element.53.slots_ref, f32[32,8,128]{2,1,0:T(8,128)} %get-tuple-element.56.gg_ref, ...), custom_call_target="tpu_custom_call" | custom-call | tf_op jit(solution)/shard_map/grads/pallas_call | solution.py:1267
  393.9 0.9 slice.23
  394.9 0.0 copy-done.8
  394.9 0.0 copy-start.13
  394.9 2.3 multiply_reduce_fusion
  397.3 0.0 copy-done.13
  397.3 0.0 copy-start.9
  397.3 2.0 fusion.11
  399.2 0.0 copy-start.12
  399.3 0.9 copy-done.12
  400.1 0.0 copy-done.9
  400.1 3.5 convolution_convert_fusion
  403.6 0.0 copy-start.11
  403.6 0.0 reduce-scatter.2.cloned.1.call-update
  403.7 0.1 pad.7.clone
  403.7 1.0 copy-done.11
  404.8 0.2 convolution_convert_fusion.1
  405.0 0.9 copy.47
  405.9 0.3 broadcast_in_dim.54
  406.2 0.0 copy-start.3
  406.2 129.6 %attend_back.1 = (bf16[256,2560]{1,0:T(8,128)(2,1)}, bf16[256,1536]{1,0:T(8,128)(2,1)}) custom-call(s32[1,256]{1,0:T(1,128)} %bitcast.45, f32[32,256]{1,0:T(8,128)} %get-tuple-element.143.cos_ref, f32[32,256]{1,0:T(8,128)} %get-tuple-element.142.sin_ref, bf16[1536,256]{1,0:T(8,128)(2,1)} %get-tuple-element.64.q_ref, ...), custom_call_target="tpu_custom_call" | custom-call | tf_op jit(solution)/shard_map/attend_back/pallas_call | solution.py:1558
  535.9 0.0 copy-start.2
  535.9 0.0 copy-start.5
  535.9 1.5 maximum_maximum_fusion.more_ref
  537.4 0.0 copy-done.3
  537.4 0.0 copy-done.2
  537.4 0.0 copy-done.5
  537.4 47.2 %finish.1 = (f32[48,1536]{1,0:T(8,128)S(1)}, f32[48,512]{1,0:T(8,128)S(1)}, f32[48,512]{1,0:T(8,128)S(1)}, f32[48,256]{1,0:T(8,128)S(1)}, f32[256,1536]{1,0:T(8,128)S(1)}, /*index=5*/f32[8,128]{1,0:T(8,128)S(1)}) custom-call(bf16[256,1536]{1,0:T(8,128)(2,1)S(1)} %copy-done.3, bf16[256,2560]{1,0:T(8,128)(2,1)S(1)} %copy-done.2, ...), custom_call_target="tpu_custom_call" | custom-call | tf_op jit(solution)/shard_map/finish/pallas_call | solution.py:1787
  584.6 0.0 copy-start.1
  584.6 1.2 copy-done.1
  585.8 0.7 copy-done.4
  586.5 0.0 copy-start.6
  586.5 0.6 copy-done.6
  587.1 0.0 copy-start.7
  587.1 0.6 copy-done.7
  587.8 0.7 copy.49
  588.5 9.1 %hand_over.1 = (f32[1536,512]{1,0:T(8,128)}, f32[1536,512]{1,0:T(8,128)}, f32[512,1536]{1,0:T(8,128)}, bf16[256,1536]{1,0:T(8,128)(2,1)}, f32[256,1536]{1,0:T(8,...) custom-call(f32[1536,512]{1,0:T(8,128)} %get-tuple-element.61.refs_0_, ...), custom_call_target="tpu_custom_call" | custom-call | tf_op jit(solution)/shard_map/hand_over/pallas_call | solution.py:1843
  597.5 0.7 slice_reduce_fusion
  598.2 0.5 slice_bitcast_fusion
  598.8 1.6 convert_element_type.40
  (13 shorter events, 0.2 us)
Async XLA Ops:
  7.2 192.0 %copy-start = (bf16[256,1536]{1,0:T(8,128)(2,1)S(1)}, bf16[256,1536]{1,0:T(8,128)(2,1)}, u32[]{:S(2)}) copy-start(bf16[256,1536]{1,0:T(8,128)(2,1)} %x_in.1) | copy-start | bytes 2359300
  7.2 192.0 %all-gather.2.cloned.1.call-start = ((), (), s32[]{:S(2)}) async-start(), calls=%async_computation.1 | async-start | bytes 4866048 | tf_op jit(solution)/shard_map/all_gather | solution.py:1889
  7.9 590.8 %reduce-scatter.2.cloned.1.call-start = ((), (), s32[]{:S(2)}) async-start(), calls=%async_computation.2 | async-start | bytes 4866048 | tf_op jit(solution)/shard_map/reduce_scatter | solution.py:1999
  9.5 4.3 copy-start.14
  203.3 191.6 %copy-start.8 = (f32[256,1536]{1,0:T(8,128)}, f32[256,1536]{1,0:T(8,128)S(1)}, u32[]{:S(2)}) copy-start(f32[256,1536]{1,0:T(8,128)S(1)} %get-tuple-element.149.residual_in) | copy-start | bytes 4718596
  203.5 2.4 copy-start.10
  394.9 2.4 copy-start.13
  397.3 2.9 copy-start.9
  399.2 0.9 copy-start.12
  403.6 1.1 copy-start.11
  406.2 131.2 %copy-start.3 = (bf16[256,1536]{1,0:T(8,128)(2,1)S(1)}, bf16[256,1536]{1,0:T(8,128)(2,1)}, u32[]{:S(2)}) copy-start(bf16[256,1536]{1,0:T(8,128)(2,1)} %get-tuple-element.71.n_ref) | copy-start | bytes 2359300
  535.9 1.5 copy-start.2
  535.9 1.5 copy-start.5
  584.6 1.2 copy-start.1
  585.8 0.7 copy-start.4
  586.5 0.6 copy-start.6
  587.1 0.6 copy-start.7
Sparse Core Ops, SparseCore 0:
  10.9 82.1 all-gather.1
  403.8 133.6 reduce-scatter.1
